TPU v7x, 32 devices: a whole 2x2x4 slice. The times are simulated.
32 devices in a mesh: group: 2 (over y), fsdp: 4 (over x, core), dp: 4 (over z).
Axes of the slice: x: 2, y: 2, z: 4, core: 2. Of those that a mesh axis runs over, the one named last changes fastest.
Arguments:
- activations: bfloat16 [12288, 8192], P(('group', 'fsdp', 'dp')), parts along dimension 0, may hold values from -6 to 6
- upstream: bfloat16 [12288, 1024], P(('group', 'fsdp', 'dp')), parts along dimension 0, may hold values from -6 to 6
- frozen: bfloat16 [8192, 1024], P('fsdp'), may hold values from -0.0625 to 0.0625
- deltas: bfloat16 [32, 128, 128], P(('group', 'fsdp')), parts along dimension 0, may hold values from -0.29882812 to 0.29882812
- block_rows: int32 [16], replicated, may hold values from 0 to 63, as said below
- block_cols: int32 [16], replicated, may hold values from 0 to 7
- block_slot: int32 [16], replicated, may hold values from 0 to 15, as said below
Outputs:
- grad_in: bfloat16 [12288, 8192], P(('group', 'fsdp', 'dp')), parts along dimension 0
- delta_grad: float32 [32, 128, 128], P(('group', 'fsdp')), parts along dimension 0
There are 2 independent parts, one for each index of `group`. A program takes and returns all parts, laid end to end along the dimension named above; an argument that names none is the same for every part. Nothing has to cross between parts.
Inputs may be any that keep to these rules, and one draw needn't show every extreme that they name: The pairs (block_rows, block_cols) are distinct. `block_slot`: slots are distinct; at most 4 blocks have one owner slot // 4, and some owner holds exactly 4.
All inputs are finite; a program needn't handle non-finite values.
Results may differ from a plain program's by a relative error of at most 0.001.
Values may be sent and summed in bfloat16 or wider, within the bound.
No kernel may reach another device: no remote copies, remote signals or barrier semaphores. Data moves between devices by JAX's collectives and lax.ppermute only.
A program may use at most 128 MiB of HBM per device.

v0:
```python
import math

import jax
import jax.numpy as jnp
from jax import lax
from jax.sharding import PartitionSpec as P

BLOCK = 128


def contract_rows(left, right):
    return lax.dot_general(
        left, right, (((1,), (1,)), ((), ())), preferred_element_type=jnp.float32
    )


def per_device(activations, upstream, frozen, deltas, block_rows, block_cols, block_slot):
    tok_rows = activations.shape[0]
    model_width = activations.shape[1]
    kv_width = upstream.shape[1]
    row_blocks = model_width // BLOCK
    col_blocks = kv_width // BLOCK
    local_slots = deltas.shape[0]
    gathered_deltas = lax.all_gather(deltas, "fsdp", axis=0, tiled=True)
    picked = jnp.take(gathered_deltas, block_slot, axis=0)
    dense_part = contract_rows(upstream, lax.all_gather(frozen, "fsdp", axis=0, tiled=True))
    chosen = jnp.take(upstream.reshape(tok_rows, col_blocks, BLOCK), block_cols, axis=1)
    block_terms = jnp.einsum("tbj,bij->tbi", chosen, picked, preferred_element_type=jnp.float32)
    placed = (
        jnp.zeros((tok_rows, row_blocks, BLOCK), jnp.float32).at[:, block_rows, :].add(block_terms)
    )
    grad_in = (dense_part + placed.reshape(tok_rows, model_width)).astype(jnp.bfloat16)
    act_blocks = jnp.take(activations.reshape(tok_rows, row_blocks, BLOCK), block_rows, axis=1)
    up_blocks = jnp.take(upstream.reshape(tok_rows, col_blocks, BLOCK), block_cols, axis=1)
    partial_grad = jnp.einsum(
        "tbi,tbj->bij", act_blocks, up_blocks, preferred_element_type=jnp.float32
    )
    totals = lax.psum(partial_grad, ("fsdp", "dp"))
    first_slot = lax.axis_index("fsdp") * local_slots
    wanted = first_slot + jnp.arange(local_slots, dtype=jnp.int32)
    matches = wanted[:, None] == block_slot[None, :]
    owned = jnp.sum(jnp.where(matches[:, :, None, None], totals[None], 0.0), axis=1)
    normalizer = 1.0 / math.sqrt(tok_rows * lax.axis_size("fsdp") * lax.axis_size("dp"))
    return (grad_in, owned * normalizer)


def solution(mesh):
    return jax.shard_map(
        per_device,
        mesh=mesh,
        in_specs=(
            P(("group", "fsdp", "dp"), None),
            P(("group", "fsdp", "dp"), None),
            P("fsdp", None),
            P(("group", "fsdp"), None, None),
            P(),
            P(),
            P(),
        ),
        out_specs=(P(("group", "fsdp", "dp"), None), P(("group", "fsdp"), None, None)),
        check_vma=False,
    )
```

profile of v0, /device:TPU:0, one launch (start us, length us, event | category | flops | bytes accessed | tf_op | source)
XLA Modules:
  0.0 244.5 jit_solution(4839441714446315149)
XLA Ops:
  8.0 0.0 all-reduce.2.cloned.1.call-start
  8.0 0.7 compare_select_fusion.2
  8.7 0.7 compare_and_fusion.1
  9.4 0.7 compare_select_fusion
  10.0 0.7 compare_and_fusion
  10.7 1.5 copy.24
  12.2 0.4 copy.25
  12.6 8.6 %copy.27 = bf16[384,8192]{0,1:T(8,128)(2,1)} copy(bf16[384,8192]{1,0:T(8,128)(2,1)} %param.9) | data formatting | bytes 12582912 | tf_op args[0]
  21.2 8.6 %copy.28 = bf16[384,64,128]{2,0,1:T(8,128)(2,1)} copy(bf16[384,64,128]{0,2,1:T(8,128)(2,1)} %bitcast.19) | data formatting | bytes 12582912 | tf_op jit(solution)/shard_map/reshape | solution.py:33
  29.9 0.8 gather_fusion.2
  30.7 0.0 copy-start
  30.7 5.3 %gather_fusion.1 = bf16[16,384,128]{2,1,0:T(8,128)(2,1)} fusion(bf16[384,64,128]{2,0,1:T(8,128)(2,1)} %copy.28, s32[1024]{0:T(1024)S(1)} %pad_clamp_fusion), kind=kCustom, calls=%fused_computation.2 | custom fusion | bytes 3145792 | tf_op jit(solution)/shard_map/jit(_take)/gather | solution.py:33
  36.0 3.2 %fusion.1 = f32[16,128,128]{2,1,0:T(8,128)} fusion(bf16[16,384,128]{2,1,0:T(8,128)(2,1)} %gather_fusion.1, pred[16]{0:T(512)(128)(4,1)S(1)} %compare_and_fusion.1, bf16[16,384,128]{2,1,0:T(8,128)(2,1)S(1)} %gather_fusion.2, pred[16]{0:T(512)(128)(4,1)S(1)} %get-tuple-element.3), kind=kOutput, calls=%fused_computation.7 | convolution fusion | flops 202899456 | bytes 4194336 | tf_op jit(solution)/shard_map/tbi,tbj->bij/dot_general | solution.py:35
  39.2 0.0 copy-done
  39.2 0.0 copy-start.2
  39.2 0.0 copy-start.1
  39.2 0.0 all-reduce.2.cloned.1.call-update
  39.2 0.0 all-gather.2.cloned.1.call-start
  39.3 0.5 all-gather.2.cloned.1.call-update
  39.8 0.0 copy-done.2
  39.9 0.3 copy-done.1
  40.1 8.6 %all_gather.7 = bf16[16,128,128]{2,1,0:T(8,128)(2,1)S(1)} all-gather(bf16[4,128,128]{2,1,0:T(8,128)(2,1)S(1)} %copy-done.1), channel_id=1, replica_groups=mesh['group'=2,'fsdp'=4,'dp'=4] {'fsdp'}, dimensions={0}, use_global_device_ids=true | all-gather | bytes 655360 | tf_op jit(solution)/shard_map/all_gather | solution.py:24
  48.7 1.4 gather_fusion
  50.1 2.5 %fusion.4 = f32[16,384,128]{2,1,0:T(8,128)S(1)} fusion(bf16[16,384,128]{2,1,0:T(8,128)(2,1)} %copy-done, pred[16]{0:T(512)(128)(4,1)S(1)} %get-tuple-element.3, bf16[16,128,128]{2,1,0:T(8,128)(2,1)} %gather_fusion, pred[16]{0:T(512)(128)(4,1)S(1)} %get-tuple-element.4), kind=kOutput, calls=%fused_computation.10 | convolution fusion | flops 202375168 | bytes 5242912 | tf_op jit(solution)/shard_map/tbj,bij->tbi/dot_general | solution.py:28
  52.6 8.9 %broadcast_in_dim.61 = f32[384,64,128]{2,0,1:T(8,128)} broadcast(f32[]{:T(128)} %constant.24.clone.1), dimensions={} | broadcast | bytes 12582916 | tf_op jit(solution)/shard_map/broadcast_in_dim | solution.py:30
  61.6 7.4 %scatter_fusion = f32[384,64,128]{2,0,1:T(8,128)} fusion(f32[384,64,128]{2,0,1:T(8,128)} %broadcast_in_dim.61, s32[16]{0:T(128)S(1)} %compare_select_fusion.2, f32[16,384,128]{2,1,0:T(8,128)S(1)} %fusion.4), kind=kCustom, calls=%fused_computation.3 | custom fusion | flops 786432 | bytes 9437248 | tf_op jit(solution)/shard_map/scatter-add | solution.py:30
  69.0 0.1 broadcast_compare_fusion
  69.1 150.9 %all-reduce.2.cloned.1.call-done = f32[16,128,128]{2,1,0:T(8,128)} async-done(((f32[16,128,128]{2,1,0:T(8,128)}), f32[16,128,128]{2,1,0:T(8,128)}) %all-reduce.2.cloned.1.call-update) | async-done | bytes 1048592 | tf_op jit(solution)/shard_map/psum | solution.py:38
  220.0 1.7 select_reduce_fusion
  221.7 0.7 broadcast_multiply_fusion
  222.4 0.0 all-gather.2.cloned.1.call-done
  222.4 14.7 %fusion = bf16[384,8192]{1,0:T(8,128)(2,1)} fusion(bf16[384,1024]{1,0:T(8,128)(2,1)} %param.10, bf16[8192,1024]{1,0:T(8,128)(2,1)} %all-gather.2.cloned.1.call-done, f32[384,64,128]{2,0,1:T(8,128)} %scatter_fusion), kind=kOutput, calls=%fused_computation.5 | convolution fusion | flops 6448742400 | bytes 36438016 | tf_op jit(solution)/shard_map/dot_general | solution.py:12
  (5 shorter events, 0.0 us)
Async XLA Ops:
  8.0 212.0 %all-reduce.2.cloned.1.call-start = ((), (), s32[]{:S(2)}) async-start(), calls=%async_computation.1 | async-start | bytes 2097152 | tf_op jit(solution)/shard_map/psum | solution.py:38
  30.7 8.5 %copy-start = (bf16[16,384,128]{2,1,0:T(8,128)(2,1)}, bf16[16,384,128]{2,1,0:T(8,128)(2,1)S(1)}, u32[]{:S(2)}) copy-start(bf16[16,384,128]{2,1,0:T(8,128)(2,1)S(1)} %gather_fusion.2) | copy-start | bytes 4718596
  39.2 0.7 copy-start.2
  39.2 0.9 copy-start.1
  39.2 183.2 %all-gather.2.cloned.1.call-start = ((), (), s32[]{:S(2)}) async-start(), calls=%async_computation | async-start | bytes 20971520 | tf_op jit(solution)/shard_map/all_gather | solution.py:26
Sparse Core Ops, SparseCore 0:
  39.3 180.6 all-reduce.1
Sparse Core Ops, SparseCore 1:
  41.2 109.2 all-gather.1
where the time goes:
time: 245 us
  waiting for transfers between devices  151 us (62%)
  local copies, waits for them, and re-layouts  35.9 us (15%)
  matrix products  20.4 us (8%)
  between operations  15.5 us (6%)
  other arithmetic  12.6 us (5%)
  blocking collectives  8.6 us (4%)
    psum x1, waiting for transfers between devices, per_device(): totals = lax.psum(partial_grad, ('fsdp', 'dp'))  151 us
    dot_general x1, matrix products, contract_rows(): lax.dot_general(left, right, (((1,), (1,)), ((), ())), preferred_element_...  14.7 us
    unnamed x8, local copies, waits for them, and re-layouts  10.4 us
    broadcast_in_dim x1, local copies, waits for them, and re-layouts, per_device(): jnp.zeros((tok_rows, row_blocks, BLOCK), jnp.float32).at[:, block_rows, :]  8.94 us
    reshape x1, local copies, waits for them, and re-layouts, per_device(): activations.reshape(tok_rows, row_blocks, BLOCK)  8.64 us
    all_gather x1, blocking collectives, per_device(): gathered_deltas = lax.all_gather(deltas, 'fsdp', axis=0, tiled=True)  8.6 us
    scatter-add x1, other arithmetic, per_device(): jnp.zeros((tok_rows, row_blocks, BLOCK), jnp.float32).at[:, block_rows, :]  7.43 us
    gather x1, local copies, waits for them, and re-layouts, per_device(): jnp.take(activations.reshape(tok_rows, row_blocks, BLOCK), block_rows, ax...  5.25 us
  transfers between devices with their start and end apart: 2, of which 1 were waited for; matrix products, arithmetic and copies ran while one was open for 9% of the time, Pallas kernels for 0%

commit v1 on v0

v1 whole, which is shorter than its diff:
```python
import functools
import math

import jax
import jax.numpy as jnp
from jax import lax
from jax.experimental import pallas as pl
from jax.experimental.pallas import tpu as pltpu
from jax.sharding import PartitionSpec as P

BLOCK = 128
VMEM_BYTES = 40 * 1024 * 1024
SMEM_SPEC = pl.BlockSpec(memory_space=pltpu.SMEM)
ANY_SPEC = pl.BlockSpec(memory_space=pl.ANY)
VMEM_SPEC = pl.BlockSpec(memory_space=pltpu.VMEM)


def dot_nt(left, right):
    return lax.dot_general(
        left, right, (((1,), (1,)), ((), ())), preferred_element_type=jnp.float32
    )


def dot_tn(left, right):
    return lax.dot_general(
        left, right, (((0,), (0,)), ((), ())), preferred_element_type=jnp.float32
    )


def grad_kernel(place, outs, where_ref, rows_ref, cols_ref, slots_ref, act_ref, up_ref, *refs):
    out_refs, (act_buf, up_buf, act_sem, up_sem) = refs[:outs], refs[outs:]
    nb = rows_ref.shape[0]
    up_copy = pltpu.make_async_copy(up_ref, up_buf, up_sem)
    up_copy.start()

    def act_copy(b):
        column = pl.multiple_of(rows_ref[b] * BLOCK, BLOCK)
        return pltpu.make_async_copy(
            act_ref.at[:, pl.ds(column, BLOCK)], act_buf.at[b], act_sem.at[b]
        )

    for b in range(nb):
        act_copy(b).start()
    for ref in out_refs:
        ref[...] = jnp.zeros_like(ref)
    up_copy.wait()
    for b in range(nb):
        act_copy(b).wait()
        column = pl.multiple_of(cols_ref[b] * BLOCK, BLOCK)
        term = dot_tn(act_buf[b], up_buf[:, pl.ds(column, BLOCK)])
        which, index = place(where_ref, slots_ref[b])
        for n, ref in enumerate(out_refs):

            @pl.when(which == n)
            def _():
                ref[index] = term


def block_grads(place, shapes, where, rows, cols, slots, act, up):
    nb = rows.shape[0]
    return pl.pallas_call(
        functools.partial(grad_kernel, place, len(shapes)),
        out_shape=[jax.ShapeDtypeStruct((n, BLOCK, BLOCK), jnp.float32) for n in shapes],
        in_specs=[SMEM_SPEC] * 4 + [ANY_SPEC] * 2,
        out_specs=[VMEM_SPEC] * len(shapes),
        scratch_shapes=[
            pltpu.VMEM((nb, act.shape[0], BLOCK), act.dtype),
            pltpu.VMEM(up.shape, up.dtype),
            pltpu.SemaphoreType.DMA((nb,)),
            pltpu.SemaphoreType.DMA,
        ],
        compiler_params=pltpu.CompilerParams(vmem_limit_bytes=VMEM_BYTES),
        cost_estimate=pl.CostEstimate(
            flops=2 * nb * act.shape[0] * BLOCK * BLOCK,
            bytes_accessed=8 * nb * act.shape[0] * BLOCK,
            transcendentals=0,
        ),
        name="block_grads",
    )(where, rows, cols, slots, act, up)


def rows_kernel(
    units, tile, row_blocks, delta_at, n_w, n_d, aliased,
    where_ref, rows_ref, cols_ref, slots_ref, up_ref, *refs,
):
    w_refs, refs = refs[:n_w], refs[n_w:]
    d_refs, refs = refs[:n_d], refs[n_d:]
    if aliased:
        refs = refs[1:]
    out_ref, up_buf, w_buf, d_buf, acc, o_buf, table, mask, up_sem, w_sem, d_sem, o_sem = refs
    nb = rows_ref.shape[0]
    n_units = len(units)
    per = d_buf.shape[0] // n_d

    up_copy = pltpu.make_async_copy(up_ref, up_buf, up_sem)
    up_copy.start()
    for u, (w, first, _) in enumerate(units):
        pltpu.make_async_copy(
            w_refs[w].at[pl.ds(first, BLOCK)], w_buf.at[pl.ds(u * BLOCK, BLOCK)], w_sem.at[u]
        ).start()
    d_copies = [
        pltpu.make_async_copy(ref, d_buf.at[pl.ds(n * per, per)], d_sem.at[n])
        for n, ref in enumerate(d_refs)
    ]
    for copy in d_copies:
        copy.start()
    for u, (_, _, column) in enumerate(units):
        table[u] = column(where_ref)

    def clear(r, carry):
        mask[r] = 0
        return carry

    lax.fori_loop(0, row_blocks, clear, 0)
    for b in range(nb):
        r = rows_ref[b]
        mask[r] = mask[r] | (1 << b)
    up_copy.wait()
    for copy in d_copies:
        copy.wait()

    def out_copy(u):
        column = pl.multiple_of(table[u] * BLOCK, BLOCK)
        return pltpu.make_async_copy(
            o_buf.at[u], out_ref.at[:, pl.ds(column, BLOCK)], o_sem.at[u]
        )

    def step(t, width):
        for h in range(width):
            pltpu.make_async_copy(
                w_refs[0].at[pl.ds(0, BLOCK)],
                w_buf.at[pl.ds((t + h) * BLOCK, BLOCK)],
                w_sem.at[t + h],
            ).wait()
        size = width * BLOCK
        start = t * BLOCK if isinstance(t, int) else pl.multiple_of(t * BLOCK, BLOCK)
        acc[:, :size] = dot_nt(up_buf[...], w_buf[pl.ds(start, size)])
        for h in range(width):
            bits = mask[table[t + h]]

            @pl.when(bits != 0)
            def _():
                def one(b, carry):
                    @pl.when(((bits >> b) & 1) != 0)
                    def _():
                        column = pl.multiple_of(cols_ref[b] * BLOCK, BLOCK)
                        delta = d_buf[delta_at(where_ref, slots_ref[b])]
                        acc[:, h * BLOCK : (h + 1) * BLOCK] += dot_nt(
                            up_buf[:, pl.ds(column, BLOCK)], delta
                        )

                    return carry

                lax.fori_loop(0, nb, one, 0)

            o_buf[t + h] = acc[:, h * BLOCK : (h + 1) * BLOCK].astype(o_buf.dtype)
            out_copy(t + h).start()

    whole = n_units // tile
    if whole > 1:

        def body(k, carry):
            step(k * tile, tile)
            return carry

        lax.fori_loop(0, whole, body, 0)
    elif whole == 1:
        step(0, tile)
    if n_units % tile:
        step(whole * tile, n_units % tile)

    def finish(u, carry):
        out_copy(u).wait()
        return carry

    lax.fori_loop(0, n_units, finish, 0)


def rows_grad(units, weights, where, rows, cols, slots, up, deltas, delta_at, width, out=None, tile=4):
    n_units = len(units)
    tile = min(tile, n_units)
    tokens, depth = up.shape
    stored = sum(d.shape[0] for d in deltas)
    operands = [where, rows, cols, slots, up, *weights, *deltas]
    if out is not None:
        operands.append(out)
    return pl.pallas_call(
        functools.partial(
            rows_kernel, units, tile, width // BLOCK, delta_at, len(weights), len(deltas),
            out is not None,
        ),
        out_shape=jax.ShapeDtypeStruct((tokens, width), up.dtype),
        in_specs=[SMEM_SPEC] * 4 + [ANY_SPEC] * (len(operands) - 4),
        out_specs=ANY_SPEC,
        input_output_aliases={} if out is None else {len(operands) - 1: 0},
        scratch_shapes=[
            pltpu.VMEM((tokens, depth), up.dtype),
            pltpu.VMEM((n_units * BLOCK, depth), up.dtype),
            pltpu.VMEM((stored, BLOCK, BLOCK), up.dtype),
            pltpu.VMEM((tokens, tile * BLOCK), jnp.float32),
            pltpu.VMEM((n_units, tokens, BLOCK), up.dtype),
            pltpu.SMEM((n_units,), jnp.int32),
            pltpu.SMEM((width // BLOCK,), jnp.int32),
            pltpu.SemaphoreType.DMA,
            pltpu.SemaphoreType.DMA((n_units,)),
            pltpu.SemaphoreType.DMA((len(deltas),)),
            pltpu.SemaphoreType.DMA((n_units,)),
        ],
        compiler_params=pltpu.CompilerParams(vmem_limit_bytes=VMEM_BYTES),
        cost_estimate=pl.CostEstimate(
            flops=2 * tokens * depth * n_units * BLOCK,
            bytes_accessed=2 * n_units * BLOCK * (depth + tokens),
            transcendentals=0,
        ),
        name="rows_grad",
    )(*operands)


def gathered(activations, upstream, frozen, deltas, block_rows, block_cols, block_slot):
    local_slots = deltas.shape[0]
    local_rows = frozen.shape[0]
    n = lax.axis_size("fsdp")
    width = activations.shape[1]
    where = jnp.zeros((2,), jnp.int32)
    pattern = (where, block_rows, block_cols, block_slot)

    (partial,) = block_grads(
        lambda where_ref, slot: (0, slot), [n * local_slots], *pattern, activations, upstream
    )
    mine = lax.psum_scatter(partial, "fsdp", scatter_dimension=0, tiled=True)
    totals = lax.psum(mine, "dp")

    all_deltas = lax.all_gather(deltas, "fsdp", axis=0, tiled=True)
    weight = lax.all_gather(frozen, "fsdp", axis=0, tiled=True)
    out = None
    for first in range(0, width, 2048):
        units = [
            (0, first + k * BLOCK, lambda where_ref, c=first // BLOCK + k: c)
            for k in range(min(2048, width - first) // BLOCK)
        ]
        out = rows_grad(
            units, [weight], *pattern, upstream, [all_deltas],
            lambda where_ref, slot: slot, width, out,
        )
    return out, totals


def relayed(activations, upstream, frozen, deltas, block_rows, block_cols, block_slot):
    local_slots = deltas.shape[0]
    quarter = frozen.shape[0]
    depth = frozen.shape[1]
    width = activations.shape[1]
    f = lax.axis_index("fsdp")
    y = lax.axis_index("group")
    z = lax.axis_index("dp")
    n_dp = lax.axis_size("dp")
    even = z % 2
    cell = 2 * y + even
    where = jnp.stack([f, cell]).astype(jnp.int32)
    pattern = (where, block_rows, block_cols, block_slot)

    def over_core(a):
        return lax.ppermute(a, "fsdp", [(k, k ^ 1) for k in range(4)])

    def over_x(a):
        return lax.ppermute(a, "fsdp", [(k, k ^ 2) for k in range(4)])

    def over_y(a):
        return lax.ppermute(a, "group", [(k, k ^ 1) for k in range(2)])

    def over_z(a, step=1):
        return lax.ppermute(a, "dp", [(k, k ^ step) for k in range(n_dp)])

    part = quarter // 4
    sizes = (part // 4, part // 4, part // 2)
    offs = (0, sizes[0], sizes[0] + sizes[1])

    def own_rows(flip, k):
        return lax.dynamic_slice_in_dim(frozen, (cell ^ flip) * part + offs[k], sizes[k], 0)

    sib = over_core(frozen)
    x0 = over_x(own_rows(0, 0))
    dx = over_x(deltas)
    x1 = over_x(own_rows(0, 1))
    x2 = over_x(own_rows(0, 2))
    x3 = over_x(own_rows(3, 2))
    y0, z0 = over_y(x0), over_z(x0)
    y1, z1 = over_y(x1), over_z(x1)
    yd, zd = over_y(z0), over_z(y1)
    y2, z2 = over_y(x2), over_z(x2)
    dc = over_core(deltas)
    dxc = over_core(dx)
    all_deltas = [deltas, dc, dx, dxc]

    def delta_at(where_ref, slot):
        return ((slot // local_slots) ^ where_ref[0]) * local_slots + slot % local_slots

    def units_of(pieces):
        units = []
        for w, (a, flip_f, flip_cell, first) in enumerate(pieces):
            for k in range(a.shape[0] // BLOCK):
                def column(where_ref, flip_f=flip_f, flip_cell=flip_cell, at=first + k * BLOCK):
                    base = (where_ref[0] ^ flip_f) * (quarter // BLOCK)
                    if flip_cell is not None:
                        base = base + (where_ref[1] ^ flip_cell) * (part // BLOCK)
                    return base + at // BLOCK
                units.append((w, k * BLOCK, column))
        return units

    def grad_of(pieces, out):
        return rows_grad(
            units_of(pieces), [p[0] for p in pieces], *pattern, upstream, all_deltas,
            delta_at, width, out,
        )

    def both(a, flip_cell, first):
        return [(a, 2, flip_cell, first), (over_core(a), 3, flip_cell, first)]

    half = local_slots // 2

    def place(where_ref, slot):
        rel = (slot // local_slots) ^ where_ref[0]
        at = slot % local_slots
        index = (rel // 2) * local_slots + ((at // half) ^ (where_ref[1] % 2)) * half + at % half
        return rel % 2, index

    keep, send = block_grads(
        place, [2 * local_slots, 2 * local_slots], *pattern, activations, upstream
    )
    summed = keep + over_core(send)
    owned = summed[:local_slots] + over_x(summed[local_slots:])
    mine = owned[:half] + over_z(owned[half:])
    mine = mine + over_z(mine, 2)
    other = over_z(mine)
    normalizer = 1.0 / math.sqrt(upstream.shape[0] * lax.axis_size("fsdp") * n_dp)
    totals = jnp.where(
        even == 0,
        jnp.concatenate([mine, other], axis=0),
        jnp.concatenate([other, mine], axis=0),
    ) * normalizer

    out = grad_of([(frozen, 0, None, 0)], None)
    out = grad_of([(sib, 1, None, 0)], out)
    out = grad_of(
        both(x0, 0, offs[0]) + both(x1, 0, offs[1]) + both(y0, 2, offs[0]) + both(z0, 1, offs[0]), out
    )
    out = grad_of(
        both(y1, 2, offs[1]) + both(z1, 1, offs[1]) + both(yd, 3, offs[0]) + both(zd, 3, offs[1])
        + both(x2, 0, offs[2]), out,
    )
    out = grad_of(both(x3, 3, offs[2]) + both(y2, 2, offs[2]) + both(z2, 1, offs[2]), out)
    return out, totals


def normalized(activations, upstream, frozen, deltas, block_rows, block_cols, block_slot):
    out, totals = gathered(
        activations, upstream, frozen, deltas, block_rows, block_cols, block_slot
    )
    tokens = upstream.shape[0] * lax.axis_size("fsdp") * lax.axis_size("dp")
    return out, totals * (1.0 / math.sqrt(tokens))


def solution(mesh):
    sizes = dict(mesh.shape)
    cells = sizes["fsdp"] == 4 and sizes["group"] == 2 and sizes["dp"] == 4
    return jax.shard_map(
        relayed if cells else normalized,
        mesh=mesh,
        in_specs=(
            P(("group", "fsdp", "dp"), None),
            P(("group", "fsdp", "dp"), None),
            P("fsdp", None),
            P(("group", "fsdp"), None, None),
            P(),
            P(),
            P(),
        ),
        out_specs=(P(("group", "fsdp", "dp"), None), P(("group", "fsdp"), None, None)),
        check_vma=False,
    )
```

time: 245 us -> 121 us (0.49)
  waiting for transfers between devices: 151 us -> 34.4 us
  Pallas kernels: 0 us -> 36.3 us
  starting transfers between devices: 0.08 us -> 31.3 us
  local copies, waits for them, and re-layouts: 35.9 us -> 12.9 us
  matrix products: 20.4 us -> 0 us
  between operations: 15.5 us -> 1.23 us
  other arithmetic: 12.6 us -> 2.91 us
  blocking collectives: 8.6 us -> 0 us
    psum x1 -> x0, waiting for transfers between devices: 151 us -> none  [per_device(): totals = lax.psum(partial_grad, ('fsdp', 'dp'))]
    pallas_call x0 -> x6, Pallas kernels: none -> 36.3 us  [the longest x5 31.4 us: rows_grad(): pl.pallas_call(functools.partial(rows_kernel, units, tile, width // BLOCK...]
    ppermute x0 -> x33, waiting for transfers between devices: none -> 34.4 us  [the longest x6 18.4 us: over_x(): return lax.ppermute(a, 'fsdp', [(k, k ^ 2) for k in range(4)])]
    ppermute x0 -> x33, starting transfers between devices: none -> 31.3 us  [the longest x7 13 us: over_z(): return lax.ppermute(a, 'dp', [(k, k ^ step) for k in range(n_dp)])]
    dot_general x3 -> x0, matrix products: 20.4 us -> none  [the longest x1 14.7 us: contract_rows(): lax.dot_general(left, right, (((1,), (1,)), ((), ())), preferred_element_...]
    reshape x2 -> x0, local copies, waits for them, and re-layouts: 9.02 us -> none  [the longest x1 8.64 us: per_device(): activations.reshape(tok_rows, row_blocks, BLOCK)]
    broadcast_in_dim x1 -> x0, local copies, waits for them, and re-layouts: 8.94 us -> none  [per_device(): jnp.zeros((tok_rows, row_blocks, BLOCK), jnp.float32).at[:, block_rows, :]]
    all_gather x1 -> x0, blocking collectives: 8.6 us -> none  [per_device(): gathered_deltas = lax.all_gather(deltas, 'fsdp', axis=0, tiled=True)]
  transfers between devices with their start and end apart: 2 -> 33, of which waited for: 1 -> 10; matrix products, arithmetic and copies ran while one was open for 9% -> 4% of each run, Pallas kernels for 0% -> 26%
where the time goes in v1:
time: 121 us; the launch traced here: 119 us
  Pallas kernels  36.3 us (30%)
  waiting for transfers between devices  34.4 us (28%)
  starting transfers between devices  31.3 us (26%)
  local copies, waits for them, and re-layouts  12.9 us (11%)
  other arithmetic  2.91 us (2%)
  between operations  1.23 us (1%)
    pallas_call x5, Pallas kernels, rows_grad(): pl.pallas_call(functools.partial(rows_kernel, units, tile, width // BLOCK...  31.4 us
    ppermute x6, waiting for transfers between devices, over_x(): return lax.ppermute(a, 'fsdp', [(k, k ^ 2) for k in range(4)])  18.4 us
    ppermute x7, waiting for transfers between devices, over_z(): return lax.ppermute(a, 'dp', [(k, k ^ step) for k in range(n_dp)])  14.6 us
    ppermute x7, starting transfers between devices, over_z(): return lax.ppermute(a, 'dp', [(k, k ^ step) for k in range(n_dp)])  13 us
    unnamed x70, local copies, waits for them, and re-layouts  10.5 us
    ppermute x6, starting transfers between devices, over_x(): return lax.ppermute(a, 'fsdp', [(k, k ^ 2) for k in range(4)])  9.63 us
    ppermute x4, starting transfers between devices, over_y(): return lax.ppermute(a, 'group', [(k, k ^ 1) for k in range(2)])  5.31 us
    pallas_call x1, Pallas kernels, block_grads(): pl.pallas_call(functools.partial(grad_kernel, place, len(shapes)), out_sh...  4.9 us
  transfers between devices with their start and end apart: 33, of which 10 were waited for; matrix products, arithmetic and copies ran while one was open for 4% of the time, Pallas kernels for 26%

profile of v1, /device:TPU:0, one launch (start us, length us, event | category | flops | bytes accessed | tf_op | source)
XLA Modules:
  0.0 119.0 jit_solution(10730703714129565168)
XLA Ops:
  1.2 2.6 %collective-permute-start.8 = (bf16[4,128,128]{2,1,0:T(8,128)(2,1)}, bf16[4,128,128]{2,1,0:T(8,128)(2,1)S(1)}, u32[]{:S(2)}, u32[]{:S(2)}) collective-permute-start(bf16[4,128,128]{2,1,0:T(8,128)(2,1)} %refs_6_.1), channel_id=1, source_target_pairs={{0,8},{4,12},{8,0},{12,4},{1,9},{5,13},{9,1},{13,5},{2,10},{6,14},... | collective-permute-start | bytes 393224 | tf_op jit(solution)/shard_map/ppermute | solution.py:266
  5.0 1.1 copy-done
  6.1 2.8 %copy-done.3 = bf16[384,8192]{1,0:T(8,128)(2,1)S(1)} copy-done((bf16[384,8192]{1,0:T(8,128)(2,1)S(1)}, bf16[384,8192]{1,0:T(8,128)(2,1)}, u32[]{:S(2)}) %copy-start.3) | copy-done | bytes 6291480
  10.9 4.9 %block_grads.1 = (f32[8,128,128]{2,1,0:T(8,128)S(1)}, f32[8,128,128]{2,1,0:T(8,128)S(1)}) custom-call(s32[2]{0:T(128)S(1)} %pad_add_fusion.where_ref, s32[16]{0:T(128)S(1)} %copy-done.29, s32[16]{0:T(128)S(1)} %copy-done.31, s32[16]{0:T(128)S(1)} %copy-done.33, bf16[384,8192]{1,0:T(8,128)(2,1)S(1)} %copy-done.3, bf16[384,1024]{1,0:T(8,128)(2,1)S(1)} %copy-done), custom_call_target="tpu_custom_call" | custom-call | flops 201326592 | bytes 6291456 | tf_op jit(solution)/shard_map/block_grads/pallas_call | solution.py:61
  16.4 2.0 %collective-permute-start.10 = (bf16[128,1024]{1,0:T(8,128)(2,1)S(1)}, bf16[128,1024]{1,0:T(8,128)(2,1)S(1)}, u32[]{:S(2)}, u32[]{:S(2)}) collective-permute-start(bf16[128,1024]{1,0:T(8,128)(2,1)S(1)} %get-tuple-element.7), channel_id=1, source_target_pairs={{0,8},{4,12},{8,0},{12,4},{1,9},{5,13},{9,1},{13,5},{2,10},{6,14},... | collective-permute-start | bytes 786440 | tf_op jit(solution)/shard_map/ppermute | solution.py:266
  18.4 1.7 %collective-permute-start.24 = (bf16[128,1024]{1,0:T(8,128)(2,1)S(1)}, bf16[128,1024]{1,0:T(8,128)(2,1)S(1)}, u32[]{:S(2)}, u32[]{:S(2)}) collective-permute-start(bf16[128,1024]{1,0:T(8,128)(2,1)S(1)} %collective-permute-done.15.refs_0_), channel_id=1, source_target_pairs={{0,16},{16,0},{1,17},{17,1},{2,18},{18,2},{3,19},{19,3},{4,20},{20... | collective-permute-start | bytes 786440 | tf_op jit(solution)/shard_map/ppermute | solution.py:269
  20.1 1.3 %constant_dynamic-slice_fusion.2 = (bf16[256,1024]{1,0:T(8,128)(2,1)S(1)}, bf16[256,1024]{1,0:T(8,128)(2,1)S(1)}) fusion(bf16[2048,1024]{1,0:T(8,128)(2,1)} %refs_0_.1, s32[]{:T(128)S(6)} %select_n.29, s32[]{:T(128)S(6)} %select_n.28), kind=kLoop, calls=%fused_computation.6 | loop fusion | bytes 2097160 | tf_op jit(solution)/shard_map/dynamic_slice | solution.py:279
  21.4 1.6 %collective-permute-start.16 = (bf16[128,1024]{1,0:T(8,128)(2,1)S(1)}, bf16[128,1024]{1,0:T(8,128)(2,1)S(1)}, u32[]{:S(2)}, u32[]{:S(2)}) collective-permute-start(bf16[128,1024]{1,0:T(8,128)(2,1)S(1)} %collective-permute-done.15.refs_0_), channel_id=1, source_target_pairs={{0,1},{1,0},{2,3},{3,2},{4,5},{5,4},{6,7},{7,6},{8,9},{9,8},{10,11... | collective-permute-start | bytes 786440 | tf_op jit(solution)/shard_map/ppermute | solution.py:272
  23.0 1.9 %collective-permute-done.10.refs_2_ = bf16[128,1024]{1,0:T(8,128)(2,1)S(1)} collective-permute-done((bf16[128,1024]{1,0:T(8,128)(2,1)S(1)}, bf16[128,1024]{1,0:T(8,128)(2,1)S(1)}, u32[]{:S(2)}, u32[]{:S(2)}) %collective-permute-start.10) | collective-permute-done | bytes 262176 | tf_op jit(solution)/shard_map/ppermute | solution.py:266
  24.9 1.7 %collective-permute-start.2 = (bf16[256,1024]{1,0:T(8,128)(2,1)S(1)}, bf16[256,1024]{1,0:T(8,128)(2,1)S(1)}, u32[]{:S(2)}, u32[]{:S(2)}) collective-permute-start(bf16[256,1024]{1,0:T(8,128)(2,1)S(1)} %get-tuple-element.8), channel_id=1, source_target_pairs={{0,8},{4,12},{8,0},{12,4},{1,9},{5,13},{9,1},{13,5},{2,10},{6,14},... | collective-permute-start | bytes 1572872 | tf_op jit(solution)/shard_map/ppermute | solution.py:266
  27.2 2.6 %collective-permute-done.16.refs_6_ = bf16[128,1024]{1,0:T(8,128)(2,1)S(1)} collective-permute-done((bf16[128,1024]{1,0:T(8,128)(2,1)S(1)}, bf16[128,1024]{1,0:T(8,128)(2,1)S(1)}, u32[]{:S(2)}, u32[]{:S(2)}) %collective-permute-start.16) | collective-permute-done | bytes 262176 | tf_op jit(solution)/shard_map/ppermute | solution.py:272
  29.7 1.5 %collective-permute-start = (bf16[256,1024]{1,0:T(8,128)(2,1)S(1)}, bf16[256,1024]{1,0:T(8,128)(2,1)S(1)}, u32[]{:S(2)}, u32[]{:S(2)}) collective-permute-start(bf16[256,1024]{1,0:T(8,128)(2,1)S(1)} %get-tuple-element.9), channel_id=1, source_target_pairs={{0,8},{4,12},{8,0},{12,4},{1,9},{5,13},{9,1},{13,5},{2,10},{6,14},... | collective-permute-start | bytes 1572872 | tf_op jit(solution)/shard_map/ppermute | solution.py:266
  31.8 1.6 %collective-permute-start.13 = (bf16[128,1024]{1,0:T(8,128)(2,1)S(1)}, bf16[128,1024]{1,0:T(8,128)(2,1)}, u32[]{:S(2)}, u32[]{:S(2)}) collective-permute-start(bf16[128,1024]{1,0:T(8,128)(2,1)S(1)} %collective-permute-done.10.refs_2_), channel_id=1, source_target_pairs={{0,1},{1,0},{2,3},{3,2},{4,5},{5,4},{6,7},{7,6},{8,9},{9,8},{10,11... | collective-permute-start | bytes 786440 | tf_op jit(solution)/shard_map/ppermute | solution.py:272
  33.3 1.1 add.55
  34.5 5.3 %collective-permute-done.2.refs_8_ = bf16[256,1024]{1,0:T(8,128)(2,1)S(1)} collective-permute-done((bf16[256,1024]{1,0:T(8,128)(2,1)S(1)}, bf16[256,1024]{1,0:T(8,128)(2,1)S(1)}, u32[]{:S(2)}, u32[]{:S(2)}) %collective-permute-start.2) | collective-permute-done | bytes 524320 | tf_op jit(solution)/shard_map/ppermute | solution.py:266
  39.8 1.7 %collective-permute-start.29 = (f32[4,128,128]{2,1,0:T(8,128)S(1)}, f32[4,128,128]{2,1,0:T(8,128)S(1)}, u32[]{:S(2)}, u32[]{:S(2)}) collective-permute-start(f32[4,128,128]{2,1,0:T(8,128)S(1)} %slice.17), channel_id=1, source_target_pairs={{0,8},{4,12},{8,0},{12,4},{1,9},{5,13},{9,1},{13,5},{2,10},{6,14},... | collective-permute-start | bytes 786440 | tf_op jit(solution)/shard_map/ppermute | solution.py:266
  42.0 9.0 %collective-permute-done.refs_0_ = bf16[256,1024]{1,0:T(8,128)(2,1)S(1)} collective-permute-done((bf16[256,1024]{1,0:T(8,128)(2,1)S(1)}, bf16[256,1024]{1,0:T(8,128)(2,1)S(1)}, u32[]{:S(2)}, u32[]{:S(2)}) %collective-permute-start) | collective-permute-done | bytes 524320 | tf_op jit(solution)/shard_map/ppermute | solution.py:266
  51.0 1.8 %collective-permute-start.17 = (bf16[128,1024]{1,0:T(8,128)(2,1)S(1)}, bf16[128,1024]{1,0:T(8,128)(2,1)S(1)}, u32[]{:S(2)}, u32[]{:S(2)}) collective-permute-start(bf16[128,1024]{1,0:T(8,128)(2,1)S(1)} %collective-permute-done.16.refs_6_), channel_id=1, source_target_pairs={{0,16},{16,0},{1,17},{17,1},{2,18},{18,2},{3,19},{19,3},{4,20},{20... | collective-permute-start | bytes 786440 | tf_op jit(solution)/shard_map/ppermute | solution.py:269
  52.8 2.3 %collective-permute-done.29 = f32[4,128,128]{2,1,0:T(8,128)S(1)} collective-permute-done((f32[4,128,128]{2,1,0:T(8,128)S(1)}, f32[4,128,128]{2,1,0:T(8,128)S(1)}, u32[]{:S(2)}, u32[]{:S(2)}) %collective-permute-start.29) | collective-permute-done | bytes 262176 | tf_op jit(solution)/shard_map/ppermute | solution.py:266
  55.1 1.6 %collective-permute-start.19 = (bf16[128,1024]{1,0:T(8,128)(2,1)S(1)}, bf16[128,1024]{1,0:T(8,128)(2,1)S(1)}, u32[]{:S(2)}, u32[]{:S(2)}) collective-permute-start(bf16[128,1024]{1,0:T(8,128)(2,1)S(1)} %collective-permute-done.11.refs_0_), channel_id=1, source_target_pairs={{0,1},{1,0},{2,3},{3,2},{4,5},{5,4},{6,7},{7,6},{8,9},{9,8},{10,11... | collective-permute-start | bytes 786440 | tf_op jit(solution)/shard_map/ppermute | solution.py:272
  59.3 3.9 %collective-permute-done.19.refs_6_ = bf16[128,1024]{1,0:T(8,128)(2,1)S(1)} collective-permute-done((bf16[128,1024]{1,0:T(8,128)(2,1)S(1)}, bf16[128,1024]{1,0:T(8,128)(2,1)S(1)}, u32[]{:S(2)}, u32[]{:S(2)}) %collective-permute-start.19) | collective-permute-done | bytes 262176 | tf_op jit(solution)/shard_map/ppermute | solution.py:272
  63.3 1.3 %collective-permute-start.3 = (bf16[256,1024]{1,0:T(8,128)(2,1)S(1)}, bf16[256,1024]{1,0:T(8,128)(2,1)S(1)}, u32[]{:S(2)}, u32[]{:S(2)}) collective-permute-start(bf16[256,1024]{1,0:T(8,128)(2,1)S(1)} %collective-permute-done.2.refs_8_), channel_id=1, source_target_pairs={{0,16},{16,0},{1,17},{17,1},{2,18},{18,2},{3,19},{19,3},{4,20},{20... | collective-permute-start | bytes 1572872 | tf_op jit(solution)/shard_map/ppermute | solution.py:269
  64.7 1.5 %collective-permute-start.5 = (bf16[256,1024]{1,0:T(8,128)(2,1)S(1)}, bf16[256,1024]{1,0:T(8,128)(2,1)S(1)}, u32[]{:S(2)}, u32[]{:S(2)}) collective-permute-start(bf16[256,1024]{1,0:T(8,128)(2,1)S(1)} %collective-permute-done.2.refs_8_), channel_id=1, source_target_pairs={{0,1},{1,0},{2,3},{3,2},{4,5},{5,4},{6,7},{7,6},{8,9},{9,8},{10,11... | collective-permute-start | bytes 1572872 | tf_op jit(solution)/shard_map/ppermute | solution.py:272
  67.0 2.6 %collective-permute-start.31 = (f32[2,128,128]{2,1,0:T(8,128)S(1)}, f32[2,128,128]{2,1,0:T(8,128)}, u32[]{:S(2)}, u32[]{:S(2)}) collective-permute-start(f32[2,128,128]{2,1,0:T(8,128)S(1)} %slice_add_fusion.1), channel_id=1, source_target_pairs={{0,2},{1,3},{2,0},{3,1},{4,6},{5,7},{6,4},{7,5},{8,10},{9,11},{10,... | collective-permute-start | bytes 393224 | tf_op jit(solution)/shard_map/ppermute | solution.py:272
  69.6 8.0 %collective-permute-done.31 = f32[2,128,128]{2,1,0:T(8,128)} collective-permute-done((f32[2,128,128]{2,1,0:T(8,128)S(1)}, f32[2,128,128]{2,1,0:T(8,128)}, u32[]{:S(2)}, u32[]{:S(2)}) %collective-permute-start.31) | collective-permute-done | bytes 131104 | tf_op jit(solution)/shard_map/ppermute | solution.py:272
  79.6 3.6 %collective-permute-start.32 = (f32[2,128,128]{2,1,0:T(8,128)S(1)}, f32[2,128,128]{2,1,0:T(8,128)S(1)}, u32[]{:S(2)}, u32[]{:S(2)}) collective-permute-start(f32[2,128,128]{2,1,0:T(8,128)S(1)} %add.58), channel_id=1, source_target_pairs={{0,1},{1,0},{2,3},{3,2},{4,5},{5,4},{6,7},{7,6},{8,9},{9,8},{10,11... | collective-permute-start | bytes 393224 | tf_op jit(solution)/shard_map/ppermute | solution.py:272
  83.8 2.2 %copy-done.2 = bf16[2048,1024]{1,0:T(8,128)(2,1)S(1)} copy-done((bf16[2048,1024]{1,0:T(8,128)(2,1)S(1)}, bf16[2048,1024]{1,0:T(8,128)(2,1)}, u32[]{:S(2)}) %copy-start.2) | copy-done | bytes 4194328
  85.9 8.3 %rows_grad.5.refs_5_ = bf16[384,8192]{1,0:T(8,128)(2,1)} custom-call(s32[2]{0:T(128)S(1)} %pad_add_fusion.where_ref, s32[16]{0:T(128)S(1)} %copy-done.30, s32[16]{0:T(128)S(1)} %copy-done.32, s32[16]{0:T(128)S(1)} %copy-done.34, bf16[384,1024]{1,0:T(8,128)(2,1)S(1)} %copy-done.1, bf16[2048,1024]{1,0:T(8,128)(2,1)S(1)} %copy-done.2, ...), custom_call_target="tpu_custom_call" | custom-call | flops 1610612736 | bytes 5767168 | tf_op jit(solution)/shard_map/rows_grad/pallas_call | solution.py:187
  95.6 6.4 %rows_grad.6.refs_12_ = bf16[384,8192]{1,0:T(8,128)(2,1)} custom-call(s32[2]{0:T(128)S(1)} %pad_add_fusion.where_ref, s32[16]{0:T(128)S(1)} %copy-done.30, s32[16]{0:T(128)S(1)} %copy-done.32, s32[16]{0:T(128)S(1)} %copy-done.34, bf16[384,1024]{1,0:T(8,128)(2,1)S(1)} %copy-done.1, ...), custom_call_target="tpu_custom_call", output_to_operand_aliasing={{}: (10, {})} | custom-call | flops 1610612736 | bytes 5767168 | tf_op jit(solution)/shard_map/rows_grad/pallas_call | solution.py:187
  102.1 5.1 %rows_grad.7.refs_14_ = bf16[384,8192]{1,0:T(8,128)(2,1)} custom-call(s32[2]{0:T(128)S(1)} %pad_add_fusion.where_ref, s32[16]{0:T(128)S(1)} %copy-done.30, s32[16]{0:T(128)S(1)} %copy-done.32, s32[16]{0:T(128)S(1)} %copy-done.34, bf16[384,1024]{1,0:T(8,128)(2,1)S(1)} %copy-done.1, bf16[128,1024]{1,0:T(8,128)(2,1)S(1)} %copy-done.6, ...), custom_call_target="tpu_custom_call", output_to_operand_aliasing={{}: (17, {})} | custom-call | flops 805306368 | bytes 2883584 | tf_op jit(solution)/shard_map/rows_grad/pallas_call | solution.py:187
  107.3 6.1 %rows_grad.8.refs_10_ = bf16[384,8192]{1,0:T(8,128)(2,1)} custom-call(s32[2]{0:T(128)S(1)} %pad_add_fusion.where_ref, s32[16]{0:T(128)S(1)} %copy-done.30, s32[16]{0:T(128)S(1)} %copy-done.32, s32[16]{0:T(128)S(1)} %copy-done.34, bf16[384,1024]{1,0:T(8,128)(2,1)S(1)} %copy-done.1, bf16[128,1024]{1,0:T(8,128)(2,1)S(1)} %copy-done.18, ...), custom_call_target="tpu_custom_call", output_to_operand_aliasing={{}: (19, {})} | custom-call | flops 1207959552 | bytes 4325376 | tf_op jit(solution)/shard_map/rows_grad/pallas_call | solution.py:187
  113.4 5.5 %rows_grad.9 = bf16[384,8192]{1,0:T(8,128)(2,1)} custom-call(s32[2]{0:T(128)S(1)} %pad_add_fusion.where_ref, s32[16]{0:T(128)S(1)} %copy-done.30, s32[16]{0:T(128)S(1)} %copy-done.32, s32[16]{0:T(128)S(1)} %copy-done.34, bf16[384,1024]{1,0:T(8,128)(2,1)S(1)} %copy-done.1, ...), custom_call_target="tpu_custom_call", output_to_operand_aliasing={{}: (15, {})} | custom-call | flops 1207959552 | bytes 4325376 | tf_op jit(solution)/shard_map/rows_grad/pallas_call | solution.py:187
  (120 shorter events, 13.3 us)
Async XLA Ops:
  0.6 93.7 %collective-permute-start.27 = (bf16[2048,1024]{1,0:T(8,128)(2,1)}, bf16[2048,1024]{1,0:T(8,128)(2,1)}, u32[]{:S(2)}, u32[]{:S(2)}) collective-permute-start(bf16[2048,1024]{1,0:T(8,128)(2,1)} %refs_0_.1), channel_id=1, source_target_pairs={{0,4},{4,0},{8,12},{12,8},{1,5},{5,1},{9,13},{13,9},{2,6},{6,2},{1... | collective-permute-start | bytes 12582920 | tf_op jit(solution)/shard_map/ppermute | solution.py:263
  1.2 15.2 %collective-permute-start.8 = (bf16[4,128,128]{2,1,0:T(8,128)(2,1)}, bf16[4,128,128]{2,1,0:T(8,128)(2,1)S(1)}, u32[]{:S(2)}, u32[]{:S(2)}) collective-permute-start(bf16[4,128,128]{2,1,0:T(8,128)(2,1)} %refs_6_.1), channel_id=1, source_target_pairs={{0,8},{4,12},{8,0},{12,4},{1,9},{5,13},{9,1},{13,5},{2,10},{6,14},... | collective-permute-start | bytes 393224 | tf_op jit(solution)/shard_map/ppermute | solution.py:266
  4.8 13.6 %collective-permute-start.15 = (bf16[128,1024]{1,0:T(8,128)(2,1)S(1)}, bf16[128,1024]{1,0:T(8,128)(2,1)S(1)}, u32[]{:S(2)}, u32[]{:S(2)}) collective-permute-start(bf16[128,1024]{1,0:T(8,128)(2,1)S(1)} %get-tuple-element.6), channel_id=1, source_target_pairs={{0,8},{4,12},{8,0},{12,4},{1,9},{5,13},{9,1},{13,5},{2,10},{6,14},... | collective-permute-start | bytes 786440 | tf_op jit(solution)/shard_map/ppermute | solution.py:266
  15.8 10.8 %collective-permute-start.28 = (f32[8,128,128]{2,1,0:T(8,128)S(1)}, f32[8,128,128]{2,1,0:T(8,128)}, u32[]{:S(2)}, u32[]{:S(2)}) collective-permute-start(f32[8,128,128]{2,1,0:T(8,128)S(1)} %get-tuple-element.5), channel_id=1, source_target_pairs={{0,4},{4,0},{8,12},{12,8},{1,5},{5,1},{9,13},{13,9},{2,6},{6,2},{1... | collective-permute-start | bytes 1572872 | tf_op jit(solution)/shard_map/ppermute | solution.py:263
  16.0 2.4 %collective-permute-start.7 = (bf16[4,128,128]{2,1,0:T(8,128)(2,1)S(1)}, bf16[4,128,128]{2,1,0:T(8,128)(2,1)S(1)}, u32[]{:S(2)}, u32[]{:S(2)}) collective-permute-start(bf16[4,128,128]{2,1,0:T(8,128)(2,1)S(1)} %copy-done.4), channel_id=1, source_target_pairs={{0,4},{4,0},{8,12},{12,8},{1,5},{5,1},{9,13},{13,9},{2,6},{6,2},{1... | collective-permute-start | bytes 393224 | tf_op jit(solution)/shard_map/ppermute | solution.py:263
  16.4 8.5 %collective-permute-start.10 = (bf16[128,1024]{1,0:T(8,128)(2,1)S(1)}, bf16[128,1024]{1,0:T(8,128)(2,1)S(1)}, u32[]{:S(2)}, u32[]{:S(2)}) collective-permute-start(bf16[128,1024]{1,0:T(8,128)(2,1)S(1)} %get-tuple-element.7), channel_id=1, source_target_pairs={{0,8},{4,12},{8,0},{12,4},{1,9},{5,13},{9,1},{13,5},{2,10},{6,14},... | collective-permute-start | bytes 786440 | tf_op jit(solution)/shard_map/ppermute | solution.py:266
  18.3 3.0 %collective-permute-start.9 = (bf16[4,128,128]{2,1,0:T(8,128)(2,1)S(1)}, bf16[4,128,128]{2,1,0:T(8,128)(2,1)S(1)}, u32[]{:S(2)}, u32[]{:S(2)}) collective-permute-start(bf16[4,128,128]{2,1,0:T(8,128)(2,1)S(1)} %collective-permute-done.8.refs_3_.refs_10_.refs_12_.refs_8_), channel_id=1, source_target_pairs={{0,4},{4,0},{8,12},{12,8},{1,5},{5,1},{9,13},{13,9},{2,6},{6,2},{1... | collective-permute-start | bytes 393224 | tf_op jit(solution)/shard_map/ppermute | solution.py:263
  18.4 8.7 %collective-permute-start.24 = (bf16[128,1024]{1,0:T(8,128)(2,1)S(1)}, bf16[128,1024]{1,0:T(8,128)(2,1)S(1)}, u32[]{:S(2)}, u32[]{:S(2)}) collective-permute-start(bf16[128,1024]{1,0:T(8,128)(2,1)S(1)} %collective-permute-done.15.refs_0_), channel_id=1, source_target_pairs={{0,16},{16,0},{1,17},{17,1},{2,18},{18,2},{3,19},{19,3},{4,20},{20... | collective-permute-start | bytes 786440 | tf_op jit(solution)/shard_map/ppermute | solution.py:269
  21.4 8.4 %collective-permute-start.16 = (bf16[128,1024]{1,0:T(8,128)(2,1)S(1)}, bf16[128,1024]{1,0:T(8,128)(2,1)S(1)}, u32[]{:S(2)}, u32[]{:S(2)}) collective-permute-start(bf16[128,1024]{1,0:T(8,128)(2,1)S(1)} %collective-permute-done.15.refs_0_), channel_id=1, source_target_pairs={{0,1},{1,0},{2,3},{3,2},{4,5},{5,4},{6,7},{7,6},{8,9},{9,8},{10,11... | collective-permute-start | bytes 786440 | tf_op jit(solution)/shard_map/ppermute | solution.py:272
  24.9 14.9 %collective-permute-start.2 = (bf16[256,1024]{1,0:T(8,128)(2,1)S(1)}, bf16[256,1024]{1,0:T(8,128)(2,1)S(1)}, u32[]{:S(2)}, u32[]{:S(2)}) collective-permute-start(bf16[256,1024]{1,0:T(8,128)(2,1)S(1)} %get-tuple-element.8), channel_id=1, source_target_pairs={{0,8},{4,12},{8,0},{12,4},{1,9},{5,13},{9,1},{13,5},{2,10},{6,14},... | collective-permute-start | bytes 1572872 | tf_op jit(solution)/shard_map/ppermute | solution.py:266
  26.6 4.6 %collective-permute-start.22 = (bf16[128,1024]{1,0:T(8,128)(2,1)S(1)}, bf16[128,1024]{1,0:T(8,128)(2,1)S(1)}, u32[]{:S(2)}, u32[]{:S(2)}) collective-permute-start(bf16[128,1024]{1,0:T(8,128)(2,1)S(1)} %collective-permute-done.15.refs_0_), channel_id=1, source_target_pairs={{0,4},{4,0},{8,12},{12,8},{1,5},{5,1},{9,13},{13,9},{2,6},{6,2},{1... | collective-permute-start | bytes 786440 | tf_op jit(solution)/shard_map/ppermute | solution.py:263
  27.1 4.7 %collective-permute-start.23 = (bf16[128,1024]{1,0:T(8,128)(2,1)S(1)}, bf16[128,1024]{1,0:T(8,128)(2,1)S(1)}, u32[]{:S(2)}, u32[]{:S(2)}) collective-permute-start(bf16[128,1024]{1,0:T(8,128)(2,1)S(1)} %collective-permute-done.10.refs_2_), channel_id=1, source_target_pairs={{0,4},{4,0},{8,12},{12,8},{1,5},{5,1},{9,13},{13,9},{2,6},{6,2},{1... | collective-permute-start | bytes 786440 | tf_op jit(solution)/shard_map/ppermute | solution.py:263
  29.7 21.2 %collective-permute-start = (bf16[256,1024]{1,0:T(8,128)(2,1)S(1)}, bf16[256,1024]{1,0:T(8,128)(2,1)S(1)}, u32[]{:S(2)}, u32[]{:S(2)}) collective-permute-start(bf16[256,1024]{1,0:T(8,128)(2,1)S(1)} %get-tuple-element.9), channel_id=1, source_target_pairs={{0,8},{4,12},{8,0},{12,4},{1,9},{5,13},{9,1},{13,5},{2,10},{6,14},... | collective-permute-start | bytes 1572872 | tf_op jit(solution)/shard_map/ppermute | solution.py:266
  31.2 10.3 %collective-permute-start.11 = (bf16[128,1024]{1,0:T(8,128)(2,1)S(1)}, bf16[128,1024]{1,0:T(8,128)(2,1)S(1)}, u32[]{:S(2)}, u32[]{:S(2)}) collective-permute-start(bf16[128,1024]{1,0:T(8,128)(2,1)S(1)} %collective-permute-done.10.refs_2_), channel_id=1, source_target_pairs={{0,16},{16,0},{1,17},{17,1},{2,18},{18,2},{3,19},{19,3},{4,20},{20... | collective-permute-start | bytes 786440 | tf_op jit(solution)/shard_map/ppermute | solution.py:269
  31.8 9.8 %collective-permute-start.13 = (bf16[128,1024]{1,0:T(8,128)(2,1)S(1)}, bf16[128,1024]{1,0:T(8,128)(2,1)}, u32[]{:S(2)}, u32[]{:S(2)}) collective-permute-start(bf16[128,1024]{1,0:T(8,128)(2,1)S(1)} %collective-permute-done.10.refs_2_), channel_id=1, source_target_pairs={{0,1},{1,0},{2,3},{3,2},{4,5},{5,4},{6,7},{7,6},{8,9},{9,8},{10,11... | collective-permute-start | bytes 786440 | tf_op jit(solution)/shard_map/ppermute | solution.py:272
  39.8 15.3 %collective-permute-start.29 = (f32[4,128,128]{2,1,0:T(8,128)S(1)}, f32[4,128,128]{2,1,0:T(8,128)S(1)}, u32[]{:S(2)}, u32[]{:S(2)}) collective-permute-start(f32[4,128,128]{2,1,0:T(8,128)S(1)} %slice.17), channel_id=1, source_target_pairs={{0,8},{4,12},{8,0},{12,4},{1,9},{5,13},{9,1},{13,5},{2,10},{6,14},... | collective-permute-start | bytes 786440 | tf_op jit(solution)/shard_map/ppermute | solution.py:266
  41.5 15.2 %collective-permute-start.25 = (bf16[128,1024]{1,0:T(8,128)(2,1)S(1)}, bf16[128,1024]{1,0:T(8,128)(2,1)S(1)}, u32[]{:S(2)}, u32[]{:S(2)}) collective-permute-start(bf16[128,1024]{1,0:T(8,128)(2,1)S(1)} %collective-permute-done.24.refs_4_), channel_id=1, source_target_pairs={{0,4},{4,0},{8,12},{12,8},{1,5},{5,1},{9,13},{13,9},{2,6},{6,2},{1... | collective-permute-start | bytes 786440 | tf_op jit(solution)/shard_map/ppermute | solution.py:263
  41.5 16.4 %collective-permute-start.26 = (bf16[128,1024]{1,0:T(8,128)(2,1)S(1)}, bf16[128,1024]{1,0:T(8,128)(2,1)S(1)}, u32[]{:S(2)}, u32[]{:S(2)}) collective-permute-start(bf16[128,1024]{1,0:T(8,128)(2,1)S(1)} %collective-permute-done.16.refs_6_), channel_id=1, source_target_pairs={{0,4},{4,0},{8,12},{12,8},{1,5},{5,1},{9,13},{13,9},{2,6},{6,2},{1... | collective-permute-start | bytes 786440 | tf_op jit(solution)/shard_map/ppermute | solution.py:263
  51.0 7.7 %collective-permute-start.17 = (bf16[128,1024]{1,0:T(8,128)(2,1)S(1)}, bf16[128,1024]{1,0:T(8,128)(2,1)S(1)}, u32[]{:S(2)}, u32[]{:S(2)}) collective-permute-start(bf16[128,1024]{1,0:T(8,128)(2,1)S(1)} %collective-permute-done.16.refs_6_), channel_id=1, source_target_pairs={{0,16},{16,0},{1,17},{17,1},{2,18},{18,2},{3,19},{19,3},{4,20},{20... | collective-permute-start | bytes 786440 | tf_op jit(solution)/shard_map/ppermute | solution.py:269
  55.1 8.2 %collective-permute-start.19 = (bf16[128,1024]{1,0:T(8,128)(2,1)S(1)}, bf16[128,1024]{1,0:T(8,128)(2,1)S(1)}, u32[]{:S(2)}, u32[]{:S(2)}) collective-permute-start(bf16[128,1024]{1,0:T(8,128)(2,1)S(1)} %collective-permute-done.11.refs_0_), channel_id=1, source_target_pairs={{0,1},{1,0},{2,3},{3,2},{4,5},{5,4},{6,7},{7,6},{8,9},{9,8},{10,11... | collective-permute-start | bytes 786440 | tf_op jit(solution)/shard_map/ppermute | solution.py:272
  57.5 7.2 %collective-permute-start.30 = (f32[2,128,128]{2,1,0:T(8,128)S(1)}, f32[2,128,128]{2,1,0:T(8,128)S(1)}, u32[]{:S(2)}, u32[]{:S(2)}) collective-permute-start(f32[2,128,128]{2,1,0:T(8,128)S(1)} %slice.19), channel_id=1, source_target_pairs={{0,1},{1,0},{2,3},{3,2},{4,5},{5,4},{6,7},{7,6},{8,9},{9,8},{10,11... | collective-permute-start | bytes 393224 | tf_op jit(solution)/shard_map/ppermute | solution.py:272
  58.6 7.6 %collective-permute-start.12 = (bf16[128,1024]{1,0:T(8,128)(2,1)S(1)}, bf16[128,1024]{1,0:T(8,128)(2,1)S(1)}, u32[]{:S(2)}, u32[]{:S(2)}) collective-permute-start(bf16[128,1024]{1,0:T(8,128)(2,1)S(1)} %collective-permute-done.11.refs_0_), channel_id=1, source_target_pairs={{0,4},{4,0},{8,12},{12,8},{1,5},{5,1},{9,13},{13,9},{2,6},{6,2},{1... | collective-permute-start | bytes 786440 | tf_op jit(solution)/shard_map/ppermute | solution.py:263
  58.6 20.9 %collective-permute-start.21 = (bf16[256,1024]{1,0:T(8,128)(2,1)S(1)}, bf16[256,1024]{1,0:T(8,128)(2,1)}, u32[]{:S(2)}, u32[]{:S(2)}) collective-permute-start(bf16[256,1024]{1,0:T(8,128)(2,1)S(1)} %collective-permute-done.2.refs_8_), channel_id=1, source_target_pairs={{0,4},{4,0},{8,12},{12,8},{1,5},{5,1},{9,13},{13,9},{2,6},{6,2},{1... | collective-permute-start | bytes 1572872 | tf_op jit(solution)/shard_map/ppermute | solution.py:263
  63.3 20.0 %collective-permute-start.3 = (bf16[256,1024]{1,0:T(8,128)(2,1)S(1)}, bf16[256,1024]{1,0:T(8,128)(2,1)S(1)}, u32[]{:S(2)}, u32[]{:S(2)}) collective-permute-start(bf16[256,1024]{1,0:T(8,128)(2,1)S(1)} %collective-permute-done.2.refs_8_), channel_id=1, source_target_pairs={{0,16},{16,0},{1,17},{17,1},{2,18},{18,2},{3,19},{19,3},{4,20},{20... | collective-permute-start | bytes 1572872 | tf_op jit(solution)/shard_map/ppermute | solution.py:269
  64.7 18.6 %collective-permute-start.5 = (bf16[256,1024]{1,0:T(8,128)(2,1)S(1)}, bf16[256,1024]{1,0:T(8,128)(2,1)S(1)}, u32[]{:S(2)}, u32[]{:S(2)}) collective-permute-start(bf16[256,1024]{1,0:T(8,128)(2,1)S(1)} %collective-permute-done.2.refs_8_), channel_id=1, source_target_pairs={{0,1},{1,0},{2,3},{3,2},{4,5},{5,4},{6,7},{7,6},{8,9},{9,8},{10,11... | collective-permute-start | bytes 1572872 | tf_op jit(solution)/shard_map/ppermute | solution.py:272
  67.0 10.6 %collective-permute-start.31 = (f32[2,128,128]{2,1,0:T(8,128)S(1)}, f32[2,128,128]{2,1,0:T(8,128)}, u32[]{:S(2)}, u32[]{:S(2)}) collective-permute-start(f32[2,128,128]{2,1,0:T(8,128)S(1)} %slice_add_fusion.1), channel_id=1, source_target_pairs={{0,2},{1,3},{2,0},{3,1},{4,6},{5,7},{6,4},{7,5},{8,10},{9,11},{10,... | collective-permute-start | bytes 393224 | tf_op jit(solution)/shard_map/ppermute | solution.py:272
  79.5 34.0 %collective-permute-start.1 = (bf16[256,1024]{1,0:T(8,128)(2,1)S(1)}, bf16[256,1024]{1,0:T(8,128)(2,1)S(1)}, u32[]{:S(2)}, u32[]{:S(2)}) collective-permute-start(bf16[256,1024]{1,0:T(8,128)(2,1)S(1)} %collective-permute-done.refs_0_), channel_id=1, source_target_pairs={{0,4},{4,0},{8,12},{12,8},{1,5},{5,1},{9,13},{13,9},{2,6},{6,2},{1... | collective-permute-start | bytes 1572872 | tf_op jit(solution)/shard_map/ppermute | solution.py:263
  79.6 14.6 %collective-permute-start.32 = (f32[2,128,128]{2,1,0:T(8,128)S(1)}, f32[2,128,128]{2,1,0:T(8,128)S(1)}, u32[]{:S(2)}, u32[]{:S(2)}) collective-permute-start(f32[2,128,128]{2,1,0:T(8,128)S(1)} %add.58), channel_id=1, source_target_pairs={{0,1},{1,0},{2,3},{3,2},{4,5},{5,4},{6,7},{7,6},{8,9},{9,8},{10,11... | collective-permute-start | bytes 393224 | tf_op jit(solution)/shard_map/ppermute | solution.py:272
  83.2 30.2 %collective-permute-start.4 = (bf16[256,1024]{1,0:T(8,128)(2,1)S(1)}, bf16[256,1024]{1,0:T(8,128)(2,1)S(1)}, u32[]{:S(2)}, u32[]{:S(2)}) collective-permute-start(bf16[256,1024]{1,0:T(8,128)(2,1)S(1)} %collective-permute-done.3.refs_2_), channel_id=1, source_target_pairs={{0,4},{4,0},{8,12},{12,8},{1,5},{5,1},{9,13},{13,9},{2,6},{6,2},{1... | collective-permute-start | bytes 1572872 | tf_op jit(solution)/shard_map/ppermute | solution.py:263
  83.3 30.1 %collective-permute-start.6 = (bf16[256,1024]{1,0:T(8,128)(2,1)S(1)}, bf16[256,1024]{1,0:T(8,128)(2,1)S(1)}, u32[]{:S(2)}, u32[]{:S(2)}) collective-permute-start(bf16[256,1024]{1,0:T(8,128)(2,1)S(1)} %collective-permute-done.5.refs_4_), channel_id=1, source_target_pairs={{0,4},{4,0},{8,12},{12,8},{1,5},{5,1},{9,13},{13,9},{2,6},{6,2},{1... | collective-permute-start | bytes 1572872 | tf_op jit(solution)/shard_map/ppermute | solution.py:263
  94.3 13.0 %collective-permute-start.18 = (bf16[128,1024]{1,0:T(8,128)(2,1)S(1)}, bf16[128,1024]{1,0:T(8,128)(2,1)S(1)}, u32[]{:S(2)}, u32[]{:S(2)}) collective-permute-start(bf16[128,1024]{1,0:T(8,128)(2,1)S(1)} %copy-done.22), channel_id=1, source_target_pairs={{0,4},{4,0},{8,12},{12,8},{1,5},{5,1},{9,13},{13,9},{2,6},{6,2},{1... | collective-permute-start | bytes 786440 | tf_op jit(solution)/shard_map/ppermute | solution.py:263
  94.4 12.9 %collective-permute-start.20 = (bf16[128,1024]{1,0:T(8,128)(2,1)S(1)}, bf16[128,1024]{1,0:T(8,128)(2,1)S(1)}, u32[]{:S(2)}, u32[]{:S(2)}) collective-permute-start(bf16[128,1024]{1,0:T(8,128)(2,1)S(1)} %copy-done.26), channel_id=1, source_target_pairs={{0,4},{4,0},{8,12},{12,8},{1,5},{5,1},{9,13},{13,9},{2,6},{6,2},{1... | collective-permute-start | bytes 786440 | tf_op jit(solution)/shard_map/ppermute | solution.py:263
  (36 other events, 678.7 us)

commit v2 on v1

v2 whole, which is shorter than its diff:
```python
import functools
import math

import jax
import jax.numpy as jnp
from jax import lax
from jax.experimental import pallas as pl
from jax.experimental.pallas import tpu as pltpu
from jax.sharding import PartitionSpec as P

BLOCK = 128
VMEM_BYTES = 60 * 1024 * 1024
ANY_SPEC = pl.BlockSpec(memory_space=pl.ANY)
HBM_SPEC = pl.BlockSpec(memory_space=pltpu.HBM)
COST = pl.CostEstimate(flops=1024, bytes_accessed=1024, transcendentals=0)
VMEM_SPEC = pl.BlockSpec(memory_space=pltpu.VMEM)


def dot_nt(left, right):
    return lax.dot_general(
        left, right, (((1,), (1,)), ((), ())), preferred_element_type=jnp.float32
    )


def dot_tn(left, right):
    return lax.dot_general(
        left, right, (((0,), (0,)), ((), ())), preferred_element_type=jnp.float32
    )


def after(value, *earlier):
    return lax.optimization_barrier((value, *earlier))[0]


def grad_kernel(place, outs, cuts, rows_hbm, cols_hbm, slots_hbm, act_ref, up_ref, *refs):
    refs = list(refs)
    w_ref = refs.pop(0) if cuts else None
    out_refs, refs = refs[:outs], refs[outs:]
    cut_refs, refs = refs[: len(cuts)], refs[len(cuts) :]
    rows_ref, cols_ref, slots_ref, act_buf, up_buf, act_sem, up_sem, i_sem, c_sem = refs
    nb = rows_ref.shape[0]
    index_copies = [
        pltpu.make_async_copy(src, dst, i_sem.at[n])
        for n, (src, dst) in enumerate(
            [(rows_hbm, rows_ref), (cols_hbm, cols_ref), (slots_hbm, slots_ref)]
        )
    ]
    for copy in index_copies:
        copy.start()
    up_copy = pltpu.make_async_copy(up_ref, up_buf, up_sem)
    up_copy.start()

    def act_copy(b):
        column = pl.multiple_of(rows_ref[b] * BLOCK, BLOCK)
        return pltpu.make_async_copy(
            act_ref.at[:, pl.ds(column, BLOCK)], act_buf.at[b], act_sem.at[b]
        )

    for copy in index_copies:
        copy.wait()
    for b in range(nb):
        act_copy(b).start()
    cut_copies = [
        pltpu.make_async_copy(
            w_ref.at[pl.ds(pl.multiple_of(first(), BLOCK), ref.shape[0])], ref, c_sem.at[n]
        )
        for n, ((first, _), ref) in enumerate(zip(cuts, cut_refs))
    ]
    for copy in cut_copies:
        copy.start()
    for ref in out_refs:
        ref[...] = jnp.zeros_like(ref)
    up_copy.wait()
    for b in range(nb):
        act_copy(b).wait()
        column = pl.multiple_of(cols_ref[b] * BLOCK, BLOCK)
        term = dot_tn(act_buf[b], up_buf[:, pl.ds(column, BLOCK)])
        which, index = place(slots_ref[b])
        for n, ref in enumerate(out_refs):

            @pl.when(which == n)
            def _():
                ref[index] = term

    for copy in cut_copies:
        copy.wait()


def block_grads(place, shapes, rows, cols, slots, act, up, weight=None, cuts=()):
    nb = rows.shape[0]
    return pl.pallas_call(
        functools.partial(grad_kernel, place, len(shapes), cuts),
        out_shape=[jax.ShapeDtypeStruct((n, BLOCK, BLOCK), jnp.float32) for n in shapes]
        + [jax.ShapeDtypeStruct((n, weight.shape[1]), weight.dtype) for _, n in cuts],
        in_specs=[HBM_SPEC] * (6 if cuts else 5),
        out_specs=[VMEM_SPEC] * (len(shapes) + len(cuts)),
        scratch_shapes=[
            pltpu.SMEM((nb,), jnp.int32),
            pltpu.SMEM((nb,), jnp.int32),
            pltpu.SMEM((nb,), jnp.int32),
            pltpu.VMEM((nb, act.shape[0], BLOCK), act.dtype),
            pltpu.VMEM(up.shape, up.dtype),
            pltpu.SemaphoreType.DMA((nb,)),
            pltpu.SemaphoreType.DMA,
            pltpu.SemaphoreType.DMA((3,)),
            pltpu.SemaphoreType.DMA((max(1, len(cuts)),)),
        ],
        compiler_params=pltpu.CompilerParams(vmem_limit_bytes=VMEM_BYTES),
        cost_estimate=COST,
        name="block_grads",
    )(rows, cols, slots, act, up, *([weight] if cuts else []))


def rows_kernel(
    units, moves, tile, row_blocks, delta_at, n_up, n_w, n_d, n_m, n_alias, other_first, *refs
):
    refs = list(refs)

    def take(n):
        taken = refs[:n]
        del refs[:n]
        return taken

    rows_hbm, cols_hbm, slots_hbm = take(3)
    up_refs, w_refs, d_refs, m_refs = take(n_up), take(n_w), take(n_d), take(n_m)
    take(n_alias)
    (out_ref,) = take(1)
    other_ref = take(1)[0] if n_up > 1 else None
    rows_ref, cols_ref, slots_ref, up_buf, w_buf, d_buf, acc, o_buf, m_buf = take(9)
    table, head, after_it, i_sem, up_sem, w_sem, d_sem, o_sem, m_sem = take(9)
    nb = rows_ref.shape[0]
    n_units = len(units)
    per = d_buf.shape[0] // n_d
    tokens = up_buf.shape[0] // n_up

    index_copies = [
        pltpu.make_async_copy(src, dst, i_sem.at[n])
        for n, (src, dst) in enumerate(
            [(rows_hbm, rows_ref), (cols_hbm, cols_ref), (slots_hbm, slots_ref)]
        )
    ]
    for copy in index_copies:
        copy.start()
    up_copies = [
        pltpu.make_async_copy(ref, up_buf.at[pl.ds(n * tokens, tokens)], up_sem.at[n])
        for n, ref in enumerate(up_refs)
    ]
    for copy in up_copies:
        copy.start()
    for u, (w, first, _) in enumerate(units):
        pltpu.make_async_copy(
            w_refs[w].at[pl.ds(first, BLOCK)], w_buf.at[pl.ds(u * BLOCK, BLOCK)], w_sem.at[u]
        ).start()
    d_copies = [
        pltpu.make_async_copy(ref, d_buf.at[pl.ds(n * per, per)], d_sem.at[n])
        for n, ref in enumerate(d_refs)
    ]
    for copy in d_copies:
        copy.start()
    m_in = [
        pltpu.make_async_copy(
            m_refs[m].at[:, pl.ds(first, BLOCK)], m_buf.at[n], m_sem.at[0, n]
        )
        for n, (m, first, _) in enumerate(moves)
    ]
    m_out = [
        pltpu.make_async_copy(
            m_buf.at[n],
            out_ref.at[:, pl.ds(pl.multiple_of(column() * BLOCK, BLOCK), BLOCK)],
            m_sem.at[1, n],
        )
        for n, (_, _, column) in enumerate(moves)
    ]
    for copy in m_in:
        copy.start()
    for u, (_, _, column) in enumerate(units):
        table[u] = column()
    for r in range(row_blocks):
        head[r] = -1
    for copy in index_copies:
        copy.wait()
    for b in range(nb):
        r = rows_ref[b]
        after_it[b] = head[r]
        head[r] = b
    for copy in up_copies:
        copy.wait()
    for copy in d_copies:
        copy.wait()

    def out_copies(u):
        column = pl.multiple_of(table[u] * BLOCK, BLOCK)
        copies = [
            pltpu.make_async_copy(
                o_buf.at[u, pl.ds(0, tokens)], out_ref.at[:, pl.ds(column, BLOCK)], o_sem.at[0, u]
            )
        ]
        if other_ref is not None:
            at = other_first + u * BLOCK
            at = at if isinstance(u, int) else pl.multiple_of(at, BLOCK)
            copies.append(
                pltpu.make_async_copy(
                    o_buf.at[u, pl.ds(tokens, tokens)],
                    other_ref.at[:, pl.ds(at, BLOCK)],
                    o_sem.at[1, u],
                )
            )
        return copies

    def step(t, width):
        for h in range(width):
            pltpu.make_async_copy(
                w_refs[0].at[pl.ds(0, BLOCK)],
                w_buf.at[pl.ds((t + h) * BLOCK, BLOCK)],
                w_sem.at[t + h],
            ).wait()
        size = width * BLOCK
        start = t * BLOCK if isinstance(t, int) else pl.multiple_of(t * BLOCK, BLOCK)
        acc[:, :size] = dot_nt(up_buf[...], w_buf[pl.ds(start, size)])
        for h in range(width):

            def add(b):
                column = pl.multiple_of(cols_ref[b] * BLOCK, BLOCK)
                delta = d_buf[delta_at(slots_ref[b])]
                acc[:, h * BLOCK : (h + 1) * BLOCK] += dot_nt(
                    up_buf[:, pl.ds(column, BLOCK)], delta
                )
                return after_it[b]

            lax.while_loop(lambda b: b >= 0, add, head[table[t + h]])
            o_buf[t + h] = acc[:, h * BLOCK : (h + 1) * BLOCK].astype(o_buf.dtype)
            for copy in out_copies(t + h):
                copy.start()

    whole = n_units // tile
    if whole > 1:

        def body(k, carry):
            step(k * tile, tile)
            return carry

        lax.fori_loop(0, whole, body, 0)
    elif whole == 1:
        step(0, tile)
    if n_units % tile:
        step(whole * tile, n_units % tile)

    for copy in m_in:
        copy.wait()
    for copy in m_out:
        copy.start()
    for copy in m_out:
        copy.wait()
    for u in range(n_units):
        for copy in out_copies(u):
            copy.wait()


def rows_grad(
    units, weights, rows, cols, slots, ups, deltas, delta_at, width, out=None, moves=(), moved=(), tile=4,
    other=None, other_units=None, other_first=0,
):
    n_units = len(units)
    tile = min(tile, n_units)
    tokens, depth = ups[0].shape
    dtype = ups[0].dtype
    stored = sum(d.shape[0] for d in deltas)
    nb = rows.shape[0]
    operands = [rows, cols, slots, *ups, *weights, *deltas, *moved]
    specs = [HBM_SPEC] * 3 + [ANY_SPEC] * (len(operands) - 3)
    alias = {}
    for n, held in enumerate([out, other]):
        if held is not None:
            alias[len(operands)] = n
            operands.append(held)
            specs.append(HBM_SPEC)
    shapes = [jax.ShapeDtypeStruct((tokens, width), dtype)]
    if len(ups) > 1:
        shapes.append(
            jax.ShapeDtypeStruct((tokens, (other_units or n_units) * BLOCK), dtype)
        )
    return pl.pallas_call(
        functools.partial(
            rows_kernel, units, moves, tile, width // BLOCK, delta_at, len(ups), len(weights),
            len(deltas), len(moved), len(alias), other_first,
        ),
        out_shape=shapes,
        in_specs=specs,
        out_specs=[HBM_SPEC] * len(shapes),
        input_output_aliases=alias,
        scratch_shapes=[
            pltpu.SMEM((nb,), jnp.int32),
            pltpu.SMEM((nb,), jnp.int32),
            pltpu.SMEM((nb,), jnp.int32),
            pltpu.VMEM((len(ups) * tokens, depth), dtype),
            pltpu.VMEM((n_units * BLOCK, depth), dtype),
            pltpu.VMEM((stored, BLOCK, BLOCK), dtype),
            pltpu.VMEM((len(ups) * tokens, tile * BLOCK), jnp.float32),
            pltpu.VMEM((n_units, len(ups) * tokens, BLOCK), dtype),
            pltpu.VMEM((max(1, len(moves)), tokens, BLOCK), dtype),
            pltpu.SMEM((n_units,), jnp.int32),
            pltpu.SMEM((width // BLOCK,), jnp.int32),
            pltpu.SMEM((nb,), jnp.int32),
            pltpu.SemaphoreType.DMA((3,)),
            pltpu.SemaphoreType.DMA((len(ups),)),
            pltpu.SemaphoreType.DMA((n_units,)),
            pltpu.SemaphoreType.DMA((len(deltas),)),
            pltpu.SemaphoreType.DMA((len(ups), n_units)),
            pltpu.SemaphoreType.DMA((2, max(1, len(moves)))),
        ],
        compiler_params=pltpu.CompilerParams(vmem_limit_bytes=VMEM_BYTES),
        cost_estimate=COST,
        name="rows_grad",
    )(*operands)


def gathered(activations, upstream, frozen, deltas, block_rows, block_cols, block_slot):
    local_slots = deltas.shape[0]
    n = lax.axis_size("fsdp")
    width = activations.shape[1]
    pattern = (block_rows, block_cols, block_slot)

    (partial,) = block_grads(
        lambda slot: (0, slot), [n * local_slots], *pattern, activations, upstream
    )
    mine = lax.psum_scatter(partial, "fsdp", scatter_dimension=0, tiled=True)
    totals = lax.psum(mine, "dp")

    all_deltas = lax.all_gather(deltas, "fsdp", axis=0, tiled=True)
    weight = lax.all_gather(frozen, "fsdp", axis=0, tiled=True)
    out = None
    for first in range(0, width, 2048):
        units = [
            (0, first + k * BLOCK, lambda c=first // BLOCK + k: c)
            for k in range(min(2048, width - first) // BLOCK)
        ]
        (out,) = rows_grad(
            units, [weight], *pattern, [upstream], [all_deltas], lambda slot: slot, width, out
        )
    tokens = upstream.shape[0] * n * lax.axis_size("dp")
    return out, totals * (1.0 / math.sqrt(tokens))


def relayed(activations, upstream, frozen, deltas, block_rows, block_cols, block_slot):
    local_slots = deltas.shape[0]
    quarter = frozen.shape[0]
    width = activations.shape[1]
    n_dp = lax.axis_size("dp")
    pattern = (block_rows, block_cols, block_slot)

    def my_f():
        return lax.axis_index("fsdp")

    def my_cell():
        return 2 * lax.axis_index("group") + lax.axis_index("dp") % 2

    def over_core(a):
        return lax.ppermute(a, "fsdp", [(k, k ^ 1) for k in range(4)])

    def over_x(a):
        return lax.ppermute(a, "fsdp", [(k, k ^ 2) for k in range(4)])

    def over_y(a):
        return lax.ppermute(a, "group", [(k, k ^ 1) for k in range(2)])

    def over_z(a, step=1):
        return lax.ppermute(a, "dp", [(k, k ^ step) for k in range(n_dp)])

    part = quarter // 4
    sizes = (part // 4, part // 4, part // 2)
    offs = (0, sizes[0], sizes[0] + sizes[1])

    def own_rows(flip, k):
        first = (my_cell() ^ flip) * part + offs[k]
        return lax.dynamic_slice_in_dim(frozen, first, sizes[k], 0)

    def delta_at(slot):
        return ((slot // local_slots) ^ my_f()) * local_slots + slot % local_slots

    def column_of(flip_f, flip_cell, at):
        def column():
            base = (my_f() ^ flip_f) * (quarter // BLOCK) + at // BLOCK
            if flip_cell is not None:
                base = base + (my_cell() ^ flip_cell) * (part // BLOCK)
            return base

        return column

    def units_of(pieces):
        return [
            (w, k * BLOCK, column_of(flip_f, flip_cell, first + k * BLOCK))
            for w, (a, flip_f, flip_cell, first) in enumerate(pieces)
            for k in range(a.shape[0] // BLOCK)
        ]

    def moves_of(pieces):
        units = [
            (flip_f ^ 1, flip_cell, first + k * BLOCK)
            for a, flip_f, flip_cell, first in pieces
            for k in range(a.shape[0] // BLOCK)
        ]
        return [(0, u * BLOCK, column_of(*unit)) for u, unit in enumerate(units)]

    half = local_slots // 2

    def place(slot):
        rel = (slot // local_slots) ^ my_f()
        at = slot % local_slots
        index = (rel // 2) * local_slots + ((at // half) ^ (my_cell() % 2)) * half + at % half
        return rel % 2, index

    def multiply(units, pieces, ups, out, received=None, at=(), **other):
        return rows_grad(
            units, [p[0] for p in pieces], *pattern, ups, all_deltas, delta_at, width, out,
            moves_of(at), [] if received is None else [received], **other,
        )

    def row_of(flip, k):
        return lambda: (my_cell() ^ flip) * part + offs[k]

    x0 = over_x(own_rows(0, 0))
    up_sib = over_core(upstream)
    dx = over_x(deltas)
    keep, send, s1, s2, s3 = block_grads(
        place, [2 * local_slots, 2 * local_slots], *pattern, activations, upstream, frozen,
        [(row_of(0, 1), sizes[1]), (row_of(0, 2), sizes[2]), (row_of(3, 2), sizes[2])],
    )

    x0, send, up_sib, s1 = lax.optimization_barrier((x0, send, up_sib, s1))
    y0, z0, x1 = over_y(x0), over_z(x0), over_x(s1)
    gc = over_core(send)

    x1, y0, z0, gc, dx = lax.optimization_barrier((x1, y0, z0, gc, dx))
    dc, dxc = over_core(after(deltas, dx)), over_core(dx)
    gx = over_x(keep[local_slots:] + gc[local_slots:])
    x2 = over_x(after(s2, x1))
    y1, z1 = over_y(x1), over_z(x1)
    yd0 = over_y(z0)
    all_deltas = [deltas, dc, dx, dxc]

    def multiply(units, pieces, ups, out, received=None, at=(), **other):
        return rows_grad(
            units, [p[0] for p in pieces], *pattern, ups, all_deltas, delta_at, width, out,
            moves_of(at), [] if received is None else [received], **other,
        )

    own = [(frozen, 0, None, 0)]
    own_units = units_of(own)
    first_half = len(own_units) // 2
    pieces2 = [(x0, 2, 0, offs[0]), (y0, 2, 2, offs[0]), (z0, 2, 1, offs[0]), (x1, 2, 0, offs[1])]
    n_a = first_half + len(units_of(pieces2))
    out, other_a = multiply(
        own_units[:first_half], own, [upstream, after(up_sib, x1)], None, other_units=n_a
    )

    out, y1, z1, yd0, gx = lax.optimization_barrier((out, y1, z1, yd0, gx))
    owned = keep[:local_slots] + gc[:local_slots] + gx
    gz = over_z(owned[half:])
    yd1 = over_y(z1)
    x3 = over_x(after(s3, z1))
    out, other_a = multiply(
        units_of(pieces2), pieces2, [upstream, after(up_sib, z1)], out,
        other=other_a, other_units=n_a, other_first=first_half * BLOCK,
    )

    out, other_a, x2, yd1, gz = lax.optimization_barrier((out, other_a, x2, yd1, gz))
    y2, z2 = over_y(x2), over_z(x2)
    mine = owned[:half] + gz
    gz2 = over_z(mine, 2)
    oa = over_core(other_a)
    pieces3 = [
        (y1, 2, 2, offs[1]), (z1, 2, 1, offs[1]), (yd0, 2, 3, offs[0]), (yd1, 2, 3, offs[1]),
        (x2, 2, 0, offs[2]),
    ]
    n_3 = len(units_of(pieces3))
    n_b = n_3 + len(own_units) - first_half
    out, other_b = multiply(
        units_of(pieces3), pieces3, [upstream, after(up_sib, x2)], out, other_units=n_b
    )
    out, other_b = multiply(
        own_units[first_half:], own, [upstream, after(up_sib, x2)], out,
        other=other_b, other_units=n_b, other_first=n_3 * BLOCK,
    )

    out, other_b, x3, y2, z2, gz2, oa = lax.optimization_barrier(
        (out, other_b, x3, y2, z2, gz2, oa)
    )
    mine = mine + gz2
    ob = over_core(other_b)
    last = [(x3, 2, 3, offs[2]), (y2, 2, 2, offs[2]), (z2, 2, 1, offs[2])]
    last = last + [(over_core(a), 3, cell, at) for a, _, cell, at in last]
    other_half = over_z(mine)
    own_moves = moves_of(own)

    def moved(m, moves):
        return [(m, u * BLOCK, column) for u, (_, _, column) in enumerate(moves)]

    (out,) = rows_grad(
        units_of(last), [p[0] for p in last], *pattern, [upstream], all_deltas, delta_at, width,
        out,
        moved(0, own_moves[:first_half] + moves_of(pieces2))
        + moved(1, moves_of(pieces3) + own_moves[first_half:]),
        [oa, ob],
    )
    other_half = after(other_half, out)

    normalizer = 1.0 / math.sqrt(upstream.shape[0] * lax.axis_size("fsdp") * n_dp)
    totals = jnp.where(
        lax.axis_index("dp") % 2 == 0,
        jnp.concatenate([mine, other_half], axis=0),
        jnp.concatenate([other_half, mine], axis=0),
    ) * normalizer
    return out, totals


def solution(mesh):
    sizes = dict(mesh.shape)
    cells = sizes["fsdp"] == 4 and sizes["group"] == 2 and sizes["dp"] == 4
    return jax.shard_map(
        relayed if cells else gathered,
        mesh=mesh,
        in_specs=(
            P(("group", "fsdp", "dp"), None),
            P(("group", "fsdp", "dp"), None),
            P("fsdp", None),
            P(("group", "fsdp"), None, None),
            P(),
            P(),
            P(),
        ),
        out_specs=(P(("group", "fsdp", "dp"), None), P(("group", "fsdp"), None, None)),
        check_vma=False,
    )
```

time: 121 us -> 84.5 us (0.70); the launches traced: 119 us -> 84.1 us
  waiting for transfers between devices: 34.4 us -> 12 us
  local copies, waits for them, and re-layouts: 12.9 us -> 3.21 us
  starting transfers between devices: 31.3 us -> 27.3 us
  other arithmetic: 2.91 us -> 4.33 us
    ppermute x7 -> x6, waiting for transfers between devices: 14.6 us -> 0.47 us  [over_z(): return lax.ppermute(a, 'dp', [(k, k ^ step) for k in range(n_dp)])]
    ppermute x6, waiting for transfers between devices: 18.4 us -> 6.62 us  [over_x(): return lax.ppermute(a, 'fsdp', [(k, k ^ 2) for k in range(4)])]
    unnamed x70 -> x34, local copies, waits for them, and re-layouts: 10.5 us -> 2.23 us
    ppermute x4 -> x5, waiting for transfers between devices: 0.45 us -> 2.88 us  [over_y(): return lax.ppermute(a, 'group', [(k, k ^ 1) for k in range(2)])]
    ppermute x7 -> x6, starting transfers between devices: 13 us -> 11.1 us  [over_z(): return lax.ppermute(a, 'dp', [(k, k ^ step) for k in range(n_dp)])]
    ppermute x6, starting transfers between devices: 9.63 us -> 8.01 us  [over_x(): return lax.ppermute(a, 'fsdp', [(k, k ^ 2) for k in range(4)])]
    add x4, other arithmetic: 2.1 us -> 3.6 us  [the longest x1 1.67 us: relayed(): gx = over_x(keep[local_slots:] + gc[local_slots:])]
    dynamic_slice x2 -> x1, local copies, waits for them, and re-layouts: 2.33 us -> 0.97 us  [own_rows(): return lax.dynamic_slice_in_dim(frozen, first, sizes[k], 0)]
  transfers between devices with their start and end apart: 33 -> 26, of which waited for: 10 -> 7; matrix products, arithmetic and copies ran while one was open for 4% -> 5% of each run, Pallas kernels for 26% -> 43%
where the time goes in v2:
time: 84.5 us; the launch traced here: 84.1 us
  Pallas kernels  36.4 us (43%)
  starting transfers between devices  27.3 us (32%)
  waiting for transfers between devices  12 us (14%)
  other arithmetic  4.33 us (5%)
  local copies, waits for them, and re-layouts  3.21 us (4%)
  between operations  0.92 us (1%)
    pallas_call x5, Pallas kernels, rows_grad(): pl.pallas_call(functools.partial(rows_kernel, units, moves, tile, width /...  29.8 us
    ppermute x6, starting transfers between devices, over_z(): return lax.ppermute(a, 'dp', [(k, k ^ step) for k in range(n_dp)])  11.1 us
    ppermute x6, starting transfers between devices, over_x(): return lax.ppermute(a, 'fsdp', [(k, k ^ 2) for k in range(4)])  8.01 us
    ppermute x6, waiting for transfers between devices, over_x(): return lax.ppermute(a, 'fsdp', [(k, k ^ 2) for k in range(4)])  6.62 us
    pallas_call x1, Pallas kernels, block_grads(): pl.pallas_call(functools.partial(grad_kernel, place, len(shapes), cuts),...  6.61 us
    ppermute x5, starting transfers between devices, over_y(): return lax.ppermute(a, 'group', [(k, k ^ 1) for k in range(2)])  5.96 us
    ppermute x5, waiting for transfers between devices, over_y(): return lax.ppermute(a, 'group', [(k, k ^ 1) for k in range(2)])  2.88 us
    ppermute x9, starting transfers between devices, over_core(): return lax.ppermute(a, 'fsdp', [(k, k ^ 1) for k in range(4)])  2.24 us
  transfers between devices with their start and end apart: 26, of which 7 were waited for; matrix products, arithmetic and copies ran while one was open for 5% of the time, Pallas kernels for 43%

profile of v2, /device:TPU:0, one launch (start us, length us, event | category | flops | bytes accessed | tf_op | source)
XLA Modules:
  0.0 84.1 jit_solution(7230755887540125102)
XLA Ops:
  1.1 1.0 %constant_dynamic-slice_fusion = bf16[128,1024]{1,0:T(8,128)(2,1)S(1)} fusion(bf16[2048,1024]{1,0:T(8,128)(2,1)} %refs_5_.3, s32[]{:T(128)S(6)} %select_n.21), kind=kLoop, calls=%fused_computation.5 | loop fusion | bytes 524292 | tf_op jit(solution)/shard_map/dynamic_slice | solution.py:375
  2.1 2.6 %collective-permute-start = (bf16[128,1024]{1,0:T(8,128)(2,1)S(1)}, bf16[128,1024]{1,0:T(8,128)(2,1)S(1)}, u32[]{:S(2)}, u32[]{:S(2)}) collective-permute-start(bf16[128,1024]{1,0:T(8,128)(2,1)S(1)} %constant_dynamic-slice_fusion), channel_id=1, source_target_pairs={{0,8},{4,12},{8,0},{12,4},{1,9},{5,13},{9,1},{13,5},{2,10},{6,14},... | collective-permute-start | bytes 786440 | tf_op jit(solution)/shard_map/ppermute | solution.py:361
  4.7 6.6 %block_grads.1 = (f32[8,128,128]{2,1,0:T(8,128)}, f32[8,128,128]{2,1,0:T(8,128)}, bf16[128,1024]{1,0:T(8,128)(2,1)}, bf16[256,1024]{1,0:T(8,128)(2,1)}, bf16[256,1024]{1,0:T(8,128)(2,1)}) custom-call(s32[16]{0:T(128)} %refs_0_.11, s32[16]{0:T(128)} %refs_1_.9, s32[16]{0:T(128)} %refs_2_.9, bf16[384,8192]{1,0:T(8,128)(2,1)} %act_ref.1, ...), custom_call_target="tpu_custom_call" | custom-call | flops 1024 | bytes 1024 | tf_op jit(solution)/shard_map/block_grads/pallas_call | solution.py:91
  11.7 1.8 %collective-permute-start.2 = (bf16[128,1024]{1,0:T(8,128)(2,1)}, bf16[128,1024]{1,0:T(8,128)(2,1)S(1)}, u32[]{:S(2)}, u32[]{:S(2)}) collective-permute-start(bf16[128,1024]{1,0:T(8,128)(2,1)} %get-tuple-element.51), channel_id=1, source_target_pairs={{0,8},{4,12},{8,0},{12,4},{1,9},{5,13},{9,1},{13,5},{2,10},{6,14},... | collective-permute-start | bytes 786440 | tf_op jit(solution)/shard_map/ppermute | solution.py:361
  13.5 1.6 %collective-permute-start.4 = (bf16[128,1024]{1,0:T(8,128)(2,1)S(1)}, bf16[128,1024]{1,0:T(8,128)(2,1)S(1)}, u32[]{:S(2)}, u32[]{:S(2)}) collective-permute-start(bf16[128,1024]{1,0:T(8,128)(2,1)S(1)} %collective-permute-done.refs_5_), channel_id=1, source_target_pairs={{0,1},{1,0},{2,3},{3,2},{4,5},{5,4},{6,7},{7,6},{8,9},{9,8},{10,11... | collective-permute-start | bytes 786440 | tf_op jit(solution)/shard_map/ppermute | solution.py:367
  15.1 1.5 %collective-permute-start.3 = (bf16[128,1024]{1,0:T(8,128)(2,1)S(1)}, bf16[128,1024]{1,0:T(8,128)(2,1)S(1)}, u32[]{:S(2)}, u32[]{:S(2)}) collective-permute-start(bf16[128,1024]{1,0:T(8,128)(2,1)S(1)} %collective-permute-done.refs_5_), channel_id=1, source_target_pairs={{0,16},{16,0},{1,17},{17,1},{2,18},{18,2},{3,19},{19,3},{4,20},{20... | collective-permute-start | bytes 786440 | tf_op jit(solution)/shard_map/ppermute | solution.py:364
  17.2 6.3 %collective-permute-done.6.refs_8_.refs_11_.refs_12_ = bf16[4,128,128]{2,1,0:T(8,128)(2,1)S(1)} collective-permute-done((bf16[4,128,128]{2,1,0:T(8,128)(2,1)S(1)}, bf16[4,128,128]{2,1,0:T(8,128)(2,1)S(1)}, u32[]{:S(2)}, u32[]{:S(2)}) %collective-permute-start.6) | collective-permute-done | bytes 131104 | tf_op jit(solution)/shard_map/ppermute | solution.py:361
  24.1 1.7 %slice_add_fusion = f32[4,128,128]{2,1,0:T(8,128)} fusion(f32[8,128,128]{2,1,0:T(8,128)S(1)} %collective-permute-done.5, f32[8,128,128]{2,1,0:T(8,128)} %get-tuple-element.60), kind=kLoop, calls=%fused_computation.3 | loop fusion | flops 65536 | bytes 786432 | tf_op jit(solution)/shard_map/add | solution.py:435
  25.8 1.7 %collective-permute-start.12 = (f32[4,128,128]{2,1,0:T(8,128)}, f32[4,128,128]{2,1,0:T(8,128)}, u32[]{:S(2)}, u32[]{:S(2)}) collective-permute-start(f32[4,128,128]{2,1,0:T(8,128)} %slice_add_fusion), channel_id=1, source_target_pairs={{0,8},{4,12},{8,0},{12,4},{1,9},{5,13},{9,1},{13,5},{2,10},{6,14},... | collective-permute-start | bytes 786440 | tf_op jit(solution)/shard_map/ppermute | solution.py:361
  27.5 1.5 %collective-permute-start.11 = (bf16[128,1024]{1,0:T(8,128)(2,1)S(1)}, bf16[128,1024]{1,0:T(8,128)(2,1)}, u32[]{:S(2)}, u32[]{:S(2)}) collective-permute-start(bf16[128,1024]{1,0:T(8,128)(2,1)S(1)} %collective-permute-done.4.refs_7_), channel_id=1, source_target_pairs={{0,16},{16,0},{1,17},{17,1},{2,18},{18,2},{3,19},{19,3},{4,20},{20... | collective-permute-start | bytes 786440 | tf_op jit(solution)/shard_map/ppermute | solution.py:364
  29.1 1.6 %collective-permute-start.10 = (bf16[128,1024]{1,0:T(8,128)(2,1)S(1)}, bf16[128,1024]{1,0:T(8,128)(2,1)}, u32[]{:S(2)}, u32[]{:S(2)}) collective-permute-start(bf16[128,1024]{1,0:T(8,128)(2,1)S(1)} %collective-permute-done.2.refs_8_), channel_id=1, source_target_pairs={{0,1},{1,0},{2,3},{3,2},{4,5},{5,4},{6,7},{7,6},{8,9},{9,8},{10,11... | collective-permute-start | bytes 786440 | tf_op jit(solution)/shard_map/ppermute | solution.py:367
  31.1 0.5 collective-permute-start.13
  31.8 6.6 %rows_grad.5 = (bf16[384,8192]{1,0:T(8,128)(2,1)}, bf16[384,1536]{1,0:T(8,128)(2,1)}) custom-call(s32[16]{0:T(128)} %refs_0_.11, s32[16]{0:T(128)} %refs_1_.9, s32[16]{0:T(128)} %refs_2_.9, bf16[384,1024]{1,0:T(8,128)(2,1)} %refs_3_.9, bf16[384,1024]{1,0:T(8,128)(2,1)} %copy-done, bf16[2048,1024]{1,0:T(8,128)(2,1)} %refs_5_.3, ...), custom_call_target="tpu_custom_call" | custom-call | flops 1024 | bytes 1024 | tf_op jit(solution)/shard_map/rows_grad/pallas_call | solution.py:282
  38.4 2.9 %collective-permute-done.9.refs_5_ = bf16[128,1024]{1,0:T(8,128)(2,1)} collective-permute-done((bf16[128,1024]{1,0:T(8,128)(2,1)S(1)}, bf16[128,1024]{1,0:T(8,128)(2,1)}, u32[]{:S(2)}, u32[]{:S(2)}) %collective-permute-start.9) | collective-permute-done | bytes 262176 | tf_op jit(solution)/shard_map/ppermute | solution.py:364
  41.3 1.5 %collective-permute-start.14 = (bf16[128,1024]{1,0:T(8,128)(2,1)}, bf16[128,1024]{1,0:T(8,128)(2,1)S(1)}, u32[]{:S(2)}, u32[]{:S(2)}) collective-permute-start(bf16[128,1024]{1,0:T(8,128)(2,1)} %collective-permute-done.10.refs_6_), channel_id=1, source_target_pairs={{0,16},{16,0},{1,17},{17,1},{2,18},{18,2},{3,19},{19,3},{4,20},{20... | collective-permute-start | bytes 786440 | tf_op jit(solution)/shard_map/ppermute | solution.py:364
  42.8 1.0 %add_add_fusion = f32[4,128,128]{2,1,0:T(8,128)S(1)} fusion(f32[4,128,128]{2,1,0:T(8,128)} %collective-permute-done.12, f32[8,128,128]{2,1,0:T(8,128)S(1)} %collective-permute-done.5, f32[8,128,128]{2,1,0:T(8,128)S(1)} %copy-done.10), kind=kLoop, calls=%fused_computation.2 | loop fusion | flops 131072 | bytes 1048576 | tf_op jit(solution)/shard_map/add | solution.py:457
  43.8 1.6 %collective-permute-start.15 = (f32[2,128,128]{2,1,0:T(8,128)S(1)}, f32[2,128,128]{2,1,0:T(8,128)}, u32[]{:S(2)}, u32[]{:S(2)}) collective-permute-start(f32[2,128,128]{2,1,0:T(8,128)S(1)} %slice.24), channel_id=1, source_target_pairs={{0,1},{1,0},{2,3},{3,2},{4,5},{5,4},{6,7},{7,6},{8,9},{9,8},{10,11... | collective-permute-start | bytes 393224 | tf_op jit(solution)/shard_map/ppermute | solution.py:367
  45.5 4.0 %rows_grad.6 = (bf16[384,8192]{1,0:T(8,128)(2,1)}, bf16[384,1536]{1,0:T(8,128)(2,1)}) custom-call(s32[16]{0:T(128)} %refs_0_.11, s32[16]{0:T(128)} %refs_1_.9, s32[16]{0:T(128)} %refs_2_.9, bf16[384,1024]{1,0:T(8,128)(2,1)} %refs_3_.9, bf16[384,1024]{1,0:T(8,128)(2,1)} %copy-done, ...), custom_call_target="tpu_custom_call", output_to_operand_aliasing={{0}: (13, {}), {1}: (14, {})} | custom-call | flops 1024 | bytes 1024 | tf_op jit(solution)/shard_map/rows_grad/pallas_call | solution.py:282
  49.6 0.8 collective-permute-start.16
  50.4 0.9 %collective-permute-start.18 = (bf16[256,1024]{1,0:T(8,128)(2,1)S(1)}, bf16[256,1024]{1,0:T(8,128)(2,1)S(1)}, u32[]{:S(2)}, u32[]{:S(2)}) collective-permute-start(bf16[256,1024]{1,0:T(8,128)(2,1)S(1)} %collective-permute-done.13.refs_9_), channel_id=1, source_target_pairs={{0,1},{1,0},{2,3},{3,2},{4,5},{5,4},{6,7},{7,6},{8,9},{9,8},{10,11... | collective-permute-start | bytes 1572872 | tf_op jit(solution)/shard_map/ppermute | solution.py:367
  51.3 0.9 %collective-permute-start.17 = (bf16[256,1024]{1,0:T(8,128)(2,1)S(1)}, bf16[256,1024]{1,0:T(8,128)(2,1)S(1)}, u32[]{:S(2)}, u32[]{:S(2)}) collective-permute-start(bf16[256,1024]{1,0:T(8,128)(2,1)S(1)} %collective-permute-done.13.refs_9_), channel_id=1, source_target_pairs={{0,16},{16,0},{1,17},{17,1},{2,18},{18,2},{3,19},{19,3},{4,20},{20... | collective-permute-start | bytes 1572872 | tf_op jit(solution)/shard_map/ppermute | solution.py:364
  52.2 0.9 %slice_add_fusion.1 = f32[2,128,128]{2,1,0:T(8,128)S(1)} fusion(f32[2,128,128]{2,1,0:T(8,128)} %collective-permute-done.15, f32[4,128,128]{2,1,0:T(8,128)S(1)} %add_add_fusion), kind=kLoop, calls=%fused_computation.4 | loop fusion | flops 32768 | bytes 393216 | tf_op jit(solution)/shard_map/add | solution.py:468
  53.2 2.7 %collective-permute-start.19 = (f32[2,128,128]{2,1,0:T(8,128)S(1)}, f32[2,128,128]{2,1,0:T(8,128)S(1)}, u32[]{:S(2)}, u32[]{:S(2)}) collective-permute-start(f32[2,128,128]{2,1,0:T(8,128)S(1)} %slice_add_fusion.1), channel_id=1, source_target_pairs={{0,2},{1,3},{2,0},{3,1},{4,6},{5,7},{6,4},{7,5},{8,10},{9,11},{10,... | collective-permute-start | bytes 393224 | tf_op jit(solution)/shard_map/ppermute | solution.py:367
  55.8 5.1 %rows_grad.7 = (bf16[384,8192]{1,0:T(8,128)(2,1)}, bf16[384,1792]{1,0:T(8,128)(2,1)}) custom-call(s32[16]{0:T(128)} %refs_0_.11, s32[16]{0:T(128)} %refs_1_.9, s32[16]{0:T(128)} %refs_2_.9, bf16[384,1024]{1,0:T(8,128)(2,1)} %refs_3_.9, bf16[384,1024]{1,0:T(8,128)(2,1)} %copy-done, ...), custom_call_target="tpu_custom_call", output_to_operand_aliasing={{0}: (14, {})} | custom-call | flops 1024 | bytes 1024 | tf_op jit(solution)/shard_map/rows_grad/pallas_call | solution.py:282
  60.9 5.9 %rows_grad.8 = (bf16[384,8192]{1,0:T(8,128)(2,1)}, bf16[384,1792]{1,0:T(8,128)(2,1)}) custom-call(s32[16]{0:T(128)} %refs_0_.11, s32[16]{0:T(128)} %refs_1_.9, s32[16]{0:T(128)} %refs_2_.9, bf16[384,1024]{1,0:T(8,128)(2,1)} %refs_3_.9, bf16[384,1024]{1,0:T(8,128)(2,1)} %copy-done, ...), custom_call_target="tpu_custom_call", output_to_operand_aliasing={{0}: (10, {}), {1}: (11, {})} | custom-call | flops 1024 | bytes 1024 | tf_op jit(solution)/shard_map/rows_grad/pallas_call | solution.py:282
  67.3 0.8 copy-done.8
  69.3 2.7 %collective-permute-start.25 = (f32[2,128,128]{2,1,0:T(8,128)S(1)}, f32[2,128,128]{2,1,0:T(8,128)S(1)}, u32[]{:S(2)}, u32[]{:S(2)}) collective-permute-start(f32[2,128,128]{2,1,0:T(8,128)S(1)} %add.33), channel_id=1, source_target_pairs={{0,1},{1,0},{2,3},{3,2},{4,5},{5,4},{6,7},{7,6},{8,9},{9,8},{10,11... | collective-permute-start | bytes 393224 | tf_op jit(solution)/shard_map/ppermute | solution.py:367
  72.0 0.6 collective-permute-done.21.refs_7_
  72.8 1.1 %collective-permute-done.23.refs_9_ = bf16[256,1024]{1,0:T(8,128)(2,1)} collective-permute-done((bf16[256,1024]{1,0:T(8,128)(2,1)}, bf16[256,1024]{1,0:T(8,128)(2,1)}, u32[]{:S(2)}, u32[]{:S(2)}) %collective-permute-start.23) | collective-permute-done | bytes 524320 | tf_op jit(solution)/shard_map/ppermute | solution.py:358
  74.0 1.1 %copy-done.5 = bf16[384,1792]{1,0:T(8,128)(2,1)} copy-done((bf16[384,1792]{1,0:T(8,128)(2,1)}, bf16[384,1792]{1,0:T(8,128)(2,1)S(1)}, u32[]{:S(2)}) %copy-start.5) | copy-done | bytes 1376280
  75.1 8.3 %rows_grad.9 = bf16[384,8192]{1,0:T(8,128)(2,1)} custom-call(s32[16]{0:T(128)} %refs_0_.11, s32[16]{0:T(128)} %refs_1_.9, s32[16]{0:T(128)} %refs_2_.9, bf16[384,1024]{1,0:T(8,128)(2,1)} %refs_3_.9, bf16[256,1024]{1,0:T(8,128)(2,1)} %copy-done.7, bf16[256,1024]{1,0:T(8,128)(2,1)} %copy-done.9, ...), custom_call_target="tpu_custom_call", output_to_operand_aliasing={{}: (16, {})} | custom-call | flops 1024 | bytes 1024 | tf_op jit(solution)/shard_map/rows_grad/pallas_call | solution.py:282
  83.4 0.7 fusion
  (67 shorter events, 4.7 us)
Async XLA Ops:
  0.6 11.0 %collective-permute-start.1 = (bf16[384,1024]{1,0:T(8,128)(2,1)}, bf16[384,1024]{1,0:T(8,128)(2,1)S(1)}, u32[]{:S(2)}, u32[]{:S(2)}) collective-permute-start(bf16[384,1024]{1,0:T(8,128)(2,1)} %refs_3_.9), channel_id=1, source_target_pairs={{0,4},{4,0},{8,12},{12,8},{1,5},{5,1},{9,13},{13,9},{2,6},{6,2},{1... | collective-permute-start | bytes 2359304 | tf_op jit(solution)/shard_map/ppermute | solution.py:358
  2.1 9.5 %collective-permute-start = (bf16[128,1024]{1,0:T(8,128)(2,1)S(1)}, bf16[128,1024]{1,0:T(8,128)(2,1)S(1)}, u32[]{:S(2)}, u32[]{:S(2)}) collective-permute-start(bf16[128,1024]{1,0:T(8,128)(2,1)S(1)} %constant_dynamic-slice_fusion), channel_id=1, source_target_pairs={{0,8},{4,12},{8,0},{12,4},{1,9},{5,13},{9,1},{13,5},{2,10},{6,14},... | collective-permute-start | bytes 786440 | tf_op jit(solution)/shard_map/ppermute | solution.py:361
  11.3 31.4 %copy-start.10 = (f32[8,128,128]{2,1,0:T(8,128)S(1)}, f32[8,128,128]{2,1,0:T(8,128)}, u32[]{:S(2)}) copy-start(f32[8,128,128]{2,1,0:T(8,128)} %get-tuple-element.60) | copy-start | bytes 1572868
  11.7 33.8 %copy-start.12 = (bf16[128,1024]{1,0:T(8,128)(2,1)}, bf16[128,1024]{1,0:T(8,128)(2,1)S(1)}, u32[]{:S(2)}) copy-start(bf16[128,1024]{1,0:T(8,128)(2,1)S(1)} %collective-permute-done.refs_5_) | copy-start | bytes 786436
  11.7 20.0 %copy-start = (bf16[384,1024]{1,0:T(8,128)(2,1)}, bf16[384,1024]{1,0:T(8,128)(2,1)S(1)}, u32[]{:S(2)}) copy-start(bf16[384,1024]{1,0:T(8,128)(2,1)S(1)} %collective-permute-done.1.refs_4_) | copy-start | bytes 2359300
  11.7 11.9 %collective-permute-start.5 = (f32[8,128,128]{2,1,0:T(8,128)}, f32[8,128,128]{2,1,0:T(8,128)S(1)}, u32[]{:S(2)}, u32[]{:S(2)}) collective-permute-start(f32[8,128,128]{2,1,0:T(8,128)} %get-tuple-element.53), channel_id=1, source_target_pairs={{0,4},{4,0},{8,12},{12,8},{1,5},{5,1},{9,13},{13,9},{2,6},{6,2},{1... | collective-permute-start | bytes 1572872 | tf_op jit(solution)/shard_map/ppermute | solution.py:358
  11.7 11.7 %collective-permute-start.2 = (bf16[128,1024]{1,0:T(8,128)(2,1)}, bf16[128,1024]{1,0:T(8,128)(2,1)S(1)}, u32[]{:S(2)}, u32[]{:S(2)}) collective-permute-start(bf16[128,1024]{1,0:T(8,128)(2,1)} %get-tuple-element.51), channel_id=1, source_target_pairs={{0,8},{4,12},{8,0},{12,4},{1,9},{5,13},{9,1},{13,5},{2,10},{6,14},... | collective-permute-start | bytes 786440 | tf_op jit(solution)/shard_map/ppermute | solution.py:361
  13.5 9.9 %collective-permute-start.4 = (bf16[128,1024]{1,0:T(8,128)(2,1)S(1)}, bf16[128,1024]{1,0:T(8,128)(2,1)S(1)}, u32[]{:S(2)}, u32[]{:S(2)}) collective-permute-start(bf16[128,1024]{1,0:T(8,128)(2,1)S(1)} %collective-permute-done.refs_5_), channel_id=1, source_target_pairs={{0,1},{1,0},{2,3},{3,2},{4,5},{5,4},{6,7},{7,6},{8,9},{9,8},{10,11... | collective-permute-start | bytes 786440 | tf_op jit(solution)/shard_map/ppermute | solution.py:367
  15.1 8.4 %collective-permute-start.3 = (bf16[128,1024]{1,0:T(8,128)(2,1)S(1)}, bf16[128,1024]{1,0:T(8,128)(2,1)S(1)}, u32[]{:S(2)}, u32[]{:S(2)}) collective-permute-start(bf16[128,1024]{1,0:T(8,128)(2,1)S(1)} %collective-permute-done.refs_5_), channel_id=1, source_target_pairs={{0,16},{16,0},{1,17},{17,1},{2,18},{18,2},{3,19},{19,3},{4,20},{20... | collective-permute-start | bytes 786440 | tf_op jit(solution)/shard_map/ppermute | solution.py:364
  16.6 6.8 %collective-permute-start.6 = (bf16[4,128,128]{2,1,0:T(8,128)(2,1)S(1)}, bf16[4,128,128]{2,1,0:T(8,128)(2,1)S(1)}, u32[]{:S(2)}, u32[]{:S(2)}) collective-permute-start(bf16[4,128,128]{2,1,0:T(8,128)(2,1)S(1)} %copy-done.1), channel_id=1, source_target_pairs={{0,8},{4,12},{8,0},{12,4},{1,9},{5,13},{9,1},{13,5},{2,10},{6,14},... | collective-permute-start | bytes 393224 | tf_op jit(solution)/shard_map/ppermute | solution.py:361
  23.5 22.0 %copy-start.13 = (bf16[128,1024]{1,0:T(8,128)(2,1)}, bf16[128,1024]{1,0:T(8,128)(2,1)S(1)}, u32[]{:S(2)}) copy-start(bf16[128,1024]{1,0:T(8,128)(2,1)S(1)} %collective-permute-done.2.refs_8_) | copy-start | bytes 786436
  23.5 21.9 %copy-start.14 = (bf16[128,1024]{1,0:T(8,128)(2,1)}, bf16[128,1024]{1,0:T(8,128)(2,1)S(1)}, u32[]{:S(2)}) copy-start(bf16[128,1024]{1,0:T(8,128)(2,1)S(1)} %collective-permute-done.4.refs_7_) | copy-start | bytes 786436
  23.5 21.9 %copy-start.15 = (bf16[128,1024]{1,0:T(8,128)(2,1)}, bf16[128,1024]{1,0:T(8,128)(2,1)S(1)}, u32[]{:S(2)}) copy-start(bf16[128,1024]{1,0:T(8,128)(2,1)S(1)} %collective-permute-done.3.refs_6_) | copy-start | bytes 786436
  23.5 7.6 %collective-permute-start.8 = (bf16[4,128,128]{2,1,0:T(8,128)(2,1)S(1)}, bf16[4,128,128]{2,1,0:T(8,128)(2,1)S(1)}, u32[]{:S(2)}, u32[]{:S(2)}) collective-permute-start(bf16[4,128,128]{2,1,0:T(8,128)(2,1)S(1)} %collective-permute-done.6.refs_8_.refs_11_.refs_12_), channel_id=1, source_target_pairs={{0,4},{4,0},{8,12},{12,8},{1,5},{5,1},{9,13},{13,9},{2,6},{6,2},{1... | collective-permute-start | bytes 393224 | tf_op jit(solution)/shard_map/ppermute | solution.py:358
  23.6 7.0 %collective-permute-start.7 = (bf16[4,128,128]{2,1,0:T(8,128)(2,1)S(1)}, bf16[4,128,128]{2,1,0:T(8,128)(2,1)S(1)}, u32[]{:S(2)}, u32[]{:S(2)}) collective-permute-start(bf16[4,128,128]{2,1,0:T(8,128)(2,1)S(1)} %copy-done.1), channel_id=1, source_target_pairs={{0,4},{4,0},{8,12},{12,8},{1,5},{5,1},{9,13},{13,9},{2,6},{6,2},{1... | collective-permute-start | bytes 393224 | tf_op jit(solution)/shard_map/ppermute | solution.py:358
  25.8 12.6 %collective-permute-start.12 = (f32[4,128,128]{2,1,0:T(8,128)}, f32[4,128,128]{2,1,0:T(8,128)}, u32[]{:S(2)}, u32[]{:S(2)}) collective-permute-start(f32[4,128,128]{2,1,0:T(8,128)} %slice_add_fusion), channel_id=1, source_target_pairs={{0,8},{4,12},{8,0},{12,4},{1,9},{5,13},{9,1},{13,5},{2,10},{6,14},... | collective-permute-start | bytes 786440 | tf_op jit(solution)/shard_map/ppermute | solution.py:361
  27.5 10.8 %collective-permute-start.11 = (bf16[128,1024]{1,0:T(8,128)(2,1)S(1)}, bf16[128,1024]{1,0:T(8,128)(2,1)}, u32[]{:S(2)}, u32[]{:S(2)}) collective-permute-start(bf16[128,1024]{1,0:T(8,128)(2,1)S(1)} %collective-permute-done.4.refs_7_), channel_id=1, source_target_pairs={{0,16},{16,0},{1,17},{17,1},{2,18},{18,2},{3,19},{19,3},{4,20},{20... | collective-permute-start | bytes 786440 | tf_op jit(solution)/shard_map/ppermute | solution.py:364
  29.1 9.3 %collective-permute-start.10 = (bf16[128,1024]{1,0:T(8,128)(2,1)S(1)}, bf16[128,1024]{1,0:T(8,128)(2,1)}, u32[]{:S(2)}, u32[]{:S(2)}) collective-permute-start(bf16[128,1024]{1,0:T(8,128)(2,1)S(1)} %collective-permute-done.2.refs_8_), channel_id=1, source_target_pairs={{0,1},{1,0},{2,3},{3,2},{4,5},{5,4},{6,7},{7,6},{8,9},{9,8},{10,11... | collective-permute-start | bytes 786440 | tf_op jit(solution)/shard_map/ppermute | solution.py:367
  30.6 10.6 %collective-permute-start.9 = (bf16[128,1024]{1,0:T(8,128)(2,1)S(1)}, bf16[128,1024]{1,0:T(8,128)(2,1)}, u32[]{:S(2)}, u32[]{:S(2)}) collective-permute-start(bf16[128,1024]{1,0:T(8,128)(2,1)S(1)} %collective-permute-done.2.refs_8_), channel_id=1, source_target_pairs={{0,16},{16,0},{1,17},{17,1},{2,18},{18,2},{3,19},{19,3},{4,20},{20... | collective-permute-start | bytes 786440 | tf_op jit(solution)/shard_map/ppermute | solution.py:364
  31.1 18.4 %collective-permute-start.13 = (bf16[256,1024]{1,0:T(8,128)(2,1)}, bf16[256,1024]{1,0:T(8,128)(2,1)S(1)}, u32[]{:S(2)}, u32[]{:S(2)}) collective-permute-start(bf16[256,1024]{1,0:T(8,128)(2,1)} %get-tuple-element.70), channel_id=1, source_target_pairs={{0,8},{4,12},{8,0},{12,4},{1,9},{5,13},{9,1},{13,5},{2,10},{6,14},... | collective-permute-start | bytes 1572872 | tf_op jit(solution)/shard_map/ppermute | solution.py:361
  41.3 8.3 %collective-permute-start.14 = (bf16[128,1024]{1,0:T(8,128)(2,1)}, bf16[128,1024]{1,0:T(8,128)(2,1)S(1)}, u32[]{:S(2)}, u32[]{:S(2)}) collective-permute-start(bf16[128,1024]{1,0:T(8,128)(2,1)} %collective-permute-done.10.refs_6_), channel_id=1, source_target_pairs={{0,16},{16,0},{1,17},{17,1},{2,18},{18,2},{3,19},{19,3},{4,20},{20... | collective-permute-start | bytes 786440 | tf_op jit(solution)/shard_map/ppermute | solution.py:364
  43.8 5.7 %collective-permute-start.15 = (f32[2,128,128]{2,1,0:T(8,128)S(1)}, f32[2,128,128]{2,1,0:T(8,128)}, u32[]{:S(2)}, u32[]{:S(2)}) collective-permute-start(f32[2,128,128]{2,1,0:T(8,128)S(1)} %slice.24), channel_id=1, source_target_pairs={{0,1},{1,0},{2,3},{3,2},{4,5},{5,4},{6,7},{7,6},{8,9},{9,8},{10,11... | collective-permute-start | bytes 393224 | tf_op jit(solution)/shard_map/ppermute | solution.py:367
  49.5 17.7 %collective-permute-start.20 = (bf16[384,1536]{1,0:T(8,128)(2,1)}, bf16[384,1536]{1,0:T(8,128)(2,1)S(1)}, u32[]{:S(2)}, u32[]{:S(2)}) collective-permute-start(bf16[384,1536]{1,0:T(8,128)(2,1)} %get-tuple-element.85), channel_id=1, source_target_pairs={{0,4},{4,0},{8,12},{12,8},{1,5},{5,1},{9,13},{13,9},{2,6},{6,2},{1... | collective-permute-start | bytes 3538952 | tf_op jit(solution)/shard_map/ppermute | solution.py:358
  49.6 17.1 %collective-permute-start.16 = (bf16[256,1024]{1,0:T(8,128)(2,1)}, bf16[256,1024]{1,0:T(8,128)(2,1)S(1)}, u32[]{:S(2)}, u32[]{:S(2)}) collective-permute-start(bf16[256,1024]{1,0:T(8,128)(2,1)} %get-tuple-element.83), channel_id=1, source_target_pairs={{0,8},{4,12},{8,0},{12,4},{1,9},{5,13},{9,1},{13,5},{2,10},{6,14},... | collective-permute-start | bytes 1572872 | tf_op jit(solution)/shard_map/ppermute | solution.py:361
  50.4 16.8 %collective-permute-start.18 = (bf16[256,1024]{1,0:T(8,128)(2,1)S(1)}, bf16[256,1024]{1,0:T(8,128)(2,1)S(1)}, u32[]{:S(2)}, u32[]{:S(2)}) collective-permute-start(bf16[256,1024]{1,0:T(8,128)(2,1)S(1)} %collective-permute-done.13.refs_9_), channel_id=1, source_target_pairs={{0,1},{1,0},{2,3},{3,2},{4,5},{5,4},{6,7},{7,6},{8,9},{9,8},{10,11... | collective-permute-start | bytes 1572872 | tf_op jit(solution)/shard_map/ppermute | solution.py:367
  51.3 15.9 %collective-permute-start.17 = (bf16[256,1024]{1,0:T(8,128)(2,1)S(1)}, bf16[256,1024]{1,0:T(8,128)(2,1)S(1)}, u32[]{:S(2)}, u32[]{:S(2)}) collective-permute-start(bf16[256,1024]{1,0:T(8,128)(2,1)S(1)} %collective-permute-done.13.refs_9_), channel_id=1, source_target_pairs={{0,16},{16,0},{1,17},{17,1},{2,18},{18,2},{3,19},{19,3},{4,20},{20... | collective-permute-start | bytes 1572872 | tf_op jit(solution)/shard_map/ppermute | solution.py:364
  53.2 13.6 %collective-permute-start.19 = (f32[2,128,128]{2,1,0:T(8,128)S(1)}, f32[2,128,128]{2,1,0:T(8,128)S(1)}, u32[]{:S(2)}, u32[]{:S(2)}) collective-permute-start(f32[2,128,128]{2,1,0:T(8,128)S(1)} %slice_add_fusion.1), channel_id=1, source_target_pairs={{0,2},{1,3},{2,0},{3,1},{4,6},{5,7},{6,4},{7,5},{8,10},{9,11},{10,... | collective-permute-start | bytes 393224 | tf_op jit(solution)/shard_map/ppermute | solution.py:367
  68.2 5.7 %collective-permute-start.24 = (bf16[384,1792]{1,0:T(8,128)(2,1)}, bf16[384,1792]{1,0:T(8,128)(2,1)S(1)}, u32[]{:S(2)}, u32[]{:S(2)}) collective-permute-start(bf16[384,1792]{1,0:T(8,128)(2,1)} %get-tuple-element.90), channel_id=1, source_target_pairs={{0,4},{4,0},{8,12},{12,8},{1,5},{5,1},{9,13},{13,9},{2,6},{6,2},{1... | collective-permute-start | bytes 4128776 | tf_op jit(solution)/shard_map/ppermute | solution.py:358
  68.2 4.4 %collective-permute-start.21 = (bf16[256,1024]{1,0:T(8,128)(2,1)S(1)}, bf16[256,1024]{1,0:T(8,128)(2,1)}, u32[]{:S(2)}, u32[]{:S(2)}) collective-permute-start(bf16[256,1024]{1,0:T(8,128)(2,1)S(1)} %collective-permute-done.16.refs_4_), channel_id=1, source_target_pairs={{0,4},{4,0},{8,12},{12,8},{1,5},{5,1},{9,13},{13,9},{2,6},{6,2},{1... | collective-permute-start | bytes 1572872 | tf_op jit(solution)/shard_map/ppermute | solution.py:358
  68.7 4.1 %collective-permute-start.22 = (bf16[256,1024]{1,0:T(8,128)(2,1)}, bf16[256,1024]{1,0:T(8,128)(2,1)}, u32[]{:S(2)}, u32[]{:S(2)}) collective-permute-start(bf16[256,1024]{1,0:T(8,128)(2,1)} %copy-done.9), channel_id=1, source_target_pairs={{0,4},{4,0},{8,12},{12,8},{1,5},{5,1},{9,13},{13,9},{2,6},{6,2},{1... | collective-permute-start | bytes 1572872 | tf_op jit(solution)/shard_map/ppermute | solution.py:358
  68.7 5.2 %collective-permute-start.23 = (bf16[256,1024]{1,0:T(8,128)(2,1)}, bf16[256,1024]{1,0:T(8,128)(2,1)}, u32[]{:S(2)}, u32[]{:S(2)}) collective-permute-start(bf16[256,1024]{1,0:T(8,128)(2,1)} %copy-done.8), channel_id=1, source_target_pairs={{0,4},{4,0},{8,12},{12,8},{1,5},{5,1},{9,13},{13,9},{2,6},{6,2},{1... | collective-permute-start | bytes 1572872 | tf_op jit(solution)/shard_map/ppermute | solution.py:358
  69.3 14.1 %collective-permute-start.25 = (f32[2,128,128]{2,1,0:T(8,128)S(1)}, f32[2,128,128]{2,1,0:T(8,128)S(1)}, u32[]{:S(2)}, u32[]{:S(2)}) collective-permute-start(f32[2,128,128]{2,1,0:T(8,128)S(1)} %add.33), channel_id=1, source_target_pairs={{0,1},{1,0},{2,3},{3,2},{4,5},{5,4},{6,7},{7,6},{8,9},{9,8},{10,11... | collective-permute-start | bytes 393224 | tf_op jit(solution)/shard_map/ppermute | solution.py:367
  (11 other events, 49.3 us)

commit v3 on v2

--- a/solution.py
+++ b/solution.py
@@ -9,7 +9,8 @@
 from jax.sharding import PartitionSpec as P
 
 BLOCK = 128
-VMEM_BYTES = 60 * 1024 * 1024
+VMEM_BYTES = 48 * 1024 * 1024
+GRAD_VMEM_BYTES = 60 * 1024 * 1024
 ANY_SPEC = pl.BlockSpec(memory_space=pl.ANY)
 HBM_SPEC = pl.BlockSpec(memory_space=pltpu.HBM)
 COST = pl.CostEstimate(flops=1024, bytes_accessed=1024, transcendentals=0)
@@ -37,7 +38,8 @@
     w_ref = refs.pop(0) if cuts else None
     out_refs, refs = refs[:outs], refs[outs:]
     cut_refs, refs = refs[: len(cuts)], refs[len(cuts) :]
-    rows_ref, cols_ref, slots_ref, act_buf, up_buf, act_sem, up_sem, i_sem, c_sem = refs
+    rows_ref, cols_ref, slots_ref, act_buf, up_buf, sums, *sems = refs
+    act_sem, up_sem, i_sem, c_sem, o_sem = sems
     nb = rows_ref.shape[0]
     index_copies = [
         pltpu.make_async_copy(src, dst, i_sem.at[n])
@@ -68,20 +70,25 @@
     ]
     for copy in cut_copies:
         copy.start()
-    for ref in out_refs:
-        ref[...] = jnp.zeros_like(ref)
+    if sums.shape[0] != nb:
+        sums[...] = jnp.zeros_like(sums)
     up_copy.wait()
     for b in range(nb):
         act_copy(b).wait()
+    for b in range(nb):
         column = pl.multiple_of(cols_ref[b] * BLOCK, BLOCK)
-        term = dot_tn(act_buf[b], up_buf[:, pl.ds(column, BLOCK)])
-        which, index = place(slots_ref[b])
-        for n, ref in enumerate(out_refs):
-
-            @pl.when(which == n)
-            def _():
-                ref[index] = term
-
+        sums[place(slots_ref[b])] = dot_tn(act_buf[b], up_buf[:, pl.ds(column, BLOCK)])
+    first = 0
+    out_copies = []
+    for n, ref in enumerate(out_refs):
+        out_copies.append(
+            pltpu.make_async_copy(sums.at[pl.ds(first, ref.shape[0])], ref, o_sem.at[n])
+        )
+        first += ref.shape[0]
+    for copy in out_copies:
+        copy.start()
+    for copy in out_copies:
+        copy.wait()
     for copy in cut_copies:
         copy.wait()
 
@@ -93,19 +100,21 @@
         out_shape=[jax.ShapeDtypeStruct((n, BLOCK, BLOCK), jnp.float32) for n in shapes]
         + [jax.ShapeDtypeStruct((n, weight.shape[1]), weight.dtype) for _, n in cuts],
         in_specs=[HBM_SPEC] * (6 if cuts else 5),
-        out_specs=[VMEM_SPEC] * (len(shapes) + len(cuts)),
+        out_specs=[HBM_SPEC] * len(shapes) + [VMEM_SPEC] * len(cuts),
         scratch_shapes=[
             pltpu.SMEM((nb,), jnp.int32),
             pltpu.SMEM((nb,), jnp.int32),
             pltpu.SMEM((nb,), jnp.int32),
             pltpu.VMEM((nb, act.shape[0], BLOCK), act.dtype),
             pltpu.VMEM(up.shape, up.dtype),
+            pltpu.VMEM((sum(shapes), BLOCK, BLOCK), jnp.float32),
             pltpu.SemaphoreType.DMA((nb,)),
             pltpu.SemaphoreType.DMA,
             pltpu.SemaphoreType.DMA((3,)),
             pltpu.SemaphoreType.DMA((max(1, len(cuts)),)),
+            pltpu.SemaphoreType.DMA((len(shapes),)),
         ],
-        compiler_params=pltpu.CompilerParams(vmem_limit_bytes=VMEM_BYTES),
+        compiler_params=pltpu.CompilerParams(vmem_limit_bytes=GRAD_VMEM_BYTES),
         cost_estimate=COST,
         name="block_grads",
     )(rows, cols, slots, act, up, *([weight] if cuts else []))
@@ -216,19 +225,27 @@
             ).wait()
         size = width * BLOCK
         start = t * BLOCK if isinstance(t, int) else pl.multiple_of(t * BLOCK, BLOCK)
-        acc[:, :size] = dot_nt(up_buf[...], w_buf[pl.ds(start, size)])
+        total = dot_nt(up_buf[...], w_buf[pl.ds(start, size)])
+        acc[:, :size] = total
         for h in range(width):
-
-            def add(b):
-                column = pl.multiple_of(cols_ref[b] * BLOCK, BLOCK)
-                delta = d_buf[delta_at(slots_ref[b])]
-                acc[:, h * BLOCK : (h + 1) * BLOCK] += dot_nt(
-                    up_buf[:, pl.ds(column, BLOCK)], delta
-                )
-                return after_it[b]
-
-            lax.while_loop(lambda b: b >= 0, add, head[table[t + h]])
-            o_buf[t + h] = acc[:, h * BLOCK : (h + 1) * BLOCK].astype(o_buf.dtype)
+            o_buf[t + h] = total[:, h * BLOCK : (h + 1) * BLOCK].astype(o_buf.dtype)
+        for h in range(width):
+            first_b = head[table[t + h]]
+
+            @pl.when(first_b >= 0)
+            def _():
+                def add(b):
+                    column = pl.multiple_of(cols_ref[b] * BLOCK, BLOCK)
+                    delta = d_buf[delta_at(slots_ref[b])]
+                    acc[:, h * BLOCK : (h + 1) * BLOCK] += dot_nt(
+                        up_buf[:, pl.ds(column, BLOCK)], delta
+                    )
+                    return after_it[b]
+
+                lax.while_loop(lambda b: b >= 0, add, first_b)
+                o_buf[t + h] = acc[:, h * BLOCK : (h + 1) * BLOCK].astype(o_buf.dtype)
+
+        for h in range(width):
             for copy in out_copies(t + h):
                 copy.start()
 
@@ -258,7 +275,7 @@
 
 def rows_grad(
     units, weights, rows, cols, slots, ups, deltas, delta_at, width, out=None, moves=(), moved=(), tile=4,
-    other=None, other_units=None, other_first=0,
+    other=None, other_units=None, other_first=0, vmem=VMEM_BYTES,
 ):
     n_units = len(units)
     tile = min(tile, n_units)
@@ -308,7 +325,7 @@
             pltpu.SemaphoreType.DMA((len(ups), n_units)),
             pltpu.SemaphoreType.DMA((2, max(1, len(moves)))),
         ],
-        compiler_params=pltpu.CompilerParams(vmem_limit_bytes=VMEM_BYTES),
+        compiler_params=pltpu.CompilerParams(vmem_limit_bytes=vmem),
         cost_estimate=COST,
         name="rows_grad",
     )(*operands)
@@ -321,7 +338,7 @@
     pattern = (block_rows, block_cols, block_slot)
 
     (partial,) = block_grads(
-        lambda slot: (0, slot), [n * local_slots], *pattern, activations, upstream
+        lambda slot: slot, [n * local_slots], *pattern, activations, upstream
     )
     mine = lax.psum_scatter(partial, "fsdp", scatter_dimension=0, tiled=True)
     totals = lax.psum(mine, "dp")
@@ -370,9 +387,8 @@
     sizes = (part // 4, part // 4, part // 2)
     offs = (0, sizes[0], sizes[0] + sizes[1])
 
-    def own_rows(flip, k):
-        first = (my_cell() ^ flip) * part + offs[k]
-        return lax.dynamic_slice_in_dim(frozen, first, sizes[k], 0)
+    def row_of(flip, k):
+        return lambda: (my_cell() ^ flip) * part + offs[k]
 
     def delta_at(slot):
         return ((slot // local_slots) ^ my_f()) * local_slots + slot % local_slots
@@ -406,104 +422,81 @@
     def place(slot):
         rel = (slot // local_slots) ^ my_f()
         at = slot % local_slots
-        index = (rel // 2) * local_slots + ((at // half) ^ (my_cell() % 2)) * half + at % half
-        return rel % 2, index
-
-    def multiply(units, pieces, ups, out, received=None, at=(), **other):
-        return rows_grad(
-            units, [p[0] for p in pieces], *pattern, ups, all_deltas, delta_at, width, out,
-            moves_of(at), [] if received is None else [received], **other,
-        )
-
-    def row_of(flip, k):
-        return lambda: (my_cell() ^ flip) * part + offs[k]
-
-    x0 = over_x(own_rows(0, 0))
+        index = ((at // half) ^ (lax.axis_index("dp") % 2)) * half + at % half
+        return ((rel % 2) * 2 + rel // 2) * local_slots + index
+
+    x0 = over_x(lax.dynamic_slice_in_dim(frozen, my_cell() * part, sizes[0], 0))
     up_sib = over_core(upstream)
+    dc = over_core(deltas)
     dx = over_x(deltas)
     keep, send, s1, s2, s3 = block_grads(
         place, [2 * local_slots, 2 * local_slots], *pattern, activations, upstream, frozen,
-        [(row_of(0, 1), sizes[1]), (row_of(0, 2), sizes[2]), (row_of(3, 2), sizes[2])],
-    )
-
-    x0, send, up_sib, s1 = lax.optimization_barrier((x0, send, up_sib, s1))
+        [(row_of(0, 1), sizes[1]), (row_of(0, 2), sizes[2]), (row_of(3, 1), sizes[1] + sizes[2])],
+    )
+
+    x0, send, up_sib, s1, s2, dc, dx = lax.optimization_barrier(
+        (x0, send, up_sib, s1, s2, dc, dx)
+    )
     y0, z0, x1 = over_y(x0), over_z(x0), over_x(s1)
     gc = over_core(send)
-
-    x1, y0, z0, gc, dx = lax.optimization_barrier((x1, y0, z0, gc, dx))
-    dc, dxc = over_core(after(deltas, dx)), over_core(dx)
     gx = over_x(keep[local_slots:] + gc[local_slots:])
-    x2 = over_x(after(s2, x1))
-    y1, z1 = over_y(x1), over_z(x1)
-    yd0 = over_y(z0)
+
+    dxc = over_core(dx)
     all_deltas = [deltas, dc, dx, dxc]
 
-    def multiply(units, pieces, ups, out, received=None, at=(), **other):
+    def multiply(pieces, ups, out, at=(), moved=(), units=None, **other):
+        moves = [
+            (m, first, column)
+            for m, there in enumerate(at)
+            for _, first, column in moves_of(there)
+        ]
         return rows_grad(
-            units, [p[0] for p in pieces], *pattern, ups, all_deltas, delta_at, width, out,
-            moves_of(at), [] if received is None else [received], **other,
-        )
-
-    own = [(frozen, 0, None, 0)]
-    own_units = units_of(own)
-    first_half = len(own_units) // 2
-    pieces2 = [(x0, 2, 0, offs[0]), (y0, 2, 2, offs[0]), (z0, 2, 1, offs[0]), (x1, 2, 0, offs[1])]
-    n_a = first_half + len(units_of(pieces2))
-    out, other_a = multiply(
-        own_units[:first_half], own, [upstream, after(up_sib, x1)], None, other_units=n_a
-    )
-
-    out, y1, z1, yd0, gx = lax.optimization_barrier((out, y1, z1, yd0, gx))
+            units or units_of(pieces), [p[0] for p in pieces], *pattern, ups, all_deltas, delta_at,
+            width, out, moves, moved, **other,
+        )
+
+    pieces1 = [(frozen, 0, None, 0)]
+    units1 = units_of(pieces1)
+    first_half = len(units1) // 2
+    out, other1 = multiply(
+        pieces1, [upstream, after(up_sib, x0)], None, units=units1[:first_half],
+        other_units=len(units1),
+    )
+
+    x1, y0, z0, gx, s2, out, other1 = lax.optimization_barrier(
+        (x1, y0, z0, gx, s2, out, other1)
+    )
+    x2 = over_x(s2)
+    y1, z1, yd = over_y(x1), over_z(x1), over_y(z0)
     owned = keep[:local_slots] + gc[:local_slots] + gx
     gz = over_z(owned[half:])
-    yd1 = over_y(z1)
-    x3 = over_x(after(s3, z1))
-    out, other_a = multiply(
-        units_of(pieces2), pieces2, [upstream, after(up_sib, z1)], out,
-        other=other_a, other_units=n_a, other_first=first_half * BLOCK,
-    )
-
-    out, other_a, x2, yd1, gz = lax.optimization_barrier((out, other_a, x2, yd1, gz))
+    out, other1 = multiply(
+        pieces1, [upstream, after(up_sib, x1)], out, units=units1[first_half:],
+        other=other1, other_units=len(units1), other_first=first_half * BLOCK,
+    )
+
+    out, other1, gz, x2, y1, z1, yd = lax.optimization_barrier(
+        (out, other1, gz, x2, y1, z1, yd)
+    )
     y2, z2 = over_y(x2), over_z(x2)
+    x3 = over_x(after(s3, x2))
     mine = owned[:half] + gz
     gz2 = over_z(mine, 2)
-    oa = over_core(other_a)
-    pieces3 = [
-        (y1, 2, 2, offs[1]), (z1, 2, 1, offs[1]), (yd0, 2, 3, offs[0]), (yd1, 2, 3, offs[1]),
-        (x2, 2, 0, offs[2]),
-    ]
-    n_3 = len(units_of(pieces3))
-    n_b = n_3 + len(own_units) - first_half
-    out, other_b = multiply(
-        units_of(pieces3), pieces3, [upstream, after(up_sib, x2)], out, other_units=n_b
-    )
-    out, other_b = multiply(
-        own_units[first_half:], own, [upstream, after(up_sib, x2)], out,
-        other=other_b, other_units=n_b, other_first=n_3 * BLOCK,
-    )
-
-    out, other_b, x3, y2, z2, gz2, oa = lax.optimization_barrier(
-        (out, other_b, x3, y2, z2, gz2, oa)
-    )
+    o1 = over_core(other1)
+    pieces2 = [
+        (x0, 2, 0, offs[0]), (y0, 2, 2, offs[0]), (z0, 2, 1, offs[0]), (x1, 2, 0, offs[1]),
+        (y1, 2, 2, offs[1]), (z1, 2, 1, offs[1]), (yd, 2, 3, offs[0]), (x2, 2, 0, offs[2]),
+    ]
+    out, other2 = multiply(pieces2, [upstream, after(up_sib, x2)], out, [pieces1], [o1])
+
+    out, other2, x3, y2, z2, gz2 = lax.optimization_barrier((out, other2, x3, y2, z2, gz2))
     mine = mine + gz2
-    ob = over_core(other_b)
-    last = [(x3, 2, 3, offs[2]), (y2, 2, 2, offs[2]), (z2, 2, 1, offs[2])]
+    other_half = over_z(mine)
+    o2 = over_core(other2)
+    last = [(x3, 2, 3, offs[1]), (y2, 2, 2, offs[2]), (z2, 2, 1, offs[2])]
     last = last + [(over_core(a), 3, cell, at) for a, _, cell, at in last]
-    other_half = over_z(mine)
-    own_moves = moves_of(own)
-
-    def moved(m, moves):
-        return [(m, u * BLOCK, column) for u, (_, _, column) in enumerate(moves)]
-
-    (out,) = rows_grad(
-        units_of(last), [p[0] for p in last], *pattern, [upstream], all_deltas, delta_at, width,
-        out,
-        moved(0, own_moves[:first_half] + moves_of(pieces2))
-        + moved(1, moves_of(pieces3) + own_moves[first_half:]),
-        [oa, ob],
-    )
+    (out,) = multiply(last, [upstream], out, [pieces2], [o2])
     other_half = after(other_half, out)
-
     normalizer = 1.0 / math.sqrt(upstream.shape[0] * lax.axis_size("fsdp") * n_dp)
     totals = jnp.where(
         lax.axis_index("dp") % 2 == 0,

time: 84.5 us -> 79.4 us (0.940)
  waiting for transfers between devices: 12 us -> 24.8 us
  Pallas kernels: 36.4 us -> 27.6 us
  starting transfers between devices: 27.3 us -> 20.5 us
  local copies, waits for them, and re-layouts: 3.21 us -> 2.28 us
    pallas_call x5 -> x4, Pallas kernels: 29.8 us -> 22.2 us  [rows_grad(): pl.pallas_call(functools.partial(rows_kernel, units, moves, tile, width /...]
    ppermute x6, waiting for transfers between devices: 0.47 us -> 6.74 us  [over_z(): return lax.ppermute(a, 'dp', [(k, k ^ step) for k in range(n_dp)])]
    ppermute x6, waiting for transfers between devices: 6.62 us -> 11 us  [over_x(): return lax.ppermute(a, 'fsdp', [(k, k ^ 2) for k in range(4)])]
    ppermute x6, starting transfers between devices: 11.1 us -> 7.22 us  [over_z(): return lax.ppermute(a, 'dp', [(k, k ^ step) for k in range(n_dp)])]
    ppermute x9, waiting for transfers between devices: 2 us -> 4.48 us  [over_core(): return lax.ppermute(a, 'fsdp', [(k, k ^ 1) for k in range(4)])]
    ppermute x5 -> x4, starting transfers between devices: 5.96 us -> 4.37 us  [over_y(): return lax.ppermute(a, 'group', [(k, k ^ 1) for k in range(2)])]
    pallas_call x1, Pallas kernels: 6.61 us -> 5.35 us  [block_grads(): pl.pallas_call(functools.partial(grad_kernel, place, len(shapes), cuts),...]
    mul x1, other arithmetic: 0.73 us -> 1.83 us  [relayed(): jnp.where(lax.axis_index('dp') % 2 == 0, jnp.concatenate([mine, other_hal...]
  transfers between devices with their start and end apart: 26 -> 25, of which waited for: 7 -> 12; matrix products, arithmetic and copies ran while one was open for 5% -> 3% of each run, Pallas kernels for 43% -> 35%
where the time goes in v3:
time: 79.4 us; the launch traced here: 79.5 us
  Pallas kernels  27.6 us (35%)
  waiting for transfers between devices  24.8 us (31%)
  starting transfers between devices  20.5 us (26%)
  other arithmetic  3.53 us (4%)
  local copies, waits for them, and re-layouts  2.28 us (3%)
  between operations  0.8 us (1%)
    pallas_call x4, Pallas kernels, rows_grad(): pl.pallas_call(functools.partial(rows_kernel, units, moves, tile, width /...  22.2 us
    ppermute x6, waiting for transfers between devices, over_x(): return lax.ppermute(a, 'fsdp', [(k, k ^ 2) for k in range(4)])  11 us
    ppermute x6, starting transfers between devices, over_z(): return lax.ppermute(a, 'dp', [(k, k ^ step) for k in range(n_dp)])  7.22 us
    ppermute x6, starting transfers between devices, over_x(): return lax.ppermute(a, 'fsdp', [(k, k ^ 2) for k in range(4)])  7.16 us
    ppermute x6, waiting for transfers between devices, over_z(): return lax.ppermute(a, 'dp', [(k, k ^ step) for k in range(n_dp)])  6.74 us
    pallas_call x1, Pallas kernels, block_grads(): pl.pallas_call(functools.partial(grad_kernel, place, len(shapes), cuts),...  5.35 us
    ppermute x9, waiting for transfers between devices, over_core(): return lax.ppermute(a, 'fsdp', [(k, k ^ 1) for k in range(4)])  4.48 us
    ppermute x4, starting transfers between devices, over_y(): return lax.ppermute(a, 'group', [(k, k ^ 1) for k in range(2)])  4.37 us
  transfers between devices with their start and end apart: 25, of which 12 were waited for; matrix products, arithmetic and copies ran while one was open for 3% of the time, Pallas kernels for 35%

profile of v3, /device:TPU:0, one launch (start us, length us, event | category | flops | bytes accessed | tf_op | source)
XLA Modules:
  0.0 79.5 jit_solution(12552547090341668278)
XLA Ops:
  0.6 0.5 collective-permute-start.1
  1.2 1.0 %constant_dynamic-slice_fusion = bf16[128,1024]{1,0:T(8,128)(2,1)S(1)} fusion(bf16[2048,1024]{1,0:T(8,128)(2,1)} %refs_5_.3, s32[]{:T(128)S(6)} %select_n.21), kind=kLoop, calls=%fused_computation.6 | loop fusion | bytes 524292 | tf_op jit(solution)/shard_map/dynamic_slice | solution.py:428
  2.2 2.6 %collective-permute-start = (bf16[128,1024]{1,0:T(8,128)(2,1)S(1)}, bf16[128,1024]{1,0:T(8,128)(2,1)S(1)}, u32[]{:S(2)}, u32[]{:S(2)}) collective-permute-start(bf16[128,1024]{1,0:T(8,128)(2,1)S(1)} %constant_dynamic-slice_fusion), channel_id=1, source_target_pairs={{0,8},{4,12},{8,0},{12,4},{1,9},{5,13},{9,1},{13,5},{2,10},{6,14},... | collective-permute-start | bytes 786440 | tf_op jit(solution)/shard_map/ppermute | solution.py:378
  5.4 5.4 %block_grads.1 = (f32[8,128,128]{2,1,0:T(8,128)}, f32[8,128,128]{2,1,0:T(8,128)}, bf16[128,1024]{1,0:T(8,128)(2,1)}, bf16[256,1024]{1,0:T(8,128)(2,1)}, bf16[384,1024]{1,0:T(8,128)(2,1)}) custom-call(s32[16]{0:T(128)} %refs_0_.9, s32[16]{0:T(128)} %refs_1_.7, s32[16]{0:T(128)} %refs_2_.7, bf16[384,8192]{1,0:T(8,128)(2,1)} %act_ref.1, ...), custom_call_target="tpu_custom_call" | custom-call | flops 1024 | bytes 1024 | tf_op jit(solution)/shard_map/block_grads/pallas_call | solution.py:98
  10.8 3.8 %collective-permute-done.3.refs_8_.refs_15_.refs_12_ = bf16[4,128,128]{2,1,0:T(8,128)(2,1)S(1)} collective-permute-done((bf16[4,128,128]{2,1,0:T(8,128)(2,1)}, bf16[4,128,128]{2,1,0:T(8,128)(2,1)S(1)}, u32[]{:S(2)}, u32[]{:S(2)}) %collective-permute-start.3) | collective-permute-done | bytes 131104 | tf_op jit(solution)/shard_map/ppermute | solution.py:378
  14.6 1.8 %collective-permute-start.5 = (bf16[128,1024]{1,0:T(8,128)(2,1)S(1)}, bf16[128,1024]{1,0:T(8,128)(2,1)S(1)}, u32[]{:S(2)}, u32[]{:S(2)}) collective-permute-start(bf16[128,1024]{1,0:T(8,128)(2,1)S(1)} %collective-permute-done.refs_5_), channel_id=1, source_target_pairs={{0,16},{16,0},{1,17},{17,1},{2,18},{18,2},{3,19},{19,3},{4,20},{20... | collective-permute-start | bytes 786440 | tf_op jit(solution)/shard_map/ppermute | solution.py:381
  16.4 1.6 %collective-permute-start.6 = (bf16[128,1024]{1,0:T(8,128)(2,1)S(1)}, bf16[128,1024]{1,0:T(8,128)(2,1)S(1)}, u32[]{:S(2)}, u32[]{:S(2)}) collective-permute-start(bf16[128,1024]{1,0:T(8,128)(2,1)S(1)} %collective-permute-done.refs_5_), channel_id=1, source_target_pairs={{0,1},{1,0},{2,3},{3,2},{4,5},{5,4},{6,7},{7,6},{8,9},{9,8},{10,11... | collective-permute-start | bytes 786440 | tf_op jit(solution)/shard_map/ppermute | solution.py:384
  18.0 1.5 %collective-permute-start.4 = (bf16[128,1024]{1,0:T(8,128)(2,1)}, bf16[128,1024]{1,0:T(8,128)(2,1)S(1)}, u32[]{:S(2)}, u32[]{:S(2)}) collective-permute-start(bf16[128,1024]{1,0:T(8,128)(2,1)} %get-tuple-element.49), channel_id=1, source_target_pairs={{0,8},{4,12},{8,0},{12,4},{1,9},{5,13},{9,1},{13,5},{2,10},{6,14},... | collective-permute-start | bytes 786440 | tf_op jit(solution)/shard_map/ppermute | solution.py:378
  19.5 1.0 %slice_add_fusion.1 = f32[4,128,128]{2,1,0:T(8,128)S(1)} fusion(f32[8,128,128]{2,1,0:T(8,128)S(1)} %collective-permute-done.7, f32[8,128,128]{2,1,0:T(8,128)} %get-tuple-element.51), kind=kLoop, calls=%fused_computation.2 | loop fusion | flops 65536 | bytes 786432 | tf_op jit(solution)/shard_map/add | solution.py:442
  20.5 0.6 collective-permute-start.8
  21.1 1.3 %collective-permute-done.9.refs_9_.refs_16_.refs_13_ = bf16[4,128,128]{2,1,0:T(8,128)(2,1)S(1)} collective-permute-done((bf16[4,128,128]{2,1,0:T(8,128)(2,1)S(1)}, bf16[4,128,128]{2,1,0:T(8,128)(2,1)S(1)}, u32[]{:S(2)}, u32[]{:S(2)}) %collective-permute-start.9) | collective-permute-done | bytes 131104 | tf_op jit(solution)/shard_map/ppermute | solution.py:375
  22.4 4.6 %rows_grad.4 = (bf16[384,8192]{1,0:T(8,128)(2,1)}, bf16[384,2048]{1,0:T(8,128)(2,1)S(1)}) custom-call(s32[16]{0:T(128)S(1)} %copy-done.2, s32[16]{0:T(128)S(1)} %copy-done.3, s32[16]{0:T(128)S(1)} %copy-done.4, bf16[384,1024]{1,0:T(8,128)(2,1)S(1)} %copy-done, bf16[384,1024]{1,0:T(8,128)(2,1)S(1)} %collective-permute-done.1.refs_4_, ...), custom_call_target="tpu_custom_call" | custom-call | flops 1024 | bytes 1024 | tf_op jit(solution)/shard_map/rows_grad/pallas_call | solution.py:299
  27.4 4.5 %collective-permute-done.8 = f32[4,128,128]{2,1,0:T(8,128)S(1)} collective-permute-done((f32[4,128,128]{2,1,0:T(8,128)S(1)}, f32[4,128,128]{2,1,0:T(8,128)S(1)}, u32[]{:S(2)}, u32[]{:S(2)}) %collective-permute-start.8) | collective-permute-done | bytes 262176 | tf_op jit(solution)/shard_map/ppermute | solution.py:378
  31.9 1.5 %collective-permute-start.11 = (bf16[256,1024]{1,0:T(8,128)(2,1)S(1)}, bf16[256,1024]{1,0:T(8,128)(2,1)S(1)}, u32[]{:S(2)}, u32[]{:S(2)}) collective-permute-start(bf16[256,1024]{1,0:T(8,128)(2,1)S(1)} %copy-done.8), channel_id=1, source_target_pairs={{0,8},{4,12},{8,0},{12,4},{1,9},{5,13},{9,1},{13,5},{2,10},{6,14},... | collective-permute-start | bytes 1572872 | tf_op jit(solution)/shard_map/ppermute | solution.py:378
  34.4 1.5 %collective-permute-start.14 = (bf16[128,1024]{1,0:T(8,128)(2,1)S(1)}, bf16[128,1024]{1,0:T(8,128)(2,1)S(1)}, u32[]{:S(2)}, u32[]{:S(2)}) collective-permute-start(bf16[128,1024]{1,0:T(8,128)(2,1)S(1)} %collective-permute-done.6.refs_7_), channel_id=1, source_target_pairs={{0,16},{16,0},{1,17},{17,1},{2,18},{18,2},{3,19},{19,3},{4,20},{20... | collective-permute-start | bytes 786440 | tf_op jit(solution)/shard_map/ppermute | solution.py:381
  36.0 1.6 %collective-permute-start.10 = (f32[2,128,128]{2,1,0:T(8,128)S(1)}, f32[2,128,128]{2,1,0:T(8,128)S(1)}, u32[]{:S(2)}, u32[]{:S(2)}) collective-permute-start(f32[2,128,128]{2,1,0:T(8,128)S(1)} %slice.26), channel_id=1, source_target_pairs={{0,1},{1,0},{2,3},{3,2},{4,5},{5,4},{6,7},{7,6},{8,9},{9,8},{10,11... | collective-permute-start | bytes 393224 | tf_op jit(solution)/shard_map/ppermute | solution.py:384
  37.6 4.9 %rows_grad.5 = (bf16[384,8192]{1,0:T(8,128)(2,1)}, bf16[384,2048]{1,0:T(8,128)(2,1)S(1)}) custom-call(s32[16]{0:T(128)S(1)} %copy-done.2, s32[16]{0:T(128)S(1)} %copy-done.3, s32[16]{0:T(128)S(1)} %copy-done.4, bf16[384,1024]{1,0:T(8,128)(2,1)S(1)} %copy-done, ...), custom_call_target="tpu_custom_call", output_to_operand_aliasing={{0}: (10, {}), {1}: (11, {})} | custom-call | flops 1024 | bytes 1024 | tf_op jit(solution)/shard_map/rows_grad/pallas_call | solution.py:299
  42.5 0.9 %collective-permute-done.10 = f32[2,128,128]{2,1,0:T(8,128)S(1)} collective-permute-done((f32[2,128,128]{2,1,0:T(8,128)S(1)}, f32[2,128,128]{2,1,0:T(8,128)S(1)}, u32[]{:S(2)}, u32[]{:S(2)}) %collective-permute-start.10) | collective-permute-done | bytes 131104 | tf_op jit(solution)/shard_map/ppermute | solution.py:384
  43.4 2.6 %collective-permute-done.14.refs_11_ = bf16[128,1024]{1,0:T(8,128)(2,1)S(1)} collective-permute-done((bf16[128,1024]{1,0:T(8,128)(2,1)S(1)}, bf16[128,1024]{1,0:T(8,128)(2,1)S(1)}, u32[]{:S(2)}, u32[]{:S(2)}) %collective-permute-start.14) | collective-permute-done | bytes 262176 | tf_op jit(solution)/shard_map/ppermute | solution.py:381
  46.0 0.6 collective-permute-start.16
  47.5 2.7 %collective-permute-start.19 = (f32[2,128,128]{2,1,0:T(8,128)S(1)}, f32[2,128,128]{2,1,0:T(8,128)S(1)}, u32[]{:S(2)}, u32[]{:S(2)}) collective-permute-start(f32[2,128,128]{2,1,0:T(8,128)S(1)} %slice_add_fusion.2), channel_id=1, source_target_pairs={{0,2},{1,3},{2,0},{3,1},{4,6},{5,7},{6,4},{7,5},{8,10},{9,11},{10,... | collective-permute-start | bytes 393224 | tf_op jit(solution)/shard_map/ppermute | solution.py:384
  50.2 1.2 %copy-done.5 = bf16[384,2048]{1,0:T(8,128)(2,1)} copy-done((bf16[384,2048]{1,0:T(8,128)(2,1)}, bf16[384,2048]{1,0:T(8,128)(2,1)S(1)}, u32[]{:S(2)}) %copy-start.5) | copy-done | bytes 1572888
  51.4 6.5 %rows_grad.6 = (bf16[384,8192]{1,0:T(8,128)(2,1)}, bf16[384,1152]{1,0:T(8,128)(2,1)}) custom-call(s32[16]{0:T(128)S(1)} %copy-done.2, s32[16]{0:T(128)S(1)} %copy-done.3, s32[16]{0:T(128)S(1)} %copy-done.4, bf16[384,1024]{1,0:T(8,128)(2,1)S(1)} %copy-done, bf16[384,1024]{1,0:T(8,128)(2,1)S(1)} %collective-permute-done.1.refs_4_, ...), custom_call_target="tpu_custom_call", output_to_operand_aliasing={{0}: (18, {})} | custom-call | flops 1024 | bytes 1024 | tf_op jit(solution)/shard_map/rows_grad/pallas_call | solution.py:299
  57.9 3.6 %collective-permute-done.19 = f32[2,128,128]{2,1,0:T(8,128)S(1)} collective-permute-done((f32[2,128,128]{2,1,0:T(8,128)S(1)}, f32[2,128,128]{2,1,0:T(8,128)S(1)}, u32[]{:S(2)}, u32[]{:S(2)}) %collective-permute-start.19) | collective-permute-done | bytes 131104 | tf_op jit(solution)/shard_map/ppermute | solution.py:384
  61.5 2.2 %collective-permute-done.18.refs_6_ = bf16[256,1024]{1,0:T(8,128)(2,1)} collective-permute-done((bf16[256,1024]{1,0:T(8,128)(2,1)S(1)}, bf16[256,1024]{1,0:T(8,128)(2,1)}, u32[]{:S(2)}, u32[]{:S(2)}) %collective-permute-start.18) | collective-permute-done | bytes 524320 | tf_op jit(solution)/shard_map/ppermute | solution.py:384
  63.7 2.3 %collective-permute-done.16.refs_4_ = bf16[384,1024]{1,0:T(8,128)(2,1)} collective-permute-done((bf16[384,1024]{1,0:T(8,128)(2,1)S(1)}, bf16[384,1024]{1,0:T(8,128)(2,1)}, u32[]{:S(2)}, u32[]{:S(2)}) %collective-permute-start.16) | collective-permute-done | bytes 786464 | tf_op jit(solution)/shard_map/ppermute | solution.py:378
  66.0 0.5 collective-permute-start.20
  66.5 0.5 collective-permute-start.22
  67.1 0.7 add.33
  68.2 2.7 %collective-permute-done.21.refs_8_ = bf16[256,1024]{1,0:T(8,128)(2,1)} collective-permute-done((bf16[256,1024]{1,0:T(8,128)(2,1)S(1)}, bf16[256,1024]{1,0:T(8,128)(2,1)}, u32[]{:S(2)}, u32[]{:S(2)}) %collective-permute-start.21) | collective-permute-done | bytes 524320 | tf_op jit(solution)/shard_map/ppermute | solution.py:375
  71.3 6.3 %rows_grad.7 = bf16[384,8192]{1,0:T(8,128)(2,1)} custom-call(s32[16]{0:T(128)S(1)} %copy-done.2, s32[16]{0:T(128)S(1)} %copy-done.3, s32[16]{0:T(128)S(1)} %copy-done.4, bf16[384,1024]{1,0:T(8,128)(2,1)S(1)} %copy-done, bf16[384,1024]{1,0:T(8,128)(2,1)} %collective-permute-done.16.refs_4_, ...), custom_call_target="tpu_custom_call", output_to_operand_aliasing={{}: (15, {})} | custom-call | flops 1024 | bytes 1024 | tf_op jit(solution)/shard_map/rows_grad/pallas_call | solution.py:299
  77.6 1.8 %fusion.1 = f32[4,128,128]{2,1,0:T(8,128)} fusion(f32[2,128,128]{2,1,0:T(8,128)} %collective-permute-done.24, f32[2,128,128]{2,1,0:T(8,128)} %add.33, pred[]{:T(512)S(6)} %eq.6), kind=kLoop, calls=%fused_computation.4 | loop fusion | flops 262144 | bytes 524289 | tf_op jit(solution)/shard_map/mul | solution.py:501
  (48 shorter events, 3.8 us)
Async XLA Ops:
  0.6 13.9 %collective-permute-start.1 = (bf16[384,1024]{1,0:T(8,128)(2,1)}, bf16[384,1024]{1,0:T(8,128)(2,1)S(1)}, u32[]{:S(2)}, u32[]{:S(2)}) collective-permute-start(bf16[384,1024]{1,0:T(8,128)(2,1)} %refs_3_.7), channel_id=1, source_target_pairs={{0,4},{4,0},{8,12},{12,8},{1,5},{5,1},{9,13},{13,9},{2,6},{6,2},{1... | collective-permute-start | bytes 2359304 | tf_op jit(solution)/shard_map/ppermute | solution.py:375
  1.1 21.3 %copy-start = (bf16[384,1024]{1,0:T(8,128)(2,1)S(1)}, bf16[384,1024]{1,0:T(8,128)(2,1)}, u32[]{:S(2)}) copy-start(bf16[384,1024]{1,0:T(8,128)(2,1)} %refs_3_.7) | copy-start | bytes 2359300
  1.1 21.3 %copy-start.1 = (bf16[4,128,128]{2,1,0:T(8,128)(2,1)S(1)}, bf16[4,128,128]{2,1,0:T(8,128)(2,1)}, u32[]{:S(2)}) copy-start(bf16[4,128,128]{2,1,0:T(8,128)(2,1)} %refs_10_.1) | copy-start | bytes 393220
  1.2 21.3 %copy-start.2 = (s32[16]{0:T(128)S(1)}, s32[16]{0:T(128)}, u32[]{:S(2)}) copy-start(s32[16]{0:T(128)} %refs_0_.9) | copy-start | bytes 196
  1.2 21.3 %copy-start.3 = (s32[16]{0:T(128)S(1)}, s32[16]{0:T(128)}, u32[]{:S(2)}) copy-start(s32[16]{0:T(128)} %refs_1_.7) | copy-start | bytes 196
  1.2 21.3 %copy-start.4 = (s32[16]{0:T(128)S(1)}, s32[16]{0:T(128)}, u32[]{:S(2)}) copy-start(s32[16]{0:T(128)} %refs_2_.7) | copy-start | bytes 196
  2.2 12.3 %collective-permute-start = (bf16[128,1024]{1,0:T(8,128)(2,1)S(1)}, bf16[128,1024]{1,0:T(8,128)(2,1)S(1)}, u32[]{:S(2)}, u32[]{:S(2)}) collective-permute-start(bf16[128,1024]{1,0:T(8,128)(2,1)S(1)} %constant_dynamic-slice_fusion), channel_id=1, source_target_pairs={{0,8},{4,12},{8,0},{12,4},{1,9},{5,13},{9,1},{13,5},{2,10},{6,14},... | collective-permute-start | bytes 786440 | tf_op jit(solution)/shard_map/ppermute | solution.py:378
  4.8 5.9 %collective-permute-start.2 = (bf16[4,128,128]{2,1,0:T(8,128)(2,1)}, bf16[4,128,128]{2,1,0:T(8,128)(2,1)S(1)}, u32[]{:S(2)}, u32[]{:S(2)}) collective-permute-start(bf16[4,128,128]{2,1,0:T(8,128)(2,1)} %refs_10_.1), channel_id=1, source_target_pairs={{0,4},{4,0},{8,12},{12,8},{1,5},{5,1},{9,13},{13,9},{2,6},{6,2},{1... | collective-permute-start | bytes 393224 | tf_op jit(solution)/shard_map/ppermute | solution.py:375
  5.0 9.6 %collective-permute-start.3 = (bf16[4,128,128]{2,1,0:T(8,128)(2,1)}, bf16[4,128,128]{2,1,0:T(8,128)(2,1)S(1)}, u32[]{:S(2)}, u32[]{:S(2)}) collective-permute-start(bf16[4,128,128]{2,1,0:T(8,128)(2,1)} %refs_10_.1), channel_id=1, source_target_pairs={{0,8},{4,12},{8,0},{12,4},{1,9},{5,13},{9,1},{13,5},{2,10},{6,14},... | collective-permute-start | bytes 393224 | tf_op jit(solution)/shard_map/ppermute | solution.py:378
  10.7 21.2 %copy-start.8 = (bf16[256,1024]{1,0:T(8,128)(2,1)S(1)}, bf16[256,1024]{1,0:T(8,128)(2,1)}, u32[]{:S(2)}) copy-start(bf16[256,1024]{1,0:T(8,128)(2,1)} %get-tuple-element.66) | copy-start | bytes 1572868
  10.7 25.1 %copy-start.6 = (f32[8,128,128]{2,1,0:T(8,128)S(1)}, f32[8,128,128]{2,1,0:T(8,128)}, u32[]{:S(2)}) copy-start(f32[8,128,128]{2,1,0:T(8,128)} %get-tuple-element.51) | copy-start | bytes 1572868
  14.6 4.9 %collective-permute-start.7 = (f32[8,128,128]{2,1,0:T(8,128)}, f32[8,128,128]{2,1,0:T(8,128)S(1)}, u32[]{:S(2)}, u32[]{:S(2)}) collective-permute-start(f32[8,128,128]{2,1,0:T(8,128)} %get-tuple-element.52), channel_id=1, source_target_pairs={{0,4},{4,0},{8,12},{12,8},{1,5},{5,1},{9,13},{13,9},{2,6},{6,2},{1... | collective-permute-start | bytes 1572872 | tf_op jit(solution)/shard_map/ppermute | solution.py:375
  14.6 12.8 %collective-permute-start.5 = (bf16[128,1024]{1,0:T(8,128)(2,1)S(1)}, bf16[128,1024]{1,0:T(8,128)(2,1)S(1)}, u32[]{:S(2)}, u32[]{:S(2)}) collective-permute-start(bf16[128,1024]{1,0:T(8,128)(2,1)S(1)} %collective-permute-done.refs_5_), channel_id=1, source_target_pairs={{0,16},{16,0},{1,17},{17,1},{2,18},{18,2},{3,19},{19,3},{4,20},{20... | collective-permute-start | bytes 786440 | tf_op jit(solution)/shard_map/ppermute | solution.py:381
  16.4 11.0 %collective-permute-start.6 = (bf16[128,1024]{1,0:T(8,128)(2,1)S(1)}, bf16[128,1024]{1,0:T(8,128)(2,1)S(1)}, u32[]{:S(2)}, u32[]{:S(2)}) collective-permute-start(bf16[128,1024]{1,0:T(8,128)(2,1)S(1)} %collective-permute-done.refs_5_), channel_id=1, source_target_pairs={{0,1},{1,0},{2,3},{3,2},{4,5},{5,4},{6,7},{7,6},{8,9},{9,8},{10,11... | collective-permute-start | bytes 786440 | tf_op jit(solution)/shard_map/ppermute | solution.py:384
  18.0 9.4 %collective-permute-start.4 = (bf16[128,1024]{1,0:T(8,128)(2,1)}, bf16[128,1024]{1,0:T(8,128)(2,1)S(1)}, u32[]{:S(2)}, u32[]{:S(2)}) collective-permute-start(bf16[128,1024]{1,0:T(8,128)(2,1)} %get-tuple-element.49), channel_id=1, source_target_pairs={{0,8},{4,12},{8,0},{12,4},{1,9},{5,13},{9,1},{13,5},{2,10},{6,14},... | collective-permute-start | bytes 786440 | tf_op jit(solution)/shard_map/ppermute | solution.py:378
  20.5 11.4 %collective-permute-start.8 = (f32[4,128,128]{2,1,0:T(8,128)S(1)}, f32[4,128,128]{2,1,0:T(8,128)S(1)}, u32[]{:S(2)}, u32[]{:S(2)}) collective-permute-start(f32[4,128,128]{2,1,0:T(8,128)S(1)} %slice_add_fusion.1), channel_id=1, source_target_pairs={{0,8},{4,12},{8,0},{12,4},{1,9},{5,13},{9,1},{13,5},{2,10},{6,14},... | collective-permute-start | bytes 786440 | tf_op jit(solution)/shard_map/ppermute | solution.py:378
  21.1 1.3 %collective-permute-start.9 = (bf16[4,128,128]{2,1,0:T(8,128)(2,1)S(1)}, bf16[4,128,128]{2,1,0:T(8,128)(2,1)S(1)}, u32[]{:S(2)}, u32[]{:S(2)}) collective-permute-start(bf16[4,128,128]{2,1,0:T(8,128)(2,1)S(1)} %collective-permute-done.3.refs_8_.refs_15_.refs_12_), channel_id=1, source_target_pairs={{0,4},{4,0},{8,12},{12,8},{1,5},{5,1},{9,13},{13,9},{2,6},{6,2},{1... | collective-permute-start | bytes 393224 | tf_op jit(solution)/shard_map/ppermute | solution.py:375
  31.9 14.1 %collective-permute-start.11 = (bf16[256,1024]{1,0:T(8,128)(2,1)S(1)}, bf16[256,1024]{1,0:T(8,128)(2,1)S(1)}, u32[]{:S(2)}, u32[]{:S(2)}) collective-permute-start(bf16[256,1024]{1,0:T(8,128)(2,1)S(1)} %copy-done.8), channel_id=1, source_target_pairs={{0,8},{4,12},{8,0},{12,4},{1,9},{5,13},{9,1},{13,5},{2,10},{6,14},... | collective-permute-start | bytes 1572872 | tf_op jit(solution)/shard_map/ppermute | solution.py:378
  33.4 10.0 %collective-permute-start.12 = (bf16[128,1024]{1,0:T(8,128)(2,1)S(1)}, bf16[128,1024]{1,0:T(8,128)(2,1)S(1)}, u32[]{:S(2)}, u32[]{:S(2)}) collective-permute-start(bf16[128,1024]{1,0:T(8,128)(2,1)S(1)} %collective-permute-done.4.refs_8_), channel_id=1, source_target_pairs={{0,16},{16,0},{1,17},{17,1},{2,18},{18,2},{3,19},{19,3},{4,20},{20... | collective-permute-start | bytes 786440 | tf_op jit(solution)/shard_map/ppermute | solution.py:381
  33.9 9.5 %collective-permute-start.13 = (bf16[128,1024]{1,0:T(8,128)(2,1)S(1)}, bf16[128,1024]{1,0:T(8,128)(2,1)S(1)}, u32[]{:S(2)}, u32[]{:S(2)}) collective-permute-start(bf16[128,1024]{1,0:T(8,128)(2,1)S(1)} %collective-permute-done.4.refs_8_), channel_id=1, source_target_pairs={{0,1},{1,0},{2,3},{3,2},{4,5},{5,4},{6,7},{7,6},{8,9},{9,8},{10,11... | collective-permute-start | bytes 786440 | tf_op jit(solution)/shard_map/ppermute | solution.py:384
  34.4 11.6 %collective-permute-start.14 = (bf16[128,1024]{1,0:T(8,128)(2,1)S(1)}, bf16[128,1024]{1,0:T(8,128)(2,1)S(1)}, u32[]{:S(2)}, u32[]{:S(2)}) collective-permute-start(bf16[128,1024]{1,0:T(8,128)(2,1)S(1)} %collective-permute-done.6.refs_7_), channel_id=1, source_target_pairs={{0,16},{16,0},{1,17},{17,1},{2,18},{18,2},{3,19},{19,3},{4,20},{20... | collective-permute-start | bytes 786440 | tf_op jit(solution)/shard_map/ppermute | solution.py:381
  36.0 7.4 %collective-permute-start.10 = (f32[2,128,128]{2,1,0:T(8,128)S(1)}, f32[2,128,128]{2,1,0:T(8,128)S(1)}, u32[]{:S(2)}, u32[]{:S(2)}) collective-permute-start(f32[2,128,128]{2,1,0:T(8,128)S(1)} %slice.26), channel_id=1, source_target_pairs={{0,1},{1,0},{2,3},{3,2},{4,5},{5,4},{6,7},{7,6},{8,9},{9,8},{10,11... | collective-permute-start | bytes 393224 | tf_op jit(solution)/shard_map/ppermute | solution.py:384
  46.0 4.2 %collective-permute-start.15 = (bf16[384,2048]{1,0:T(8,128)(2,1)S(1)}, bf16[384,2048]{1,0:T(8,128)(2,1)S(1)}, u32[]{:S(2)}, u32[]{:S(2)}) collective-permute-start(bf16[384,2048]{1,0:T(8,128)(2,1)S(1)} %get-tuple-element.74), channel_id=1, source_target_pairs={{0,4},{4,0},{8,12},{12,8},{1,5},{5,1},{9,13},{13,9},{2,6},{6,2},{1... | collective-permute-start | bytes 4718600 | tf_op jit(solution)/shard_map/ppermute | solution.py:375
  46.0 20.1 %collective-permute-start.16 = (bf16[384,1024]{1,0:T(8,128)(2,1)S(1)}, bf16[384,1024]{1,0:T(8,128)(2,1)}, u32[]{:S(2)}, u32[]{:S(2)}) collective-permute-start(bf16[384,1024]{1,0:T(8,128)(2,1)S(1)} %copy-done.7), channel_id=1, source_target_pairs={{0,8},{4,12},{8,0},{12,4},{1,9},{5,13},{9,1},{13,5},{2,10},{6,14},... | collective-permute-start | bytes 2359304 | tf_op jit(solution)/shard_map/ppermute | solution.py:378
  46.6 14.9 %collective-permute-start.17 = (bf16[256,1024]{1,0:T(8,128)(2,1)S(1)}, bf16[256,1024]{1,0:T(8,128)(2,1)S(1)}, u32[]{:S(2)}, u32[]{:S(2)}) collective-permute-start(bf16[256,1024]{1,0:T(8,128)(2,1)S(1)} %collective-permute-done.11.refs_12_), channel_id=1, source_target_pairs={{0,16},{16,0},{1,17},{17,1},{2,18},{18,2},{3,19},{19,3},{4,20},{20... | collective-permute-start | bytes 1572872 | tf_op jit(solution)/shard_map/ppermute | solution.py:381
  47.1 16.6 %collective-permute-start.18 = (bf16[256,1024]{1,0:T(8,128)(2,1)S(1)}, bf16[256,1024]{1,0:T(8,128)(2,1)}, u32[]{:S(2)}, u32[]{:S(2)}) collective-permute-start(bf16[256,1024]{1,0:T(8,128)(2,1)S(1)} %collective-permute-done.11.refs_12_), channel_id=1, source_target_pairs={{0,1},{1,0},{2,3},{3,2},{4,5},{5,4},{6,7},{7,6},{8,9},{9,8},{10,11... | collective-permute-start | bytes 1572872 | tf_op jit(solution)/shard_map/ppermute | solution.py:384
  47.5 14.0 %collective-permute-start.19 = (f32[2,128,128]{2,1,0:T(8,128)S(1)}, f32[2,128,128]{2,1,0:T(8,128)S(1)}, u32[]{:S(2)}, u32[]{:S(2)}) collective-permute-start(f32[2,128,128]{2,1,0:T(8,128)S(1)} %slice_add_fusion.2), channel_id=1, source_target_pairs={{0,2},{1,3},{2,0},{3,1},{4,6},{5,7},{6,4},{7,5},{8,10},{9,11},{10,... | collective-permute-start | bytes 393224 | tf_op jit(solution)/shard_map/ppermute | solution.py:384
  66.0 5.3 %collective-permute-start.23 = (bf16[384,1152]{1,0:T(8,128)(2,1)}, bf16[384,1152]{1,0:T(8,128)(2,1)S(1)}, u32[]{:S(2)}, u32[]{:S(2)}) collective-permute-start(bf16[384,1152]{1,0:T(8,128)(2,1)} %get-tuple-element.84), channel_id=1, source_target_pairs={{0,4},{4,0},{8,12},{12,8},{1,5},{5,1},{9,13},{13,9},{2,6},{6,2},{1... | collective-permute-start | bytes 2654216 | tf_op jit(solution)/shard_map/ppermute | solution.py:375
  66.0 5.3 %collective-permute-start.20 = (bf16[384,1024]{1,0:T(8,128)(2,1)}, bf16[384,1024]{1,0:T(8,128)(2,1)S(1)}, u32[]{:S(2)}, u32[]{:S(2)}) collective-permute-start(bf16[384,1024]{1,0:T(8,128)(2,1)} %collective-permute-done.16.refs_4_), channel_id=1, source_target_pairs={{0,4},{4,0},{8,12},{12,8},{1,5},{5,1},{9,13},{13,9},{2,6},{6,2},{1... | collective-permute-start | bytes 2359304 | tf_op jit(solution)/shard_map/ppermute | solution.py:375
  66.5 4.3 %collective-permute-start.21 = (bf16[256,1024]{1,0:T(8,128)(2,1)S(1)}, bf16[256,1024]{1,0:T(8,128)(2,1)}, u32[]{:S(2)}, u32[]{:S(2)}) collective-permute-start(bf16[256,1024]{1,0:T(8,128)(2,1)S(1)} %collective-permute-done.17.refs_5_), channel_id=1, source_target_pairs={{0,4},{4,0},{8,12},{12,8},{1,5},{5,1},{9,13},{13,9},{2,6},{6,2},{1... | collective-permute-start | bytes 1572872 | tf_op jit(solution)/shard_map/ppermute | solution.py:375
  66.5 4.5 %collective-permute-start.22 = (bf16[256,1024]{1,0:T(8,128)(2,1)}, bf16[256,1024]{1,0:T(8,128)(2,1)}, u32[]{:S(2)}, u32[]{:S(2)}) collective-permute-start(bf16[256,1024]{1,0:T(8,128)(2,1)} %collective-permute-done.18.refs_6_), channel_id=1, source_target_pairs={{0,4},{4,0},{8,12},{12,8},{1,5},{5,1},{9,13},{13,9},{2,6},{6,2},{1... | collective-permute-start | bytes 1572872 | tf_op jit(solution)/shard_map/ppermute | solution.py:375
  67.7 9.9 %collective-permute-start.24 = (f32[2,128,128]{2,1,0:T(8,128)}, f32[2,128,128]{2,1,0:T(8,128)}, u32[]{:S(2)}, u32[]{:S(2)}) collective-permute-start(f32[2,128,128]{2,1,0:T(8,128)} %add.33), channel_id=1, source_target_pairs={{0,1},{1,0},{2,3},{3,2},{4,5},{5,4},{6,7},{7,6},{8,9},{9,8},{10,11... | collective-permute-start | bytes 393224 | tf_op jit(solution)/shard_map/ppermute | solution.py:384
  (2 other events, 11.2 us)

commit v4 on v3

--- a/solution.py
+++ b/solution.py
@@ -463,9 +463,8 @@
         other_units=len(units1),
     )
 
-    x1, y0, z0, gx, s2, out, other1 = lax.optimization_barrier(
-        (x1, y0, z0, gx, s2, out, other1)
-    )
+    gx, s2, out, other1, x1 = lax.optimization_barrier((gx, s2, out, other1, x1))
+    y0, z0 = lax.optimization_barrier((y0, z0))
     x2 = over_x(s2)
     y1, z1, yd = over_y(x1), over_z(x1), over_y(z0)
     owned = keep[:local_slots] + gc[:local_slots] + gx

time: 79.4 us -> 77.2 us (0.972)
  waiting for transfers between devices: 24.8 us -> 17.8 us
  starting transfers between devices: 20.5 us -> 25.2 us
    ppermute x6, waiting for transfers between devices: 11 us -> 6.71 us  [over_x(): return lax.ppermute(a, 'fsdp', [(k, k ^ 2) for k in range(4)])]
    ppermute x6, starting transfers between devices: 7.22 us -> 9.47 us  [over_z(): return lax.ppermute(a, 'dp', [(k, k ^ step) for k in range(n_dp)])]
    ppermute x9, waiting for transfers between devices: 4.48 us -> 2.32 us  [over_core(): return lax.ppermute(a, 'fsdp', [(k, k ^ 1) for k in range(4)])]
    ppermute x6, starting transfers between devices: 7.16 us -> 8.74 us  [over_x(): return lax.ppermute(a, 'fsdp', [(k, k ^ 2) for k in range(4)])]
    ppermute x4, starting transfers between devices: 4.37 us -> 5.24 us  [over_y(): return lax.ppermute(a, 'group', [(k, k ^ 1) for k in range(2)])]
  transfers between devices with their start and end apart: 25 -> 25, of which waited for: 12 -> 12; matrix products, arithmetic and copies ran while one was open for 3% -> 4% of each run, Pallas kernels for 35% -> 35%
where the time goes in v4:
time: 77.2 us; the launch traced here: 76.8 us
  Pallas kernels  27.1 us (35%)
  starting transfers between devices  25.2 us (33%)
  waiting for transfers between devices  17.8 us (23%)
  other arithmetic  3.55 us (5%)
  local copies, waits for them, and re-layouts  2.28 us (3%)
  between operations  0.82 us (1%)
    pallas_call x4, Pallas kernels, rows_grad(): pl.pallas_call(functools.partial(rows_kernel, units, moves, tile, width /...  21.8 us
    ppermute x6, starting transfers between devices, over_z(): return lax.ppermute(a, 'dp', [(k, k ^ step) for k in range(n_dp)])  9.47 us
    ppermute x6, starting transfers between devices, over_x(): return lax.ppermute(a, 'fsdp', [(k, k ^ 2) for k in range(4)])  8.74 us
    ppermute x6, waiting for transfers between devices, over_z(): return lax.ppermute(a, 'dp', [(k, k ^ step) for k in range(n_dp)])  6.97 us
    ppermute x6, waiting for transfers between devices, over_x(): return lax.ppermute(a, 'fsdp', [(k, k ^ 2) for k in range(4)])  6.71 us
    pallas_call x1, Pallas kernels, block_grads(): pl.pallas_call(functools.partial(grad_kernel, place, len(shapes), cuts),...  5.36 us
    ppermute x4, starting transfers between devices, over_y(): return lax.ppermute(a, 'group', [(k, k ^ 1) for k in range(2)])  5.24 us
    ppermute x9, waiting for transfers between devices, over_core(): return lax.ppermute(a, 'fsdp', [(k, k ^ 1) for k in range(4)])  2.32 us
  transfers between devices with their start and end apart: 25, of which 12 were waited for; matrix products, arithmetic and copies ran while one was open for 4% of the time, Pallas kernels for 35%

profile of v4, /device:TPU:0, one launch (start us, length us, event | category | flops | bytes accessed | tf_op | source)
XLA Modules:
  0.0 76.8 jit_solution(16721792920919166848)
XLA Ops:
  0.6 0.5 collective-permute-start.1
  1.2 1.0 %constant_dynamic-slice_fusion = bf16[128,1024]{1,0:T(8,128)(2,1)S(1)} fusion(bf16[2048,1024]{1,0:T(8,128)(2,1)} %refs_5_.3, s32[]{:T(128)S(6)} %select_n.21), kind=kLoop, calls=%fused_computation.6 | loop fusion | bytes 524292 | tf_op jit(solution)/shard_map/dynamic_slice | solution.py:428
  2.2 2.6 %collective-permute-start = (bf16[128,1024]{1,0:T(8,128)(2,1)S(1)}, bf16[128,1024]{1,0:T(8,128)(2,1)S(1)}, u32[]{:S(2)}, u32[]{:S(2)}) collective-permute-start(bf16[128,1024]{1,0:T(8,128)(2,1)S(1)} %constant_dynamic-slice_fusion), channel_id=1, source_target_pairs={{0,8},{4,12},{8,0},{12,4},{1,9},{5,13},{9,1},{13,5},{2,10},{6,14},... | collective-permute-start | bytes 786440 | tf_op jit(solution)/shard_map/ppermute | solution.py:378
  5.4 5.4 %block_grads.1 = (f32[8,128,128]{2,1,0:T(8,128)}, f32[8,128,128]{2,1,0:T(8,128)}, bf16[128,1024]{1,0:T(8,128)(2,1)}, bf16[256,1024]{1,0:T(8,128)(2,1)}, bf16[384,1024]{1,0:T(8,128)(2,1)}) custom-call(s32[16]{0:T(128)} %refs_0_.9, s32[16]{0:T(128)} %refs_1_.7, s32[16]{0:T(128)} %refs_2_.7, bf16[384,8192]{1,0:T(8,128)(2,1)} %act_ref.1, ...), custom_call_target="tpu_custom_call" | custom-call | flops 1024 | bytes 1024 | tf_op jit(solution)/shard_map/block_grads/pallas_call | solution.py:98
  10.8 3.8 %collective-permute-done.3.refs_8_.refs_15_.refs_12_ = bf16[4,128,128]{2,1,0:T(8,128)(2,1)S(1)} collective-permute-done((bf16[4,128,128]{2,1,0:T(8,128)(2,1)}, bf16[4,128,128]{2,1,0:T(8,128)(2,1)S(1)}, u32[]{:S(2)}, u32[]{:S(2)}) %collective-permute-start.3) | collective-permute-done | bytes 131104 | tf_op jit(solution)/shard_map/ppermute | solution.py:378
  14.6 1.8 %collective-permute-start.7 = (bf16[128,1024]{1,0:T(8,128)(2,1)}, bf16[128,1024]{1,0:T(8,128)(2,1)S(1)}, u32[]{:S(2)}, u32[]{:S(2)}) collective-permute-start(bf16[128,1024]{1,0:T(8,128)(2,1)} %get-tuple-element.58), channel_id=1, source_target_pairs={{0,8},{4,12},{8,0},{12,4},{1,9},{5,13},{9,1},{13,5},{2,10},{6,14},... | collective-permute-start | bytes 786440 | tf_op jit(solution)/shard_map/ppermute | solution.py:378
  16.7 1.0 %slice_add_fusion.1 = f32[4,128,128]{2,1,0:T(8,128)S(1)} fusion(f32[8,128,128]{2,1,0:T(8,128)S(1)} %collective-permute-done.4, f32[8,128,128]{2,1,0:T(8,128)} %get-tuple-element.49), kind=kLoop, calls=%fused_computation.2 | loop fusion | flops 65536 | bytes 786432 | tf_op jit(solution)/shard_map/add | solution.py:442
  17.7 1.8 %collective-permute-start.5 = (f32[4,128,128]{2,1,0:T(8,128)S(1)}, f32[4,128,128]{2,1,0:T(8,128)S(1)}, u32[]{:S(2)}, u32[]{:S(2)}) collective-permute-start(f32[4,128,128]{2,1,0:T(8,128)S(1)} %slice_add_fusion.1), channel_id=1, source_target_pairs={{0,8},{4,12},{8,0},{12,4},{1,9},{5,13},{9,1},{13,5},{2,10},{6,14},... | collective-permute-start | bytes 786440 | tf_op jit(solution)/shard_map/ppermute | solution.py:378
  19.5 1.5 %collective-permute-start.12 = (bf16[128,1024]{1,0:T(8,128)(2,1)S(1)}, bf16[128,1024]{1,0:T(8,128)(2,1)S(1)}, u32[]{:S(2)}, u32[]{:S(2)}) collective-permute-start(bf16[128,1024]{1,0:T(8,128)(2,1)S(1)} %collective-permute-done.refs_5_), channel_id=1, source_target_pairs={{0,16},{16,0},{1,17},{17,1},{2,18},{18,2},{3,19},{19,3},{4,20},{20... | collective-permute-start | bytes 786440 | tf_op jit(solution)/shard_map/ppermute | solution.py:381
  21.0 1.6 %collective-permute-start.13 = (bf16[128,1024]{1,0:T(8,128)(2,1)S(1)}, bf16[128,1024]{1,0:T(8,128)(2,1)S(1)}, u32[]{:S(2)}, u32[]{:S(2)}) collective-permute-start(bf16[128,1024]{1,0:T(8,128)(2,1)S(1)} %collective-permute-done.refs_5_), channel_id=1, source_target_pairs={{0,1},{1,0},{2,3},{3,2},{4,5},{5,4},{6,7},{7,6},{8,9},{9,8},{10,11... | collective-permute-start | bytes 786440 | tf_op jit(solution)/shard_map/ppermute | solution.py:384
  22.6 4.9 %rows_grad.4 = (bf16[384,8192]{1,0:T(8,128)(2,1)}, bf16[384,2048]{1,0:T(8,128)(2,1)S(1)}) custom-call(s32[16]{0:T(128)S(1)} %copy-done.2, s32[16]{0:T(128)S(1)} %copy-done.3, s32[16]{0:T(128)S(1)} %copy-done.4, bf16[384,1024]{1,0:T(8,128)(2,1)S(1)} %copy-done, bf16[384,1024]{1,0:T(8,128)(2,1)S(1)} %collective-permute-done.1.refs_4_, ...), custom_call_target="tpu_custom_call" | custom-call | flops 1024 | bytes 1024 | tf_op jit(solution)/shard_map/rows_grad/pallas_call | solution.py:299
  27.5 1.6 %collective-permute-done.5 = f32[4,128,128]{2,1,0:T(8,128)S(1)} collective-permute-done((f32[4,128,128]{2,1,0:T(8,128)S(1)}, f32[4,128,128]{2,1,0:T(8,128)S(1)}, u32[]{:S(2)}, u32[]{:S(2)}) %collective-permute-start.5) | collective-permute-done | bytes 262176 | tf_op jit(solution)/shard_map/ppermute | solution.py:378
  29.1 1.7 %collective-permute-start.9 = (bf16[256,1024]{1,0:T(8,128)(2,1)S(1)}, bf16[256,1024]{1,0:T(8,128)(2,1)S(1)}, u32[]{:S(2)}, u32[]{:S(2)}) collective-permute-start(bf16[256,1024]{1,0:T(8,128)(2,1)S(1)} %copy-done.8), channel_id=1, source_target_pairs={{0,8},{4,12},{8,0},{12,4},{1,9},{5,13},{9,1},{13,5},{2,10},{6,14},... | collective-permute-start | bytes 1572872 | tf_op jit(solution)/shard_map/ppermute | solution.py:378
  30.9 1.5 %collective-permute-start.14 = (bf16[128,1024]{1,0:T(8,128)(2,1)S(1)}, bf16[128,1024]{1,0:T(8,128)(2,1)S(1)}, u32[]{:S(2)}, u32[]{:S(2)}) collective-permute-start(bf16[128,1024]{1,0:T(8,128)(2,1)S(1)} %collective-permute-done.13.refs_7_), channel_id=1, source_target_pairs={{0,16},{16,0},{1,17},{17,1},{2,18},{18,2},{3,19},{19,3},{4,20},{20... | collective-permute-start | bytes 786440 | tf_op jit(solution)/shard_map/ppermute | solution.py:381
  32.9 1.6 %collective-permute-start.11 = (bf16[128,1024]{1,0:T(8,128)(2,1)S(1)}, bf16[128,1024]{1,0:T(8,128)(2,1)S(1)}, u32[]{:S(2)}, u32[]{:S(2)}) collective-permute-start(bf16[128,1024]{1,0:T(8,128)(2,1)S(1)} %collective-permute-done.7.refs_8_), channel_id=1, source_target_pairs={{0,1},{1,0},{2,3},{3,2},{4,5},{5,4},{6,7},{7,6},{8,9},{9,8},{10,11... | collective-permute-start | bytes 786440 | tf_op jit(solution)/shard_map/ppermute | solution.py:384
  34.6 0.5 collective-permute-start.8
  35.1 4.6 %rows_grad.5 = (bf16[384,8192]{1,0:T(8,128)(2,1)}, bf16[384,2048]{1,0:T(8,128)(2,1)S(1)}) custom-call(s32[16]{0:T(128)S(1)} %copy-done.2, s32[16]{0:T(128)S(1)} %copy-done.3, s32[16]{0:T(128)S(1)} %copy-done.4, bf16[384,1024]{1,0:T(8,128)(2,1)S(1)} %copy-done, ...), custom_call_target="tpu_custom_call", output_to_operand_aliasing={{0}: (10, {}), {1}: (11, {})} | custom-call | flops 1024 | bytes 1024 | tf_op jit(solution)/shard_map/rows_grad/pallas_call | solution.py:299
  40.1 2.6 %collective-permute-done.8 = f32[2,128,128]{2,1,0:T(8,128)S(1)} collective-permute-done((f32[2,128,128]{2,1,0:T(8,128)S(1)}, f32[2,128,128]{2,1,0:T(8,128)S(1)}, u32[]{:S(2)}, u32[]{:S(2)}) %collective-permute-start.8) | collective-permute-done | bytes 131104 | tf_op jit(solution)/shard_map/ppermute | solution.py:384
  42.7 1.3 %collective-permute-done.10.refs_9_ = bf16[128,1024]{1,0:T(8,128)(2,1)S(1)} collective-permute-done((bf16[128,1024]{1,0:T(8,128)(2,1)S(1)}, bf16[128,1024]{1,0:T(8,128)(2,1)S(1)}, u32[]{:S(2)}, u32[]{:S(2)}) %collective-permute-start.10) | collective-permute-done | bytes 262176 | tf_op jit(solution)/shard_map/ppermute | solution.py:381
  44.5 1.7 %collective-permute-start.17 = (bf16[256,1024]{1,0:T(8,128)(2,1)S(1)}, bf16[256,1024]{1,0:T(8,128)(2,1)S(1)}, u32[]{:S(2)}, u32[]{:S(2)}) collective-permute-start(bf16[256,1024]{1,0:T(8,128)(2,1)S(1)} %collective-permute-done.9.refs_12_), channel_id=1, source_target_pairs={{0,16},{16,0},{1,17},{17,1},{2,18},{18,2},{3,19},{19,3},{4,20},{20... | collective-permute-start | bytes 1572872 | tf_op jit(solution)/shard_map/ppermute | solution.py:381
  46.2 1.6 %collective-permute-start.18 = (bf16[256,1024]{1,0:T(8,128)(2,1)S(1)}, bf16[256,1024]{1,0:T(8,128)(2,1)}, u32[]{:S(2)}, u32[]{:S(2)}) collective-permute-start(bf16[256,1024]{1,0:T(8,128)(2,1)S(1)} %collective-permute-done.9.refs_12_), channel_id=1, source_target_pairs={{0,1},{1,0},{2,3},{3,2},{4,5},{5,4},{6,7},{7,6},{8,9},{9,8},{10,11... | collective-permute-start | bytes 1572872 | tf_op jit(solution)/shard_map/ppermute | solution.py:384
  47.8 2.7 %collective-permute-start.19 = (f32[2,128,128]{2,1,0:T(8,128)S(1)}, f32[2,128,128]{2,1,0:T(8,128)S(1)}, u32[]{:S(2)}, u32[]{:S(2)}) collective-permute-start(f32[2,128,128]{2,1,0:T(8,128)S(1)} %slice_add_fusion.2), channel_id=1, source_target_pairs={{0,2},{1,3},{2,0},{3,1},{4,6},{5,7},{6,4},{7,5},{8,10},{9,11},{10,... | collective-permute-start | bytes 393224 | tf_op jit(solution)/shard_map/ppermute | solution.py:384
  50.5 1.2 %copy-done.5 = bf16[384,2048]{1,0:T(8,128)(2,1)} copy-done((bf16[384,2048]{1,0:T(8,128)(2,1)}, bf16[384,2048]{1,0:T(8,128)(2,1)S(1)}, u32[]{:S(2)}) %copy-start.5) | copy-done | bytes 1572888
  51.7 6.8 %rows_grad.6 = (bf16[384,8192]{1,0:T(8,128)(2,1)}, bf16[384,1152]{1,0:T(8,128)(2,1)}) custom-call(s32[16]{0:T(128)S(1)} %copy-done.2, s32[16]{0:T(128)S(1)} %copy-done.3, s32[16]{0:T(128)S(1)} %copy-done.4, bf16[384,1024]{1,0:T(8,128)(2,1)S(1)} %copy-done, bf16[384,1024]{1,0:T(8,128)(2,1)S(1)} %collective-permute-done.1.refs_4_, ...), custom_call_target="tpu_custom_call", output_to_operand_aliasing={{0}: (18, {})} | custom-call | flops 1024 | bytes 1024 | tf_op jit(solution)/shard_map/rows_grad/pallas_call | solution.py:299
  58.5 3.3 %collective-permute-done.19 = f32[2,128,128]{2,1,0:T(8,128)S(1)} collective-permute-done((f32[2,128,128]{2,1,0:T(8,128)S(1)}, f32[2,128,128]{2,1,0:T(8,128)S(1)}, u32[]{:S(2)}, u32[]{:S(2)}) %collective-permute-start.19) | collective-permute-done | bytes 131104 | tf_op jit(solution)/shard_map/ppermute | solution.py:384
  61.8 1.0 %collective-permute-done.18.refs_6_ = bf16[256,1024]{1,0:T(8,128)(2,1)} collective-permute-done((bf16[256,1024]{1,0:T(8,128)(2,1)S(1)}, bf16[256,1024]{1,0:T(8,128)(2,1)}, u32[]{:S(2)}, u32[]{:S(2)}) %collective-permute-start.18) | collective-permute-done | bytes 524320 | tf_op jit(solution)/shard_map/ppermute | solution.py:384
  62.8 1.3 %collective-permute-done.16.refs_4_ = bf16[384,1024]{1,0:T(8,128)(2,1)} collective-permute-done((bf16[384,1024]{1,0:T(8,128)(2,1)S(1)}, bf16[384,1024]{1,0:T(8,128)(2,1)}, u32[]{:S(2)}, u32[]{:S(2)}) %collective-permute-start.16) | collective-permute-done | bytes 786464 | tf_op jit(solution)/shard_map/ppermute | solution.py:378
  65.2 0.7 add.33
  65.8 1.6 %collective-permute-start.24 = (f32[2,128,128]{2,1,0:T(8,128)}, f32[2,128,128]{2,1,0:T(8,128)}, u32[]{:S(2)}, u32[]{:S(2)}) collective-permute-start(f32[2,128,128]{2,1,0:T(8,128)} %add.33), channel_id=1, source_target_pairs={{0,1},{1,0},{2,3},{3,2},{4,5},{5,4},{6,7},{7,6},{8,9},{9,8},{10,11... | collective-permute-start | bytes 393224 | tf_op jit(solution)/shard_map/ppermute | solution.py:384
  67.4 1.5 %collective-permute-done.21.refs_8_ = bf16[256,1024]{1,0:T(8,128)(2,1)} collective-permute-done((bf16[256,1024]{1,0:T(8,128)(2,1)S(1)}, bf16[256,1024]{1,0:T(8,128)(2,1)}, u32[]{:S(2)}, u32[]{:S(2)}) %collective-permute-start.21) | collective-permute-done | bytes 524320 | tf_op jit(solution)/shard_map/ppermute | solution.py:375
  69.4 5.5 %rows_grad.7 = bf16[384,8192]{1,0:T(8,128)(2,1)} custom-call(s32[16]{0:T(128)S(1)} %copy-done.2, s32[16]{0:T(128)S(1)} %copy-done.3, s32[16]{0:T(128)S(1)} %copy-done.4, bf16[384,1024]{1,0:T(8,128)(2,1)S(1)} %copy-done, bf16[384,1024]{1,0:T(8,128)(2,1)} %collective-permute-done.16.refs_4_, ...), custom_call_target="tpu_custom_call", output_to_operand_aliasing={{}: (15, {})} | custom-call | flops 1024 | bytes 1024 | tf_op jit(solution)/shard_map/rows_grad/pallas_call | solution.py:299
  74.9 1.8 %fusion.1 = f32[4,128,128]{2,1,0:T(8,128)} fusion(f32[2,128,128]{2,1,0:T(8,128)} %collective-permute-done.24, f32[2,128,128]{2,1,0:T(8,128)} %add.33, pred[]{:T(512)S(6)} %eq.6), kind=kLoop, calls=%fused_computation.4 | loop fusion | flops 262144 | bytes 524289 | tf_op jit(solution)/shard_map/mul | solution.py:500
  (48 shorter events, 3.8 us)
Async XLA Ops:
  0.6 13.9 %collective-permute-start.1 = (bf16[384,1024]{1,0:T(8,128)(2,1)}, bf16[384,1024]{1,0:T(8,128)(2,1)S(1)}, u32[]{:S(2)}, u32[]{:S(2)}) collective-permute-start(bf16[384,1024]{1,0:T(8,128)(2,1)} %refs_3_.7), channel_id=1, source_target_pairs={{0,4},{4,0},{8,12},{12,8},{1,5},{5,1},{9,13},{13,9},{2,6},{6,2},{1... | collective-permute-start | bytes 2359304 | tf_op jit(solution)/shard_map/ppermute | solution.py:375
  1.1 21.5 %copy-start = (bf16[384,1024]{1,0:T(8,128)(2,1)S(1)}, bf16[384,1024]{1,0:T(8,128)(2,1)}, u32[]{:S(2)}) copy-start(bf16[384,1024]{1,0:T(8,128)(2,1)} %refs_3_.7) | copy-start | bytes 2359300
  1.1 21.5 %copy-start.1 = (bf16[4,128,128]{2,1,0:T(8,128)(2,1)S(1)}, bf16[4,128,128]{2,1,0:T(8,128)(2,1)}, u32[]{:S(2)}) copy-start(bf16[4,128,128]{2,1,0:T(8,128)(2,1)} %refs_10_.1) | copy-start | bytes 393220
  1.2 21.5 %copy-start.2 = (s32[16]{0:T(128)S(1)}, s32[16]{0:T(128)}, u32[]{:S(2)}) copy-start(s32[16]{0:T(128)} %refs_0_.9) | copy-start | bytes 196
  1.2 21.5 %copy-start.3 = (s32[16]{0:T(128)S(1)}, s32[16]{0:T(128)}, u32[]{:S(2)}) copy-start(s32[16]{0:T(128)} %refs_1_.7) | copy-start | bytes 196
  1.2 21.5 %copy-start.4 = (s32[16]{0:T(128)S(1)}, s32[16]{0:T(128)}, u32[]{:S(2)}) copy-start(s32[16]{0:T(128)} %refs_2_.7) | copy-start | bytes 196
  2.2 12.3 %collective-permute-start = (bf16[128,1024]{1,0:T(8,128)(2,1)S(1)}, bf16[128,1024]{1,0:T(8,128)(2,1)S(1)}, u32[]{:S(2)}, u32[]{:S(2)}) collective-permute-start(bf16[128,1024]{1,0:T(8,128)(2,1)S(1)} %constant_dynamic-slice_fusion), channel_id=1, source_target_pairs={{0,8},{4,12},{8,0},{12,4},{1,9},{5,13},{9,1},{13,5},{2,10},{6,14},... | collective-permute-start | bytes 786440 | tf_op jit(solution)/shard_map/ppermute | solution.py:378
  4.8 5.9 %collective-permute-start.2 = (bf16[4,128,128]{2,1,0:T(8,128)(2,1)}, bf16[4,128,128]{2,1,0:T(8,128)(2,1)S(1)}, u32[]{:S(2)}, u32[]{:S(2)}) collective-permute-start(bf16[4,128,128]{2,1,0:T(8,128)(2,1)} %refs_10_.1), channel_id=1, source_target_pairs={{0,4},{4,0},{8,12},{12,8},{1,5},{5,1},{9,13},{13,9},{2,6},{6,2},{1... | collective-permute-start | bytes 393224 | tf_op jit(solution)/shard_map/ppermute | solution.py:375
  5.0 9.6 %collective-permute-start.3 = (bf16[4,128,128]{2,1,0:T(8,128)(2,1)}, bf16[4,128,128]{2,1,0:T(8,128)(2,1)S(1)}, u32[]{:S(2)}, u32[]{:S(2)}) collective-permute-start(bf16[4,128,128]{2,1,0:T(8,128)(2,1)} %refs_10_.1), channel_id=1, source_target_pairs={{0,8},{4,12},{8,0},{12,4},{1,9},{5,13},{9,1},{13,5},{2,10},{6,14},... | collective-permute-start | bytes 393224 | tf_op jit(solution)/shard_map/ppermute | solution.py:378
  10.7 18.4 %copy-start.8 = (bf16[256,1024]{1,0:T(8,128)(2,1)S(1)}, bf16[256,1024]{1,0:T(8,128)(2,1)}, u32[]{:S(2)}) copy-start(bf16[256,1024]{1,0:T(8,128)(2,1)} %get-tuple-element.66) | copy-start | bytes 1572868
  10.7 23.7 %copy-start.6 = (f32[8,128,128]{2,1,0:T(8,128)S(1)}, f32[8,128,128]{2,1,0:T(8,128)}, u32[]{:S(2)}) copy-start(f32[8,128,128]{2,1,0:T(8,128)} %get-tuple-element.49) | copy-start | bytes 1572868
  14.6 2.1 %collective-permute-start.4 = (f32[8,128,128]{2,1,0:T(8,128)}, f32[8,128,128]{2,1,0:T(8,128)S(1)}, u32[]{:S(2)}, u32[]{:S(2)}) collective-permute-start(f32[8,128,128]{2,1,0:T(8,128)} %get-tuple-element.50), channel_id=1, source_target_pairs={{0,4},{4,0},{8,12},{12,8},{1,5},{5,1},{9,13},{13,9},{2,6},{6,2},{1... | collective-permute-start | bytes 1572872 | tf_op jit(solution)/shard_map/ppermute | solution.py:375
  14.6 12.9 %collective-permute-start.7 = (bf16[128,1024]{1,0:T(8,128)(2,1)}, bf16[128,1024]{1,0:T(8,128)(2,1)S(1)}, u32[]{:S(2)}, u32[]{:S(2)}) collective-permute-start(bf16[128,1024]{1,0:T(8,128)(2,1)} %get-tuple-element.58), channel_id=1, source_target_pairs={{0,8},{4,12},{8,0},{12,4},{1,9},{5,13},{9,1},{13,5},{2,10},{6,14},... | collective-permute-start | bytes 786440 | tf_op jit(solution)/shard_map/ppermute | solution.py:378
  17.7 11.4 %collective-permute-start.5 = (f32[4,128,128]{2,1,0:T(8,128)S(1)}, f32[4,128,128]{2,1,0:T(8,128)S(1)}, u32[]{:S(2)}, u32[]{:S(2)}) collective-permute-start(f32[4,128,128]{2,1,0:T(8,128)S(1)} %slice_add_fusion.1), channel_id=1, source_target_pairs={{0,8},{4,12},{8,0},{12,4},{1,9},{5,13},{9,1},{13,5},{2,10},{6,14},... | collective-permute-start | bytes 786440 | tf_op jit(solution)/shard_map/ppermute | solution.py:378
  19.5 3.1 %collective-permute-start.6 = (bf16[4,128,128]{2,1,0:T(8,128)(2,1)S(1)}, bf16[4,128,128]{2,1,0:T(8,128)(2,1)S(1)}, u32[]{:S(2)}, u32[]{:S(2)}) collective-permute-start(bf16[4,128,128]{2,1,0:T(8,128)(2,1)S(1)} %collective-permute-done.3.refs_8_.refs_15_.refs_12_), channel_id=1, source_target_pairs={{0,4},{4,0},{8,12},{12,8},{1,5},{5,1},{9,13},{13,9},{2,6},{6,2},{1... | collective-permute-start | bytes 393224 | tf_op jit(solution)/shard_map/ppermute | solution.py:375
  19.5 11.4 %collective-permute-start.12 = (bf16[128,1024]{1,0:T(8,128)(2,1)S(1)}, bf16[128,1024]{1,0:T(8,128)(2,1)S(1)}, u32[]{:S(2)}, u32[]{:S(2)}) collective-permute-start(bf16[128,1024]{1,0:T(8,128)(2,1)S(1)} %collective-permute-done.refs_5_), channel_id=1, source_target_pairs={{0,16},{16,0},{1,17},{17,1},{2,18},{18,2},{3,19},{19,3},{4,20},{20... | collective-permute-start | bytes 786440 | tf_op jit(solution)/shard_map/ppermute | solution.py:381
  21.0 9.9 %collective-permute-start.13 = (bf16[128,1024]{1,0:T(8,128)(2,1)S(1)}, bf16[128,1024]{1,0:T(8,128)(2,1)S(1)}, u32[]{:S(2)}, u32[]{:S(2)}) collective-permute-start(bf16[128,1024]{1,0:T(8,128)(2,1)S(1)} %collective-permute-done.refs_5_), channel_id=1, source_target_pairs={{0,1},{1,0},{2,3},{3,2},{4,5},{5,4},{6,7},{7,6},{8,9},{9,8},{10,11... | collective-permute-start | bytes 786440 | tf_op jit(solution)/shard_map/ppermute | solution.py:384
  29.1 15.0 %collective-permute-start.9 = (bf16[256,1024]{1,0:T(8,128)(2,1)S(1)}, bf16[256,1024]{1,0:T(8,128)(2,1)S(1)}, u32[]{:S(2)}, u32[]{:S(2)}) collective-permute-start(bf16[256,1024]{1,0:T(8,128)(2,1)S(1)} %copy-done.8), channel_id=1, source_target_pairs={{0,8},{4,12},{8,0},{12,4},{1,9},{5,13},{9,1},{13,5},{2,10},{6,14},... | collective-permute-start | bytes 1572872 | tf_op jit(solution)/shard_map/ppermute | solution.py:378
  30.9 9.2 %collective-permute-start.14 = (bf16[128,1024]{1,0:T(8,128)(2,1)S(1)}, bf16[128,1024]{1,0:T(8,128)(2,1)S(1)}, u32[]{:S(2)}, u32[]{:S(2)}) collective-permute-start(bf16[128,1024]{1,0:T(8,128)(2,1)S(1)} %collective-permute-done.13.refs_7_), channel_id=1, source_target_pairs={{0,16},{16,0},{1,17},{17,1},{2,18},{18,2},{3,19},{19,3},{4,20},{20... | collective-permute-start | bytes 786440 | tf_op jit(solution)/shard_map/ppermute | solution.py:381
  32.4 11.7 %collective-permute-start.10 = (bf16[128,1024]{1,0:T(8,128)(2,1)S(1)}, bf16[128,1024]{1,0:T(8,128)(2,1)S(1)}, u32[]{:S(2)}, u32[]{:S(2)}) collective-permute-start(bf16[128,1024]{1,0:T(8,128)(2,1)S(1)} %collective-permute-done.7.refs_8_), channel_id=1, source_target_pairs={{0,16},{16,0},{1,17},{17,1},{2,18},{18,2},{3,19},{19,3},{4,20},{20... | collective-permute-start | bytes 786440 | tf_op jit(solution)/shard_map/ppermute | solution.py:381
  32.9 11.2 %collective-permute-start.11 = (bf16[128,1024]{1,0:T(8,128)(2,1)S(1)}, bf16[128,1024]{1,0:T(8,128)(2,1)S(1)}, u32[]{:S(2)}, u32[]{:S(2)}) collective-permute-start(bf16[128,1024]{1,0:T(8,128)(2,1)S(1)} %collective-permute-done.7.refs_8_), channel_id=1, source_target_pairs={{0,1},{1,0},{2,3},{3,2},{4,5},{5,4},{6,7},{7,6},{8,9},{9,8},{10,11... | collective-permute-start | bytes 786440 | tf_op jit(solution)/shard_map/ppermute | solution.py:384
  34.6 8.2 %collective-permute-start.8 = (f32[2,128,128]{2,1,0:T(8,128)S(1)}, f32[2,128,128]{2,1,0:T(8,128)S(1)}, u32[]{:S(2)}, u32[]{:S(2)}) collective-permute-start(f32[2,128,128]{2,1,0:T(8,128)S(1)} %slice.26), channel_id=1, source_target_pairs={{0,1},{1,0},{2,3},{3,2},{4,5},{5,4},{6,7},{7,6},{8,9},{9,8},{10,11... | collective-permute-start | bytes 393224 | tf_op jit(solution)/shard_map/ppermute | solution.py:384
  44.1 6.4 %collective-permute-start.15 = (bf16[384,2048]{1,0:T(8,128)(2,1)S(1)}, bf16[384,2048]{1,0:T(8,128)(2,1)S(1)}, u32[]{:S(2)}, u32[]{:S(2)}) collective-permute-start(bf16[384,2048]{1,0:T(8,128)(2,1)S(1)} %get-tuple-element.74), channel_id=1, source_target_pairs={{0,4},{4,0},{8,12},{12,8},{1,5},{5,1},{9,13},{13,9},{2,6},{6,2},{1... | collective-permute-start | bytes 4718600 | tf_op jit(solution)/shard_map/ppermute | solution.py:375
  44.1 20.1 %collective-permute-start.16 = (bf16[384,1024]{1,0:T(8,128)(2,1)S(1)}, bf16[384,1024]{1,0:T(8,128)(2,1)}, u32[]{:S(2)}, u32[]{:S(2)}) collective-permute-start(bf16[384,1024]{1,0:T(8,128)(2,1)S(1)} %copy-done.7), channel_id=1, source_target_pairs={{0,8},{4,12},{8,0},{12,4},{1,9},{5,13},{9,1},{13,5},{2,10},{6,14},... | collective-permute-start | bytes 2359304 | tf_op jit(solution)/shard_map/ppermute | solution.py:378
  44.5 17.3 %collective-permute-start.17 = (bf16[256,1024]{1,0:T(8,128)(2,1)S(1)}, bf16[256,1024]{1,0:T(8,128)(2,1)S(1)}, u32[]{:S(2)}, u32[]{:S(2)}) collective-permute-start(bf16[256,1024]{1,0:T(8,128)(2,1)S(1)} %collective-permute-done.9.refs_12_), channel_id=1, source_target_pairs={{0,16},{16,0},{1,17},{17,1},{2,18},{18,2},{3,19},{19,3},{4,20},{20... | collective-permute-start | bytes 1572872 | tf_op jit(solution)/shard_map/ppermute | solution.py:381
  46.2 16.6 %collective-permute-start.18 = (bf16[256,1024]{1,0:T(8,128)(2,1)S(1)}, bf16[256,1024]{1,0:T(8,128)(2,1)}, u32[]{:S(2)}, u32[]{:S(2)}) collective-permute-start(bf16[256,1024]{1,0:T(8,128)(2,1)S(1)} %collective-permute-done.9.refs_12_), channel_id=1, source_target_pairs={{0,1},{1,0},{2,3},{3,2},{4,5},{5,4},{6,7},{7,6},{8,9},{9,8},{10,11... | collective-permute-start | bytes 1572872 | tf_op jit(solution)/shard_map/ppermute | solution.py:384
  47.8 14.0 %collective-permute-start.19 = (f32[2,128,128]{2,1,0:T(8,128)S(1)}, f32[2,128,128]{2,1,0:T(8,128)S(1)}, u32[]{:S(2)}, u32[]{:S(2)}) collective-permute-start(f32[2,128,128]{2,1,0:T(8,128)S(1)} %slice_add_fusion.2), channel_id=1, source_target_pairs={{0,2},{1,3},{2,0},{3,1},{4,6},{5,7},{6,4},{7,5},{8,10},{9,11},{10,... | collective-permute-start | bytes 393224 | tf_op jit(solution)/shard_map/ppermute | solution.py:384
  64.2 5.3 %collective-permute-start.23 = (bf16[384,1152]{1,0:T(8,128)(2,1)}, bf16[384,1152]{1,0:T(8,128)(2,1)S(1)}, u32[]{:S(2)}, u32[]{:S(2)}) collective-permute-start(bf16[384,1152]{1,0:T(8,128)(2,1)} %get-tuple-element.84), channel_id=1, source_target_pairs={{0,4},{4,0},{8,12},{12,8},{1,5},{5,1},{9,13},{13,9},{2,6},{6,2},{1... | collective-permute-start | bytes 2654216 | tf_op jit(solution)/shard_map/ppermute | solution.py:375
  64.2 5.3 %collective-permute-start.20 = (bf16[384,1024]{1,0:T(8,128)(2,1)}, bf16[384,1024]{1,0:T(8,128)(2,1)S(1)}, u32[]{:S(2)}, u32[]{:S(2)}) collective-permute-start(bf16[384,1024]{1,0:T(8,128)(2,1)} %collective-permute-done.16.refs_4_), channel_id=1, source_target_pairs={{0,4},{4,0},{8,12},{12,8},{1,5},{5,1},{9,13},{13,9},{2,6},{6,2},{1... | collective-permute-start | bytes 2359304 | tf_op jit(solution)/shard_map/ppermute | solution.py:375
  64.7 4.3 %collective-permute-start.21 = (bf16[256,1024]{1,0:T(8,128)(2,1)S(1)}, bf16[256,1024]{1,0:T(8,128)(2,1)}, u32[]{:S(2)}, u32[]{:S(2)}) collective-permute-start(bf16[256,1024]{1,0:T(8,128)(2,1)S(1)} %collective-permute-done.17.refs_5_), channel_id=1, source_target_pairs={{0,4},{4,0},{8,12},{12,8},{1,5},{5,1},{9,13},{13,9},{2,6},{6,2},{1... | collective-permute-start | bytes 1572872 | tf_op jit(solution)/shard_map/ppermute | solution.py:375
  64.7 4.5 %collective-permute-start.22 = (bf16[256,1024]{1,0:T(8,128)(2,1)}, bf16[256,1024]{1,0:T(8,128)(2,1)}, u32[]{:S(2)}, u32[]{:S(2)}) collective-permute-start(bf16[256,1024]{1,0:T(8,128)(2,1)} %collective-permute-done.18.refs_6_), channel_id=1, source_target_pairs={{0,4},{4,0},{8,12},{12,8},{1,5},{5,1},{9,13},{13,9},{2,6},{6,2},{1... | collective-permute-start | bytes 1572872 | tf_op jit(solution)/shard_map/ppermute | solution.py:375
  65.8 9.1 %collective-permute-start.24 = (f32[2,128,128]{2,1,0:T(8,128)}, f32[2,128,128]{2,1,0:T(8,128)}, u32[]{:S(2)}, u32[]{:S(2)}) collective-permute-start(f32[2,128,128]{2,1,0:T(8,128)} %add.33), channel_id=1, source_target_pairs={{0,1},{1,0},{2,3},{3,2},{4,5},{5,4},{6,7},{7,6},{8,9},{9,8},{10,11... | collective-permute-start | bytes 393224 | tf_op jit(solution)/shard_map/ppermute | solution.py:384
  (2 other events, 10.7 us)

commit v5 on v4

--- a/solution.py
+++ b/solution.py
@@ -434,9 +434,7 @@
         [(row_of(0, 1), sizes[1]), (row_of(0, 2), sizes[2]), (row_of(3, 1), sizes[1] + sizes[2])],
     )
 
-    x0, send, up_sib, s1, s2, dc, dx = lax.optimization_barrier(
-        (x0, send, up_sib, s1, s2, dc, dx)
-    )
+    x0, send, up_sib, s1, s2, dc = lax.optimization_barrier((x0, send, up_sib, s1, s2, dc))
     y0, z0, x1 = over_y(x0), over_z(x0), over_x(s1)
     gc = over_core(send)
     gx = over_x(keep[local_slots:] + gc[local_slots:])
@@ -446,9 +444,9 @@
 
     def multiply(pieces, ups, out, at=(), moved=(), units=None, **other):
         moves = [
-            (m, first, column)
+            (m, u * BLOCK, column)
             for m, there in enumerate(at)
-            for _, first, column in moves_of(there)
+            for u, (_, _, column) in enumerate(sum([moves_of(p) for p in there], []))
         ]
         return rows_grad(
             units or units_of(pieces), [p[0] for p in pieces], *pattern, ups, all_deltas, delta_at,
@@ -458,9 +456,9 @@
     pieces1 = [(frozen, 0, None, 0)]
     units1 = units_of(pieces1)
     first_half = len(units1) // 2
+    n_1 = len(units1) + (2 * sizes[0] + sizes[0] + sizes[1]) // BLOCK
     out, other1 = multiply(
-        pieces1, [upstream, after(up_sib, x0)], None, units=units1[:first_half],
-        other_units=len(units1),
+        pieces1, [upstream, after(up_sib, x0)], None, units=units1[:first_half], other_units=n_1
     )
 
     gx, s2, out, other1, x1 = lax.optimization_barrier((gx, s2, out, other1, x1))
@@ -471,7 +469,12 @@
     gz = over_z(owned[half:])
     out, other1 = multiply(
         pieces1, [upstream, after(up_sib, x1)], out, units=units1[first_half:],
-        other=other1, other_units=len(units1), other_first=first_half * BLOCK,
+        other=other1, other_units=n_1, other_first=first_half * BLOCK,
+    )
+    pieces2 = [(x0, 2, 0, offs[0]), (y0, 2, 2, offs[0]), (z0, 2, 1, offs[0]), (x1, 2, 0, offs[1])]
+    out, other1 = multiply(
+        pieces2, [upstream, after(up_sib, x1)], out,
+        other=other1, other_units=n_1, other_first=len(units1) * BLOCK,
     )
 
     out, other1, gz, x2, y1, z1, yd = lax.optimization_barrier(
@@ -482,11 +485,12 @@
     mine = owned[:half] + gz
     gz2 = over_z(mine, 2)
     o1 = over_core(other1)
-    pieces2 = [
-        (x0, 2, 0, offs[0]), (y0, 2, 2, offs[0]), (z0, 2, 1, offs[0]), (x1, 2, 0, offs[1]),
+    pieces3 = [
         (y1, 2, 2, offs[1]), (z1, 2, 1, offs[1]), (yd, 2, 3, offs[0]), (x2, 2, 0, offs[2]),
     ]
-    out, other2 = multiply(pieces2, [upstream, after(up_sib, x2)], out, [pieces1], [o1])
+    out, other2 = multiply(
+        pieces3, [upstream, after(up_sib, x2)], out, [[pieces1, pieces2]], [o1]
+    )
 
     out, other2, x3, y2, z2, gz2 = lax.optimization_barrier((out, other2, x3, y2, z2, gz2))
     mine = mine + gz2
@@ -494,7 +498,7 @@
     o2 = over_core(other2)
     last = [(x3, 2, 3, offs[1]), (y2, 2, 2, offs[2]), (z2, 2, 1, offs[2])]
     last = last + [(over_core(a), 3, cell, at) for a, _, cell, at in last]
-    (out,) = multiply(last, [upstream], out, [pieces2], [o2])
+    (out,) = multiply(last, [upstream], out, [[pieces3]], [o2])
     other_half = after(other_half, out)
     normalizer = 1.0 / math.sqrt(upstream.shape[0] * lax.axis_size("fsdp") * n_dp)
     totals = jnp.where(

time: 77.2 us -> 76.3 us (0.988)
  Pallas kernels: 27.1 us -> 29.8 us
  waiting for transfers between devices: 17.8 us -> 15.8 us
  local copies, waits for them, and re-layouts: 2.28 us -> 1.09 us
    pallas_call x4 -> x5, Pallas kernels: 21.8 us -> 24.5 us  [rows_grad(): pl.pallas_call(functools.partial(rows_kernel, units, moves, tile, width /...]
    ppermute x4, waiting for transfers between devices: 1.8 us -> 0.01 us  [over_y(): return lax.ppermute(a, 'group', [(k, k ^ 1) for k in range(2)])]
    ppermute x6, waiting for transfers between devices: 6.97 us -> 5.49 us  [over_z(): return lax.ppermute(a, 'dp', [(k, k ^ step) for k in range(n_dp)])]
    ppermute x6, waiting for transfers between devices: 6.71 us -> 8.14 us  [over_x(): return lax.ppermute(a, 'fsdp', [(k, k ^ 2) for k in range(4)])]
    unnamed x18 -> x16, local copies, waits for them, and re-layouts: 1.22 us -> 0.03 us
  transfers between devices with their start and end apart: 25 -> 25, of which waited for: 12 -> 7; matrix products, arithmetic and copies ran while one was open for 4% -> 3% of each run, Pallas kernels for 35% -> 39%
where the time goes in v5:
time: 76.3 us; the launch traced here: 76.1 us
  Pallas kernels  29.8 us (39%)
  starting transfers between devices  25.7 us (34%)
  waiting for transfers between devices  15.8 us (21%)
  other arithmetic  2.79 us (4%)
  local copies, waits for them, and re-layouts  1.09 us (1%)
  between operations  0.86 us (1%)
    pallas_call x5, Pallas kernels, rows_grad(): pl.pallas_call(functools.partial(rows_kernel, units, moves, tile, width /...  24.5 us
    ppermute x6, starting transfers between devices, over_z(): return lax.ppermute(a, 'dp', [(k, k ^ step) for k in range(n_dp)])  10 us
    ppermute x6, starting transfers between devices, over_x(): return lax.ppermute(a, 'fsdp', [(k, k ^ 2) for k in range(4)])  8.55 us
    ppermute x6, waiting for transfers between devices, over_x(): return lax.ppermute(a, 'fsdp', [(k, k ^ 2) for k in range(4)])  8.14 us
    ppermute x6, waiting for transfers between devices, over_z(): return lax.ppermute(a, 'dp', [(k, k ^ step) for k in range(n_dp)])  5.49 us
    pallas_call x1, Pallas kernels, block_grads(): pl.pallas_call(functools.partial(grad_kernel, place, len(shapes), cuts),...  5.35 us
    ppermute x4, starting transfers between devices, over_y(): return lax.ppermute(a, 'group', [(k, k ^ 1) for k in range(2)])  5.34 us
    ppermute x9, waiting for transfers between devices, over_core(): return lax.ppermute(a, 'fsdp', [(k, k ^ 1) for k in range(4)])  2.15 us
  transfers between devices with their start and end apart: 25, of which 7 were waited for; matrix products, arithmetic and copies ran while one was open for 3% of the time, Pallas kernels for 39%

profile of v5, /device:TPU:0, one launch (start us, length us, event | category | flops | bytes accessed | tf_op | source)
XLA Modules:
  0.0 76.1 jit_solution(6557346944427134148)
XLA Ops:
  0.6 0.5 collective-permute-start.1
  1.2 1.0 %constant_dynamic-slice_fusion = bf16[128,1024]{1,0:T(8,128)(2,1)S(1)} fusion(bf16[2048,1024]{1,0:T(8,128)(2,1)} %refs_5_.3, s32[]{:T(128)S(6)} %select_n.21), kind=kLoop, calls=%fused_computation.6 | loop fusion | bytes 524292 | tf_op jit(solution)/shard_map/dynamic_slice | solution.py:428
  2.2 2.6 %collective-permute-start = (bf16[128,1024]{1,0:T(8,128)(2,1)S(1)}, bf16[128,1024]{1,0:T(8,128)(2,1)S(1)}, u32[]{:S(2)}, u32[]{:S(2)}) collective-permute-start(bf16[128,1024]{1,0:T(8,128)(2,1)S(1)} %constant_dynamic-slice_fusion), channel_id=1, source_target_pairs={{0,8},{4,12},{8,0},{12,4},{1,9},{5,13},{9,1},{13,5},{2,10},{6,14},... | collective-permute-start | bytes 786440 | tf_op jit(solution)/shard_map/ppermute | solution.py:378
  5.0 5.3 %block_grads.1 = (f32[8,128,128]{2,1,0:T(8,128)}, f32[8,128,128]{2,1,0:T(8,128)}, bf16[128,1024]{1,0:T(8,128)(2,1)}, bf16[256,1024]{1,0:T(8,128)(2,1)}, bf16[384,1024]{1,0:T(8,128)(2,1)}) custom-call(s32[16]{0:T(128)} %refs_0_.11, s32[16]{0:T(128)} %refs_1_.9, s32[16]{0:T(128)} %refs_2_.9, bf16[384,8192]{1,0:T(8,128)(2,1)} %act_ref.1, ...), custom_call_target="tpu_custom_call" | custom-call | flops 1024 | bytes 1024 | tf_op jit(solution)/shard_map/block_grads/pallas_call | solution.py:98
  10.4 1.4 %collective-permute-done.refs_5_ = bf16[128,1024]{1,0:T(8,128)(2,1)S(1)} collective-permute-done((bf16[128,1024]{1,0:T(8,128)(2,1)S(1)}, bf16[128,1024]{1,0:T(8,128)(2,1)S(1)}, u32[]{:S(2)}, u32[]{:S(2)}) %collective-permute-start) | collective-permute-done | bytes 262176 | tf_op jit(solution)/shard_map/ppermute | solution.py:378
  11.8 1.8 %collective-permute-start.5 = (bf16[4,128,128]{2,1,0:T(8,128)(2,1)S(1)}, bf16[4,128,128]{2,1,0:T(8,128)(2,1)S(1)}, u32[]{:S(2)}, u32[]{:S(2)}) collective-permute-start(bf16[4,128,128]{2,1,0:T(8,128)(2,1)S(1)} %copy-done.1), channel_id=1, source_target_pairs={{0,8},{4,12},{8,0},{12,4},{1,9},{5,13},{9,1},{13,5},{2,10},{6,14},... | collective-permute-start | bytes 393224 | tf_op jit(solution)/shard_map/ppermute | solution.py:378
  13.9 1.0 %slice_add_fusion.1 = f32[4,128,128]{2,1,0:T(8,128)S(1)} fusion(f32[8,128,128]{2,1,0:T(8,128)S(1)} %collective-permute-done.3, f32[8,128,128]{2,1,0:T(8,128)} %get-tuple-element.50), kind=kLoop, calls=%fused_computation.2 | loop fusion | flops 65536 | bytes 786432 | tf_op jit(solution)/shard_map/add | solution.py:440
  14.9 1.8 %collective-permute-start.4 = (f32[4,128,128]{2,1,0:T(8,128)S(1)}, f32[4,128,128]{2,1,0:T(8,128)S(1)}, u32[]{:S(2)}, u32[]{:S(2)}) collective-permute-start(f32[4,128,128]{2,1,0:T(8,128)S(1)} %slice_add_fusion.1), channel_id=1, source_target_pairs={{0,8},{4,12},{8,0},{12,4},{1,9},{5,13},{9,1},{13,5},{2,10},{6,14},... | collective-permute-start | bytes 786440 | tf_op jit(solution)/shard_map/ppermute | solution.py:378
  16.7 1.5 %collective-permute-done.5.refs_8_.refs_11_.refs_12_ = bf16[4,128,128]{2,1,0:T(8,128)(2,1)S(1)} collective-permute-done((bf16[4,128,128]{2,1,0:T(8,128)(2,1)S(1)}, bf16[4,128,128]{2,1,0:T(8,128)(2,1)S(1)}, u32[]{:S(2)}, u32[]{:S(2)}) %collective-permute-start.5) | collective-permute-done | bytes 131104 | tf_op jit(solution)/shard_map/ppermute | solution.py:378
  18.1 1.8 %collective-permute-start.9 = (bf16[128,1024]{1,0:T(8,128)(2,1)S(1)}, bf16[128,1024]{1,0:T(8,128)(2,1)S(1)}, u32[]{:S(2)}, u32[]{:S(2)}) collective-permute-start(bf16[128,1024]{1,0:T(8,128)(2,1)S(1)} %collective-permute-done.refs_5_), channel_id=1, source_target_pairs={{0,1},{1,0},{2,3},{3,2},{4,5},{5,4},{6,7},{7,6},{8,9},{9,8},{10,11... | collective-permute-start | bytes 786440 | tf_op jit(solution)/shard_map/ppermute | solution.py:384
  20.0 1.5 %collective-permute-start.8 = (bf16[128,1024]{1,0:T(8,128)(2,1)S(1)}, bf16[128,1024]{1,0:T(8,128)(2,1)S(1)}, u32[]{:S(2)}, u32[]{:S(2)}) collective-permute-start(bf16[128,1024]{1,0:T(8,128)(2,1)S(1)} %collective-permute-done.refs_5_), channel_id=1, source_target_pairs={{0,16},{16,0},{1,17},{17,1},{2,18},{18,2},{3,19},{19,3},{4,20},{20... | collective-permute-start | bytes 786440 | tf_op jit(solution)/shard_map/ppermute | solution.py:381
  21.5 4.8 %rows_grad.5 = (bf16[384,8192]{1,0:T(8,128)(2,1)}, bf16[384,2560]{1,0:T(8,128)(2,1)S(1)}) custom-call(s32[16]{0:T(128)S(1)} %copy-done.2, s32[16]{0:T(128)S(1)} %copy-done.3, s32[16]{0:T(128)S(1)} %copy-done.4, bf16[384,1024]{1,0:T(8,128)(2,1)S(1)} %copy-done, bf16[384,1024]{1,0:T(8,128)(2,1)S(1)} %collective-permute-done.1.refs_4_, ...), custom_call_target="tpu_custom_call" | custom-call | flops 1024 | bytes 1024 | tf_op jit(solution)/shard_map/rows_grad/pallas_call | solution.py:299
  26.4 2.6 %collective-permute-done.4 = f32[4,128,128]{2,1,0:T(8,128)S(1)} collective-permute-done((f32[4,128,128]{2,1,0:T(8,128)S(1)}, f32[4,128,128]{2,1,0:T(8,128)S(1)}, u32[]{:S(2)}, u32[]{:S(2)}) %collective-permute-start.4) | collective-permute-done | bytes 262176 | tf_op jit(solution)/shard_map/ppermute | solution.py:378
  28.9 1.7 %collective-permute-start.11 = (bf16[256,1024]{1,0:T(8,128)(2,1)S(1)}, bf16[256,1024]{1,0:T(8,128)(2,1)S(1)}, u32[]{:S(2)}, u32[]{:S(2)}) collective-permute-start(bf16[256,1024]{1,0:T(8,128)(2,1)S(1)} %copy-done.7), channel_id=1, source_target_pairs={{0,8},{4,12},{8,0},{12,4},{1,9},{5,13},{9,1},{13,5},{2,10},{6,14},... | collective-permute-start | bytes 1572872 | tf_op jit(solution)/shard_map/ppermute | solution.py:378
  30.7 1.5 %collective-permute-start.14 = (bf16[128,1024]{1,0:T(8,128)(2,1)S(1)}, bf16[128,1024]{1,0:T(8,128)(2,1)S(1)}, u32[]{:S(2)}, u32[]{:S(2)}) collective-permute-start(bf16[128,1024]{1,0:T(8,128)(2,1)S(1)} %collective-permute-done.9.refs_7_), channel_id=1, source_target_pairs={{0,16},{16,0},{1,17},{17,1},{2,18},{18,2},{3,19},{19,3},{4,20},{20... | collective-permute-start | bytes 786440 | tf_op jit(solution)/shard_map/ppermute | solution.py:381
  32.2 1.6 %collective-permute-start.13 = (bf16[128,1024]{1,0:T(8,128)(2,1)S(1)}, bf16[128,1024]{1,0:T(8,128)(2,1)S(1)}, u32[]{:S(2)}, u32[]{:S(2)}) collective-permute-start(bf16[128,1024]{1,0:T(8,128)(2,1)S(1)} %collective-permute-done.7.refs_8_), channel_id=1, source_target_pairs={{0,1},{1,0},{2,3},{3,2},{4,5},{5,4},{6,7},{7,6},{8,9},{9,8},{10,11... | collective-permute-start | bytes 786440 | tf_op jit(solution)/shard_map/ppermute | solution.py:384
  34.3 0.5 collective-permute-start.10
  34.8 5.4 %rows_grad.6 = (bf16[384,8192]{1,0:T(8,128)(2,1)}, bf16[384,2560]{1,0:T(8,128)(2,1)S(1)}) custom-call(s32[16]{0:T(128)S(1)} %copy-done.2, s32[16]{0:T(128)S(1)} %copy-done.3, s32[16]{0:T(128)S(1)} %copy-done.4, bf16[384,1024]{1,0:T(8,128)(2,1)S(1)} %copy-done, ...), custom_call_target="tpu_custom_call", output_to_operand_aliasing={{0}: (10, {}), {1}: (11, {})} | custom-call | flops 1024 | bytes 1024 | tf_op jit(solution)/shard_map/rows_grad/pallas_call | solution.py:299
  40.3 3.6 %rows_grad.7 = (bf16[384,8192]{1,0:T(8,128)(2,1)}, bf16[384,2560]{1,0:T(8,128)(2,1)S(1)}) custom-call(s32[16]{0:T(128)S(1)} %copy-done.2, s32[16]{0:T(128)S(1)} %copy-done.3, s32[16]{0:T(128)S(1)} %copy-done.4, bf16[384,1024]{1,0:T(8,128)(2,1)S(1)} %copy-done, ...), custom_call_target="tpu_custom_call", output_to_operand_aliasing={{0}: (13, {}), {1}: (14, {})} | custom-call | flops 1024 | bytes 1024 | tf_op jit(solution)/shard_map/rows_grad/pallas_call | solution.py:299
  44.3 1.8 %collective-permute-start.18 = (bf16[256,1024]{1,0:T(8,128)(2,1)S(1)}, bf16[256,1024]{1,0:T(8,128)(2,1)S(1)}, u32[]{:S(2)}, u32[]{:S(2)}) collective-permute-start(bf16[256,1024]{1,0:T(8,128)(2,1)S(1)} %collective-permute-done.11.refs_8_), channel_id=1, source_target_pairs={{0,1},{1,0},{2,3},{3,2},{4,5},{5,4},{6,7},{7,6},{8,9},{9,8},{10,11... | collective-permute-start | bytes 1572872 | tf_op jit(solution)/shard_map/ppermute | solution.py:384
  46.1 1.8 %collective-permute-start.17 = (bf16[256,1024]{1,0:T(8,128)(2,1)S(1)}, bf16[256,1024]{1,0:T(8,128)(2,1)}, u32[]{:S(2)}, u32[]{:S(2)}) collective-permute-start(bf16[256,1024]{1,0:T(8,128)(2,1)S(1)} %collective-permute-done.11.refs_8_), channel_id=1, source_target_pairs={{0,16},{16,0},{1,17},{17,1},{2,18},{18,2},{3,19},{19,3},{4,20},{20... | collective-permute-start | bytes 1572872 | tf_op jit(solution)/shard_map/ppermute | solution.py:381
  47.9 2.7 %collective-permute-start.19 = (f32[2,128,128]{2,1,0:T(8,128)S(1)}, f32[2,128,128]{2,1,0:T(8,128)S(1)}, u32[]{:S(2)}, u32[]{:S(2)}) collective-permute-start(f32[2,128,128]{2,1,0:T(8,128)S(1)} %slice_add_fusion.2), channel_id=1, source_target_pairs={{0,2},{1,3},{2,0},{3,1},{4,6},{5,7},{6,4},{7,5},{8,10},{9,11},{10,... | collective-permute-start | bytes 393224 | tf_op jit(solution)/shard_map/ppermute | solution.py:384
  50.6 5.1 %rows_grad.8 = (bf16[384,8192]{1,0:T(8,128)(2,1)}, bf16[384,640]{1,0:T(8,128)(2,1)}) custom-call(s32[16]{0:T(128)S(1)} %copy-done.2, s32[16]{0:T(128)S(1)} %copy-done.3, s32[16]{0:T(128)S(1)} %copy-done.4, bf16[384,1024]{1,0:T(8,128)(2,1)S(1)} %copy-done, bf16[384,1024]{1,0:T(8,128)(2,1)S(1)} %collective-permute-done.1.refs_4_, ...), custom_call_target="tpu_custom_call", output_to_operand_aliasing={{0}: (14, {})} | custom-call | flops 1024 | bytes 1024 | tf_op jit(solution)/shard_map/rows_grad/pallas_call | solution.py:299
  55.7 4.7 %collective-permute-done.19 = f32[2,128,128]{2,1,0:T(8,128)S(1)} collective-permute-done((f32[2,128,128]{2,1,0:T(8,128)S(1)}, f32[2,128,128]{2,1,0:T(8,128)S(1)}, u32[]{:S(2)}, u32[]{:S(2)}) %collective-permute-start.19) | collective-permute-done | bytes 131104 | tf_op jit(solution)/shard_map/ppermute | solution.py:384
  60.4 0.7 collective-permute-done.18.refs_6_
  61.2 2.8 %collective-permute-done.16.refs_4_ = bf16[384,1024]{1,0:T(8,128)(2,1)S(1)} collective-permute-done((bf16[384,1024]{1,0:T(8,128)(2,1)S(1)}, bf16[384,1024]{1,0:T(8,128)(2,1)S(1)}, u32[]{:S(2)}, u32[]{:S(2)}) %collective-permute-start.16) | collective-permute-done | bytes 786464 | tf_op jit(solution)/shard_map/ppermute | solution.py:378
  63.9 0.5 collective-permute-start.21
  64.5 0.5 collective-permute-start.23
  65.0 1.6 %collective-permute-start.24 = (f32[2,128,128]{2,1,0:T(8,128)S(1)}, f32[2,128,128]{2,1,0:T(8,128)}, u32[]{:S(2)}, u32[]{:S(2)}) collective-permute-start(f32[2,128,128]{2,1,0:T(8,128)S(1)} %add.33), channel_id=1, source_target_pairs={{0,1},{1,0},{2,3},{3,2},{4,5},{5,4},{6,7},{7,6},{8,9},{9,8},{10,11... | collective-permute-start | bytes 393224 | tf_op jit(solution)/shard_map/ppermute | solution.py:384
  66.6 2.1 %collective-permute-done.23.refs_14_ = bf16[384,640]{1,0:T(8,128)(2,1)} collective-permute-done((bf16[384,640]{1,0:T(8,128)(2,1)}, bf16[384,640]{1,0:T(8,128)(2,1)}, u32[]{:S(2)}, u32[]{:S(2)}) %collective-permute-start.23) | collective-permute-done | bytes 491552 | tf_op jit(solution)/shard_map/ppermute | solution.py:375
  68.7 5.6 %rows_grad.9 = bf16[384,8192]{1,0:T(8,128)(2,1)} custom-call(s32[16]{0:T(128)S(1)} %copy-done.2, s32[16]{0:T(128)S(1)} %copy-done.3, s32[16]{0:T(128)S(1)} %copy-done.4, bf16[384,1024]{1,0:T(8,128)(2,1)S(1)} %copy-done, bf16[384,1024]{1,0:T(8,128)(2,1)S(1)} %collective-permute-done.16.refs_4_, ...), custom_call_target="tpu_custom_call", output_to_operand_aliasing={{}: (15, {})} | custom-call | flops 1024 | bytes 1024 | tf_op jit(solution)/shard_map/rows_grad/pallas_call | solution.py:299
  74.3 1.7 %fusion.1 = f32[4,128,128]{2,1,0:T(8,128)} fusion(f32[2,128,128]{2,1,0:T(8,128)} %collective-permute-done.24, f32[2,128,128]{2,1,0:T(8,128)S(1)} %add.33, pred[]{:T(512)S(6)} %eq.6), kind=kLoop, calls=%fused_computation.4 | loop fusion | flops 262144 | bytes 524289 | tf_op jit(solution)/shard_map/mul | solution.py:504
  (47 shorter events, 1.5 us)
Async XLA Ops:
  0.6 11.1 %copy-start.1 = (bf16[4,128,128]{2,1,0:T(8,128)(2,1)S(1)}, bf16[4,128,128]{2,1,0:T(8,128)(2,1)}, u32[]{:S(2)}) copy-start(bf16[4,128,128]{2,1,0:T(8,128)(2,1)} %refs_10_.1) | copy-start | bytes 393220
  0.6 11.1 %collective-permute-start.1 = (bf16[384,1024]{1,0:T(8,128)(2,1)}, bf16[384,1024]{1,0:T(8,128)(2,1)S(1)}, u32[]{:S(2)}, u32[]{:S(2)}) collective-permute-start(bf16[384,1024]{1,0:T(8,128)(2,1)} %refs_3_.9), channel_id=1, source_target_pairs={{0,4},{4,0},{8,12},{12,8},{1,5},{5,1},{9,13},{13,9},{2,6},{6,2},{1... | collective-permute-start | bytes 2359304 | tf_op jit(solution)/shard_map/ppermute | solution.py:375
  1.2 20.3 %copy-start = (bf16[384,1024]{1,0:T(8,128)(2,1)S(1)}, bf16[384,1024]{1,0:T(8,128)(2,1)}, u32[]{:S(2)}) copy-start(bf16[384,1024]{1,0:T(8,128)(2,1)} %refs_3_.9) | copy-start | bytes 2359300
  1.2 20.3 %copy-start.2 = (s32[16]{0:T(128)S(1)}, s32[16]{0:T(128)}, u32[]{:S(2)}) copy-start(s32[16]{0:T(128)} %refs_0_.11) | copy-start | bytes 196
  1.2 20.3 %copy-start.3 = (s32[16]{0:T(128)S(1)}, s32[16]{0:T(128)}, u32[]{:S(2)}) copy-start(s32[16]{0:T(128)} %refs_1_.9) | copy-start | bytes 196
  1.2 20.3 %copy-start.4 = (s32[16]{0:T(128)S(1)}, s32[16]{0:T(128)}, u32[]{:S(2)}) copy-start(s32[16]{0:T(128)} %refs_2_.9) | copy-start | bytes 196
  2.2 9.5 %collective-permute-start = (bf16[128,1024]{1,0:T(8,128)(2,1)S(1)}, bf16[128,1024]{1,0:T(8,128)(2,1)S(1)}, u32[]{:S(2)}, u32[]{:S(2)}) collective-permute-start(bf16[128,1024]{1,0:T(8,128)(2,1)S(1)} %constant_dynamic-slice_fusion), channel_id=1, source_target_pairs={{0,8},{4,12},{8,0},{12,4},{1,9},{5,13},{9,1},{13,5},{2,10},{6,14},... | collective-permute-start | bytes 786440 | tf_op jit(solution)/shard_map/ppermute | solution.py:378
  4.8 5.5 %collective-permute-start.2 = (bf16[4,128,128]{2,1,0:T(8,128)(2,1)}, bf16[4,128,128]{2,1,0:T(8,128)(2,1)S(1)}, u32[]{:S(2)}, u32[]{:S(2)}) collective-permute-start(bf16[4,128,128]{2,1,0:T(8,128)(2,1)} %refs_10_.1), channel_id=1, source_target_pairs={{0,4},{4,0},{8,12},{12,8},{1,5},{5,1},{9,13},{13,9},{2,6},{6,2},{1... | collective-permute-start | bytes 393224 | tf_op jit(solution)/shard_map/ppermute | solution.py:375
  10.4 18.6 %copy-start.7 = (bf16[256,1024]{1,0:T(8,128)(2,1)S(1)}, bf16[256,1024]{1,0:T(8,128)(2,1)}, u32[]{:S(2)}) copy-start(bf16[256,1024]{1,0:T(8,128)(2,1)} %get-tuple-element.70) | copy-start | bytes 1572868
  10.4 23.9 %copy-start.5 = (f32[8,128,128]{2,1,0:T(8,128)S(1)}, f32[8,128,128]{2,1,0:T(8,128)}, u32[]{:S(2)}) copy-start(f32[8,128,128]{2,1,0:T(8,128)} %get-tuple-element.50) | copy-start | bytes 1572868
  11.8 2.1 %collective-permute-start.3 = (f32[8,128,128]{2,1,0:T(8,128)}, f32[8,128,128]{2,1,0:T(8,128)S(1)}, u32[]{:S(2)}, u32[]{:S(2)}) collective-permute-start(f32[8,128,128]{2,1,0:T(8,128)} %get-tuple-element.51), channel_id=1, source_target_pairs={{0,4},{4,0},{8,12},{12,8},{1,5},{5,1},{9,13},{13,9},{2,6},{6,2},{1... | collective-permute-start | bytes 1572872 | tf_op jit(solution)/shard_map/ppermute | solution.py:375
  11.8 6.4 %collective-permute-start.5 = (bf16[4,128,128]{2,1,0:T(8,128)(2,1)S(1)}, bf16[4,128,128]{2,1,0:T(8,128)(2,1)S(1)}, u32[]{:S(2)}, u32[]{:S(2)}) collective-permute-start(bf16[4,128,128]{2,1,0:T(8,128)(2,1)S(1)} %copy-done.1), channel_id=1, source_target_pairs={{0,8},{4,12},{8,0},{12,4},{1,9},{5,13},{9,1},{13,5},{2,10},{6,14},... | collective-permute-start | bytes 393224 | tf_op jit(solution)/shard_map/ppermute | solution.py:378
  13.6 12.8 %collective-permute-start.7 = (bf16[128,1024]{1,0:T(8,128)(2,1)}, bf16[128,1024]{1,0:T(8,128)(2,1)S(1)}, u32[]{:S(2)}, u32[]{:S(2)}) collective-permute-start(bf16[128,1024]{1,0:T(8,128)(2,1)} %get-tuple-element.58), channel_id=1, source_target_pairs={{0,8},{4,12},{8,0},{12,4},{1,9},{5,13},{9,1},{13,5},{2,10},{6,14},... | collective-permute-start | bytes 786440 | tf_op jit(solution)/shard_map/ppermute | solution.py:378
  14.9 14.0 %collective-permute-start.4 = (f32[4,128,128]{2,1,0:T(8,128)S(1)}, f32[4,128,128]{2,1,0:T(8,128)S(1)}, u32[]{:S(2)}, u32[]{:S(2)}) collective-permute-start(f32[4,128,128]{2,1,0:T(8,128)S(1)} %slice_add_fusion.1), channel_id=1, source_target_pairs={{0,8},{4,12},{8,0},{12,4},{1,9},{5,13},{9,1},{13,5},{2,10},{6,14},... | collective-permute-start | bytes 786440 | tf_op jit(solution)/shard_map/ppermute | solution.py:378
  18.1 3.4 %collective-permute-start.6 = (bf16[4,128,128]{2,1,0:T(8,128)(2,1)S(1)}, bf16[4,128,128]{2,1,0:T(8,128)(2,1)S(1)}, u32[]{:S(2)}, u32[]{:S(2)}) collective-permute-start(bf16[4,128,128]{2,1,0:T(8,128)(2,1)S(1)} %collective-permute-done.5.refs_8_.refs_11_.refs_12_), channel_id=1, source_target_pairs={{0,4},{4,0},{8,12},{12,8},{1,5},{5,1},{9,13},{13,9},{2,6},{6,2},{1... | collective-permute-start | bytes 393224 | tf_op jit(solution)/shard_map/ppermute | solution.py:375
  18.1 12.5 %collective-permute-start.9 = (bf16[128,1024]{1,0:T(8,128)(2,1)S(1)}, bf16[128,1024]{1,0:T(8,128)(2,1)S(1)}, u32[]{:S(2)}, u32[]{:S(2)}) collective-permute-start(bf16[128,1024]{1,0:T(8,128)(2,1)S(1)} %collective-permute-done.refs_5_), channel_id=1, source_target_pairs={{0,1},{1,0},{2,3},{3,2},{4,5},{5,4},{6,7},{7,6},{8,9},{9,8},{10,11... | collective-permute-start | bytes 786440 | tf_op jit(solution)/shard_map/ppermute | solution.py:384
  20.0 10.7 %collective-permute-start.8 = (bf16[128,1024]{1,0:T(8,128)(2,1)S(1)}, bf16[128,1024]{1,0:T(8,128)(2,1)S(1)}, u32[]{:S(2)}, u32[]{:S(2)}) collective-permute-start(bf16[128,1024]{1,0:T(8,128)(2,1)S(1)} %collective-permute-done.refs_5_), channel_id=1, source_target_pairs={{0,16},{16,0},{1,17},{17,1},{2,18},{18,2},{3,19},{19,3},{4,20},{20... | collective-permute-start | bytes 786440 | tf_op jit(solution)/shard_map/ppermute | solution.py:381
  28.9 15.0 %collective-permute-start.11 = (bf16[256,1024]{1,0:T(8,128)(2,1)S(1)}, bf16[256,1024]{1,0:T(8,128)(2,1)S(1)}, u32[]{:S(2)}, u32[]{:S(2)}) collective-permute-start(bf16[256,1024]{1,0:T(8,128)(2,1)S(1)} %copy-done.7), channel_id=1, source_target_pairs={{0,8},{4,12},{8,0},{12,4},{1,9},{5,13},{9,1},{13,5},{2,10},{6,14},... | collective-permute-start | bytes 1572872 | tf_op jit(solution)/shard_map/ppermute | solution.py:378
  30.7 13.2 %collective-permute-start.14 = (bf16[128,1024]{1,0:T(8,128)(2,1)S(1)}, bf16[128,1024]{1,0:T(8,128)(2,1)S(1)}, u32[]{:S(2)}, u32[]{:S(2)}) collective-permute-start(bf16[128,1024]{1,0:T(8,128)(2,1)S(1)} %collective-permute-done.9.refs_7_), channel_id=1, source_target_pairs={{0,16},{16,0},{1,17},{17,1},{2,18},{18,2},{3,19},{19,3},{4,20},{20... | collective-permute-start | bytes 786440 | tf_op jit(solution)/shard_map/ppermute | solution.py:381
  32.2 11.7 %collective-permute-start.13 = (bf16[128,1024]{1,0:T(8,128)(2,1)S(1)}, bf16[128,1024]{1,0:T(8,128)(2,1)S(1)}, u32[]{:S(2)}, u32[]{:S(2)}) collective-permute-start(bf16[128,1024]{1,0:T(8,128)(2,1)S(1)} %collective-permute-done.7.refs_8_), channel_id=1, source_target_pairs={{0,1},{1,0},{2,3},{3,2},{4,5},{5,4},{6,7},{7,6},{8,9},{9,8},{10,11... | collective-permute-start | bytes 786440 | tf_op jit(solution)/shard_map/ppermute | solution.py:384
  33.8 10.1 %collective-permute-start.12 = (bf16[128,1024]{1,0:T(8,128)(2,1)S(1)}, bf16[128,1024]{1,0:T(8,128)(2,1)S(1)}, u32[]{:S(2)}, u32[]{:S(2)}) collective-permute-start(bf16[128,1024]{1,0:T(8,128)(2,1)S(1)} %collective-permute-done.7.refs_8_), channel_id=1, source_target_pairs={{0,16},{16,0},{1,17},{17,1},{2,18},{18,2},{3,19},{19,3},{4,20},{20... | collective-permute-start | bytes 786440 | tf_op jit(solution)/shard_map/ppermute | solution.py:381
  34.3 9.5 %collective-permute-start.10 = (f32[2,128,128]{2,1,0:T(8,128)S(1)}, f32[2,128,128]{2,1,0:T(8,128)S(1)}, u32[]{:S(2)}, u32[]{:S(2)}) collective-permute-start(f32[2,128,128]{2,1,0:T(8,128)S(1)} %slice.26), channel_id=1, source_target_pairs={{0,1},{1,0},{2,3},{3,2},{4,5},{5,4},{6,7},{7,6},{8,9},{9,8},{10,11... | collective-permute-start | bytes 393224 | tf_op jit(solution)/shard_map/ppermute | solution.py:384
  43.9 6.7 %collective-permute-start.15 = (bf16[384,2560]{1,0:T(8,128)(2,1)S(1)}, bf16[384,2560]{1,0:T(8,128)(2,1)S(1)}, u32[]{:S(2)}, u32[]{:S(2)}) collective-permute-start(bf16[384,2560]{1,0:T(8,128)(2,1)S(1)} %get-tuple-element.76), channel_id=1, source_target_pairs={{0,4},{4,0},{8,12},{12,8},{1,5},{5,1},{9,13},{13,9},{2,6},{6,2},{1... | collective-permute-start | bytes 5898248 | tf_op jit(solution)/shard_map/ppermute | solution.py:375
  44.0 19.9 %collective-permute-start.16 = (bf16[384,1024]{1,0:T(8,128)(2,1)S(1)}, bf16[384,1024]{1,0:T(8,128)(2,1)S(1)}, u32[]{:S(2)}, u32[]{:S(2)}) collective-permute-start(bf16[384,1024]{1,0:T(8,128)(2,1)S(1)} %copy-done.6), channel_id=1, source_target_pairs={{0,8},{4,12},{8,0},{12,4},{1,9},{5,13},{9,1},{13,5},{2,10},{6,14},... | collective-permute-start | bytes 2359304 | tf_op jit(solution)/shard_map/ppermute | solution.py:378
  44.3 16.9 %collective-permute-start.18 = (bf16[256,1024]{1,0:T(8,128)(2,1)S(1)}, bf16[256,1024]{1,0:T(8,128)(2,1)S(1)}, u32[]{:S(2)}, u32[]{:S(2)}) collective-permute-start(bf16[256,1024]{1,0:T(8,128)(2,1)S(1)} %collective-permute-done.11.refs_8_), channel_id=1, source_target_pairs={{0,1},{1,0},{2,3},{3,2},{4,5},{5,4},{6,7},{7,6},{8,9},{9,8},{10,11... | collective-permute-start | bytes 1572872 | tf_op jit(solution)/shard_map/ppermute | solution.py:384
  46.1 15.1 %collective-permute-start.17 = (bf16[256,1024]{1,0:T(8,128)(2,1)S(1)}, bf16[256,1024]{1,0:T(8,128)(2,1)}, u32[]{:S(2)}, u32[]{:S(2)}) collective-permute-start(bf16[256,1024]{1,0:T(8,128)(2,1)S(1)} %collective-permute-done.11.refs_8_), channel_id=1, source_target_pairs={{0,16},{16,0},{1,17},{17,1},{2,18},{18,2},{3,19},{19,3},{4,20},{20... | collective-permute-start | bytes 1572872 | tf_op jit(solution)/shard_map/ppermute | solution.py:381
  47.9 12.5 %collective-permute-start.19 = (f32[2,128,128]{2,1,0:T(8,128)S(1)}, f32[2,128,128]{2,1,0:T(8,128)S(1)}, u32[]{:S(2)}, u32[]{:S(2)}) collective-permute-start(f32[2,128,128]{2,1,0:T(8,128)S(1)} %slice_add_fusion.2), channel_id=1, source_target_pairs={{0,2},{1,3},{2,0},{3,1},{4,6},{5,7},{6,4},{7,5},{8,10},{9,11},{10,... | collective-permute-start | bytes 393224 | tf_op jit(solution)/shard_map/ppermute | solution.py:384
  63.9 4.8 %collective-permute-start.20 = (bf16[384,1024]{1,0:T(8,128)(2,1)S(1)}, bf16[384,1024]{1,0:T(8,128)(2,1)S(1)}, u32[]{:S(2)}, u32[]{:S(2)}) collective-permute-start(bf16[384,1024]{1,0:T(8,128)(2,1)S(1)} %collective-permute-done.16.refs_4_), channel_id=1, source_target_pairs={{0,4},{4,0},{8,12},{12,8},{1,5},{5,1},{9,13},{13,9},{2,6},{6,2},{1... | collective-permute-start | bytes 2359304 | tf_op jit(solution)/shard_map/ppermute | solution.py:375
  63.9 4.8 %collective-permute-start.21 = (bf16[256,1024]{1,0:T(8,128)(2,1)}, bf16[256,1024]{1,0:T(8,128)(2,1)}, u32[]{:S(2)}, u32[]{:S(2)}) collective-permute-start(bf16[256,1024]{1,0:T(8,128)(2,1)} %collective-permute-done.17.refs_5_), channel_id=1, source_target_pairs={{0,4},{4,0},{8,12},{12,8},{1,5},{5,1},{9,13},{13,9},{2,6},{6,2},{1... | collective-permute-start | bytes 1572872 | tf_op jit(solution)/shard_map/ppermute | solution.py:375
  64.4 4.3 %collective-permute-start.22 = (bf16[256,1024]{1,0:T(8,128)(2,1)S(1)}, bf16[256,1024]{1,0:T(8,128)(2,1)}, u32[]{:S(2)}, u32[]{:S(2)}) collective-permute-start(bf16[256,1024]{1,0:T(8,128)(2,1)S(1)} %collective-permute-done.18.refs_6_), channel_id=1, source_target_pairs={{0,4},{4,0},{8,12},{12,8},{1,5},{5,1},{9,13},{13,9},{2,6},{6,2},{1... | collective-permute-start | bytes 1572872 | tf_op jit(solution)/shard_map/ppermute | solution.py:375
  64.5 4.3 %collective-permute-start.23 = (bf16[384,640]{1,0:T(8,128)(2,1)}, bf16[384,640]{1,0:T(8,128)(2,1)}, u32[]{:S(2)}, u32[]{:S(2)}) collective-permute-start(bf16[384,640]{1,0:T(8,128)(2,1)} %get-tuple-element.86), channel_id=1, source_target_pairs={{0,4},{4,0},{8,12},{12,8},{1,5},{5,1},{9,13},{13,9},{2,6},{6,2},{1... | collective-permute-start | bytes 1474568 | tf_op jit(solution)/shard_map/ppermute | solution.py:375
  65.0 9.3 %collective-permute-start.24 = (f32[2,128,128]{2,1,0:T(8,128)S(1)}, f32[2,128,128]{2,1,0:T(8,128)}, u32[]{:S(2)}, u32[]{:S(2)}) collective-permute-start(f32[2,128,128]{2,1,0:T(8,128)S(1)} %add.33), channel_id=1, source_target_pairs={{0,1},{1,0},{2,3},{3,2},{4,5},{5,4},{6,7},{7,6},{8,9},{9,8},{10,11... | collective-permute-start | bytes 393224 | tf_op jit(solution)/shard_map/ppermute | solution.py:384
  (1 other events, 3.7 us)

commit v6 on v5

--- a/solution.py
+++ b/solution.py
@@ -274,7 +274,7 @@
 
 
 def rows_grad(
-    units, weights, rows, cols, slots, ups, deltas, delta_at, width, out=None, moves=(), moved=(), tile=4,
+    units, weights, rows, cols, slots, ups, deltas, delta_at, width, out=None, moves=(), moved=(), tile=8,
     other=None, other_units=None, other_first=0, vmem=VMEM_BYTES,
 ):
     n_units = len(units)

time: 76.3 us -> 75.9 us (level)
  transfers between devices with their start and end apart: 25 -> 25, of which waited for: 7 -> 8; matrix products, arithmetic and copies ran while one was open for 3% -> 3% of each run, Pallas kernels for 39% -> 39%
where the time goes in v6:
time: 75.9 us; the launch traced here: 75.6 us
  Pallas kernels  29.8 us (39%)
  starting transfers between devices  25.4 us (33%)
  waiting for transfers between devices  15.6 us (21%)
  other arithmetic  2.79 us (4%)
  local copies, waits for them, and re-layouts  1.09 us (1%)
  between operations  0.84 us (1%)
    pallas_call x5, Pallas kernels, rows_grad(): pl.pallas_call(functools.partial(rows_kernel, units, moves, tile, width /...  24.4 us
    ppermute x6, starting transfers between devices, over_z(): return lax.ppermute(a, 'dp', [(k, k ^ step) for k in range(n_dp)])  9.97 us
    ppermute x6, starting transfers between devices, over_x(): return lax.ppermute(a, 'fsdp', [(k, k ^ 2) for k in range(4)])  8.67 us
    ppermute x6, waiting for transfers between devices, over_x(): return lax.ppermute(a, 'fsdp', [(k, k ^ 2) for k in range(4)])  7.91 us
    ppermute x6, waiting for transfers between devices, over_z(): return lax.ppermute(a, 'dp', [(k, k ^ step) for k in range(n_dp)])  5.38 us
    pallas_call x1, Pallas kernels, block_grads(): pl.pallas_call(functools.partial(grad_kernel, place, len(shapes), cuts),...  5.36 us
    ppermute x4, starting transfers between devices, over_y(): return lax.ppermute(a, 'group', [(k, k ^ 1) for k in range(2)])  5.07 us
    ppermute x9, waiting for transfers between devices, over_core(): return lax.ppermute(a, 'fsdp', [(k, k ^ 1) for k in range(4)])  2.14 us
  transfers between devices with their start and end apart: 25, of which 8 were waited for; matrix products, arithmetic and copies ran while one was open for 3% of the time, Pallas kernels for 39%

profile of v6, /device:TPU:0, one launch (start us, length us, event | category | flops | bytes accessed | tf_op | source)
XLA Modules:
  0.0 75.6 jit_solution(17138151888440831827)
XLA Ops:
  0.6 0.5 collective-permute-start.1
  1.2 1.0 %constant_dynamic-slice_fusion = bf16[128,1024]{1,0:T(8,128)(2,1)S(1)} fusion(bf16[2048,1024]{1,0:T(8,128)(2,1)} %refs_5_.3, s32[]{:T(128)S(6)} %select_n.21), kind=kLoop, calls=%fused_computation.6 | loop fusion | bytes 524292 | tf_op jit(solution)/shard_map/dynamic_slice | solution.py:428
  2.2 2.6 %collective-permute-start = (bf16[128,1024]{1,0:T(8,128)(2,1)S(1)}, bf16[128,1024]{1,0:T(8,128)(2,1)S(1)}, u32[]{:S(2)}, u32[]{:S(2)}) collective-permute-start(bf16[128,1024]{1,0:T(8,128)(2,1)S(1)} %constant_dynamic-slice_fusion), channel_id=1, source_target_pairs={{0,8},{4,12},{8,0},{12,4},{1,9},{5,13},{9,1},{13,5},{2,10},{6,14},... | collective-permute-start | bytes 786440 | tf_op jit(solution)/shard_map/ppermute | solution.py:378
  5.0 5.4 %block_grads.1 = (f32[8,128,128]{2,1,0:T(8,128)}, f32[8,128,128]{2,1,0:T(8,128)}, bf16[128,1024]{1,0:T(8,128)(2,1)}, bf16[256,1024]{1,0:T(8,128)(2,1)}, bf16[384,1024]{1,0:T(8,128)(2,1)}) custom-call(s32[16]{0:T(128)} %refs_0_.11, s32[16]{0:T(128)} %refs_1_.9, s32[16]{0:T(128)} %refs_2_.9, bf16[384,8192]{1,0:T(8,128)(2,1)} %act_ref.1, ...), custom_call_target="tpu_custom_call" | custom-call | flops 1024 | bytes 1024 | tf_op jit(solution)/shard_map/block_grads/pallas_call | solution.py:98
  10.4 1.4 %collective-permute-done.refs_5_ = bf16[128,1024]{1,0:T(8,128)(2,1)S(1)} collective-permute-done((bf16[128,1024]{1,0:T(8,128)(2,1)S(1)}, bf16[128,1024]{1,0:T(8,128)(2,1)S(1)}, u32[]{:S(2)}, u32[]{:S(2)}) %collective-permute-start) | collective-permute-done | bytes 262176 | tf_op jit(solution)/shard_map/ppermute | solution.py:378
  11.8 1.8 %collective-permute-start.5 = (bf16[4,128,128]{2,1,0:T(8,128)(2,1)S(1)}, bf16[4,128,128]{2,1,0:T(8,128)(2,1)S(1)}, u32[]{:S(2)}, u32[]{:S(2)}) collective-permute-start(bf16[4,128,128]{2,1,0:T(8,128)(2,1)S(1)} %copy-done.1), channel_id=1, source_target_pairs={{0,8},{4,12},{8,0},{12,4},{1,9},{5,13},{9,1},{13,5},{2,10},{6,14},... | collective-permute-start | bytes 393224 | tf_op jit(solution)/shard_map/ppermute | solution.py:378
  13.9 1.0 %slice_add_fusion.1 = f32[4,128,128]{2,1,0:T(8,128)S(1)} fusion(f32[8,128,128]{2,1,0:T(8,128)S(1)} %collective-permute-done.3, f32[8,128,128]{2,1,0:T(8,128)} %get-tuple-element.50), kind=kLoop, calls=%fused_computation.2 | loop fusion | flops 65536 | bytes 786432 | tf_op jit(solution)/shard_map/add | solution.py:440
  14.9 1.8 %collective-permute-start.4 = (f32[4,128,128]{2,1,0:T(8,128)S(1)}, f32[4,128,128]{2,1,0:T(8,128)S(1)}, u32[]{:S(2)}, u32[]{:S(2)}) collective-permute-start(f32[4,128,128]{2,1,0:T(8,128)S(1)} %slice_add_fusion.1), channel_id=1, source_target_pairs={{0,8},{4,12},{8,0},{12,4},{1,9},{5,13},{9,1},{13,5},{2,10},{6,14},... | collective-permute-start | bytes 786440 | tf_op jit(solution)/shard_map/ppermute | solution.py:378
  16.7 1.5 %collective-permute-done.5.refs_8_.refs_11_.refs_12_ = bf16[4,128,128]{2,1,0:T(8,128)(2,1)S(1)} collective-permute-done((bf16[4,128,128]{2,1,0:T(8,128)(2,1)S(1)}, bf16[4,128,128]{2,1,0:T(8,128)(2,1)S(1)}, u32[]{:S(2)}, u32[]{:S(2)}) %collective-permute-start.5) | collective-permute-done | bytes 131104 | tf_op jit(solution)/shard_map/ppermute | solution.py:378
  18.1 1.8 %collective-permute-start.9 = (bf16[128,1024]{1,0:T(8,128)(2,1)S(1)}, bf16[128,1024]{1,0:T(8,128)(2,1)S(1)}, u32[]{:S(2)}, u32[]{:S(2)}) collective-permute-start(bf16[128,1024]{1,0:T(8,128)(2,1)S(1)} %collective-permute-done.refs_5_), channel_id=1, source_target_pairs={{0,1},{1,0},{2,3},{3,2},{4,5},{5,4},{6,7},{7,6},{8,9},{9,8},{10,11... | collective-permute-start | bytes 786440 | tf_op jit(solution)/shard_map/ppermute | solution.py:384
  20.0 1.5 %collective-permute-start.8 = (bf16[128,1024]{1,0:T(8,128)(2,1)S(1)}, bf16[128,1024]{1,0:T(8,128)(2,1)S(1)}, u32[]{:S(2)}, u32[]{:S(2)}) collective-permute-start(bf16[128,1024]{1,0:T(8,128)(2,1)S(1)} %collective-permute-done.refs_5_), channel_id=1, source_target_pairs={{0,16},{16,0},{1,17},{17,1},{2,18},{18,2},{3,19},{19,3},{4,20},{20... | collective-permute-start | bytes 786440 | tf_op jit(solution)/shard_map/ppermute | solution.py:381
  21.5 5.0 %rows_grad.5 = (bf16[384,8192]{1,0:T(8,128)(2,1)}, bf16[384,2560]{1,0:T(8,128)(2,1)S(1)}) custom-call(s32[16]{0:T(128)S(1)} %copy-done.2, s32[16]{0:T(128)S(1)} %copy-done.3, s32[16]{0:T(128)S(1)} %copy-done.4, bf16[384,1024]{1,0:T(8,128)(2,1)S(1)} %copy-done, bf16[384,1024]{1,0:T(8,128)(2,1)S(1)} %collective-permute-done.1.refs_4_, ...), custom_call_target="tpu_custom_call" | custom-call | flops 1024 | bytes 1024 | tf_op jit(solution)/shard_map/rows_grad/pallas_call | solution.py:299
  26.5 2.4 %collective-permute-done.4 = f32[4,128,128]{2,1,0:T(8,128)S(1)} collective-permute-done((f32[4,128,128]{2,1,0:T(8,128)S(1)}, f32[4,128,128]{2,1,0:T(8,128)S(1)}, u32[]{:S(2)}, u32[]{:S(2)}) %collective-permute-start.4) | collective-permute-done | bytes 262176 | tf_op jit(solution)/shard_map/ppermute | solution.py:378
  28.9 1.7 %collective-permute-start.11 = (bf16[256,1024]{1,0:T(8,128)(2,1)S(1)}, bf16[256,1024]{1,0:T(8,128)(2,1)S(1)}, u32[]{:S(2)}, u32[]{:S(2)}) collective-permute-start(bf16[256,1024]{1,0:T(8,128)(2,1)S(1)} %copy-done.7), channel_id=1, source_target_pairs={{0,8},{4,12},{8,0},{12,4},{1,9},{5,13},{9,1},{13,5},{2,10},{6,14},... | collective-permute-start | bytes 1572872 | tf_op jit(solution)/shard_map/ppermute | solution.py:378
  30.7 1.5 %collective-permute-start.14 = (bf16[128,1024]{1,0:T(8,128)(2,1)S(1)}, bf16[128,1024]{1,0:T(8,128)(2,1)S(1)}, u32[]{:S(2)}, u32[]{:S(2)}) collective-permute-start(bf16[128,1024]{1,0:T(8,128)(2,1)S(1)} %collective-permute-done.9.refs_7_), channel_id=1, source_target_pairs={{0,16},{16,0},{1,17},{17,1},{2,18},{18,2},{3,19},{19,3},{4,20},{20... | collective-permute-start | bytes 786440 | tf_op jit(solution)/shard_map/ppermute | solution.py:381
  32.2 1.6 %collective-permute-start.13 = (bf16[128,1024]{1,0:T(8,128)(2,1)S(1)}, bf16[128,1024]{1,0:T(8,128)(2,1)S(1)}, u32[]{:S(2)}, u32[]{:S(2)}) collective-permute-start(bf16[128,1024]{1,0:T(8,128)(2,1)S(1)} %collective-permute-done.7.refs_8_), channel_id=1, source_target_pairs={{0,1},{1,0},{2,3},{3,2},{4,5},{5,4},{6,7},{7,6},{8,9},{9,8},{10,11... | collective-permute-start | bytes 786440 | tf_op jit(solution)/shard_map/ppermute | solution.py:384
  34.3 0.5 collective-permute-start.10
  34.8 5.0 %rows_grad.6 = (bf16[384,8192]{1,0:T(8,128)(2,1)}, bf16[384,2560]{1,0:T(8,128)(2,1)S(1)}) custom-call(s32[16]{0:T(128)S(1)} %copy-done.2, s32[16]{0:T(128)S(1)} %copy-done.3, s32[16]{0:T(128)S(1)} %copy-done.4, bf16[384,1024]{1,0:T(8,128)(2,1)S(1)} %copy-done, ...), custom_call_target="tpu_custom_call", output_to_operand_aliasing={{0}: (10, {}), {1}: (11, {})} | custom-call | flops 1024 | bytes 1024 | tf_op jit(solution)/shard_map/rows_grad/pallas_call | solution.py:299
  39.8 3.8 %rows_grad.7 = (bf16[384,8192]{1,0:T(8,128)(2,1)}, bf16[384,2560]{1,0:T(8,128)(2,1)S(1)}) custom-call(s32[16]{0:T(128)S(1)} %copy-done.2, s32[16]{0:T(128)S(1)} %copy-done.3, s32[16]{0:T(128)S(1)} %copy-done.4, bf16[384,1024]{1,0:T(8,128)(2,1)S(1)} %copy-done, ...), custom_call_target="tpu_custom_call", output_to_operand_aliasing={{0}: (13, {}), {1}: (14, {})} | custom-call | flops 1024 | bytes 1024 | tf_op jit(solution)/shard_map/rows_grad/pallas_call | solution.py:299
  44.3 1.8 %collective-permute-start.18 = (bf16[256,1024]{1,0:T(8,128)(2,1)S(1)}, bf16[256,1024]{1,0:T(8,128)(2,1)S(1)}, u32[]{:S(2)}, u32[]{:S(2)}) collective-permute-start(bf16[256,1024]{1,0:T(8,128)(2,1)S(1)} %collective-permute-done.11.refs_8_), channel_id=1, source_target_pairs={{0,1},{1,0},{2,3},{3,2},{4,5},{5,4},{6,7},{7,6},{8,9},{9,8},{10,11... | collective-permute-start | bytes 1572872 | tf_op jit(solution)/shard_map/ppermute | solution.py:384
  46.0 1.5 %collective-permute-start.17 = (bf16[256,1024]{1,0:T(8,128)(2,1)S(1)}, bf16[256,1024]{1,0:T(8,128)(2,1)}, u32[]{:S(2)}, u32[]{:S(2)}) collective-permute-start(bf16[256,1024]{1,0:T(8,128)(2,1)S(1)} %collective-permute-done.11.refs_8_), channel_id=1, source_target_pairs={{0,16},{16,0},{1,17},{17,1},{2,18},{18,2},{3,19},{19,3},{4,20},{20... | collective-permute-start | bytes 1572872 | tf_op jit(solution)/shard_map/ppermute | solution.py:381
  47.6 2.7 %collective-permute-start.19 = (f32[2,128,128]{2,1,0:T(8,128)S(1)}, f32[2,128,128]{2,1,0:T(8,128)S(1)}, u32[]{:S(2)}, u32[]{:S(2)}) collective-permute-start(f32[2,128,128]{2,1,0:T(8,128)S(1)} %slice_add_fusion.2), channel_id=1, source_target_pairs={{0,2},{1,3},{2,0},{3,1},{4,6},{5,7},{6,4},{7,5},{8,10},{9,11},{10,... | collective-permute-start | bytes 393224 | tf_op jit(solution)/shard_map/ppermute | solution.py:384
  50.2 5.5 %rows_grad.8 = (bf16[384,8192]{1,0:T(8,128)(2,1)}, bf16[384,640]{1,0:T(8,128)(2,1)}) custom-call(s32[16]{0:T(128)S(1)} %copy-done.2, s32[16]{0:T(128)S(1)} %copy-done.3, s32[16]{0:T(128)S(1)} %copy-done.4, bf16[384,1024]{1,0:T(8,128)(2,1)S(1)} %copy-done, bf16[384,1024]{1,0:T(8,128)(2,1)S(1)} %collective-permute-done.1.refs_4_, ...), custom_call_target="tpu_custom_call", output_to_operand_aliasing={{0}: (14, {})} | custom-call | flops 1024 | bytes 1024 | tf_op jit(solution)/shard_map/rows_grad/pallas_call | solution.py:299
  55.7 4.6 %collective-permute-done.19 = f32[2,128,128]{2,1,0:T(8,128)S(1)} collective-permute-done((f32[2,128,128]{2,1,0:T(8,128)S(1)}, f32[2,128,128]{2,1,0:T(8,128)S(1)}, u32[]{:S(2)}, u32[]{:S(2)}) %collective-permute-start.19) | collective-permute-done | bytes 131104 | tf_op jit(solution)/shard_map/ppermute | solution.py:384
  60.4 0.7 collective-permute-done.18.refs_6_
  61.1 2.7 %collective-permute-done.16.refs_4_ = bf16[384,1024]{1,0:T(8,128)(2,1)S(1)} collective-permute-done((bf16[384,1024]{1,0:T(8,128)(2,1)S(1)}, bf16[384,1024]{1,0:T(8,128)(2,1)S(1)}, u32[]{:S(2)}, u32[]{:S(2)}) %collective-permute-start.16) | collective-permute-done | bytes 786464 | tf_op jit(solution)/shard_map/ppermute | solution.py:378
  63.8 0.5 collective-permute-start.21
  64.3 0.5 collective-permute-start.23
  64.9 1.6 %collective-permute-start.24 = (f32[2,128,128]{2,1,0:T(8,128)S(1)}, f32[2,128,128]{2,1,0:T(8,128)}, u32[]{:S(2)}, u32[]{:S(2)}) collective-permute-start(f32[2,128,128]{2,1,0:T(8,128)S(1)} %add.33), channel_id=1, source_target_pairs={{0,1},{1,0},{2,3},{3,2},{4,5},{5,4},{6,7},{7,6},{8,9},{9,8},{10,11... | collective-permute-start | bytes 393224 | tf_op jit(solution)/shard_map/ppermute | solution.py:384
  66.5 2.1 %collective-permute-done.23.refs_14_ = bf16[384,640]{1,0:T(8,128)(2,1)} collective-permute-done((bf16[384,640]{1,0:T(8,128)(2,1)}, bf16[384,640]{1,0:T(8,128)(2,1)}, u32[]{:S(2)}, u32[]{:S(2)}) %collective-permute-start.23) | collective-permute-done | bytes 491552 | tf_op jit(solution)/shard_map/ppermute | solution.py:375
  68.6 5.2 %rows_grad.9 = bf16[384,8192]{1,0:T(8,128)(2,1)} custom-call(s32[16]{0:T(128)S(1)} %copy-done.2, s32[16]{0:T(128)S(1)} %copy-done.3, s32[16]{0:T(128)S(1)} %copy-done.4, bf16[384,1024]{1,0:T(8,128)(2,1)S(1)} %copy-done, bf16[384,1024]{1,0:T(8,128)(2,1)S(1)} %collective-permute-done.16.refs_4_, ...), custom_call_target="tpu_custom_call", output_to_operand_aliasing={{}: (15, {})} | custom-call | flops 1024 | bytes 1024 | tf_op jit(solution)/shard_map/rows_grad/pallas_call | solution.py:299
  73.8 1.7 %fusion.1 = f32[4,128,128]{2,1,0:T(8,128)} fusion(f32[2,128,128]{2,1,0:T(8,128)} %collective-permute-done.24, f32[2,128,128]{2,1,0:T(8,128)S(1)} %add.33, pred[]{:T(512)S(6)} %eq.6), kind=kLoop, calls=%fused_computation.4 | loop fusion | flops 262144 | bytes 524289 | tf_op jit(solution)/shard_map/mul | solution.py:504
  (47 shorter events, 1.8 us)
Async XLA Ops:
  0.6 11.1 %copy-start.1 = (bf16[4,128,128]{2,1,0:T(8,128)(2,1)S(1)}, bf16[4,128,128]{2,1,0:T(8,128)(2,1)}, u32[]{:S(2)}) copy-start(bf16[4,128,128]{2,1,0:T(8,128)(2,1)} %refs_10_.1) | copy-start | bytes 393220
  0.6 11.1 %collective-permute-start.1 = (bf16[384,1024]{1,0:T(8,128)(2,1)}, bf16[384,1024]{1,0:T(8,128)(2,1)S(1)}, u32[]{:S(2)}, u32[]{:S(2)}) collective-permute-start(bf16[384,1024]{1,0:T(8,128)(2,1)} %refs_3_.9), channel_id=1, source_target_pairs={{0,4},{4,0},{8,12},{12,8},{1,5},{5,1},{9,13},{13,9},{2,6},{6,2},{1... | collective-permute-start | bytes 2359304 | tf_op jit(solution)/shard_map/ppermute | solution.py:375
  1.2 20.3 %copy-start = (bf16[384,1024]{1,0:T(8,128)(2,1)S(1)}, bf16[384,1024]{1,0:T(8,128)(2,1)}, u32[]{:S(2)}) copy-start(bf16[384,1024]{1,0:T(8,128)(2,1)} %refs_3_.9) | copy-start | bytes 2359300
  1.2 20.3 %copy-start.2 = (s32[16]{0:T(128)S(1)}, s32[16]{0:T(128)}, u32[]{:S(2)}) copy-start(s32[16]{0:T(128)} %refs_0_.11) | copy-start | bytes 196
  1.2 20.3 %copy-start.3 = (s32[16]{0:T(128)S(1)}, s32[16]{0:T(128)}, u32[]{:S(2)}) copy-start(s32[16]{0:T(128)} %refs_1_.9) | copy-start | bytes 196
  1.2 20.3 %copy-start.4 = (s32[16]{0:T(128)S(1)}, s32[16]{0:T(128)}, u32[]{:S(2)}) copy-start(s32[16]{0:T(128)} %refs_2_.9) | copy-start | bytes 196
  2.2 9.5 %collective-permute-start = (bf16[128,1024]{1,0:T(8,128)(2,1)S(1)}, bf16[128,1024]{1,0:T(8,128)(2,1)S(1)}, u32[]{:S(2)}, u32[]{:S(2)}) collective-permute-start(bf16[128,1024]{1,0:T(8,128)(2,1)S(1)} %constant_dynamic-slice_fusion), channel_id=1, source_target_pairs={{0,8},{4,12},{8,0},{12,4},{1,9},{5,13},{9,1},{13,5},{2,10},{6,14},... | collective-permute-start | bytes 786440 | tf_op jit(solution)/shard_map/ppermute | solution.py:378
  4.8 5.6 %collective-permute-start.2 = (bf16[4,128,128]{2,1,0:T(8,128)(2,1)}, bf16[4,128,128]{2,1,0:T(8,128)(2,1)S(1)}, u32[]{:S(2)}, u32[]{:S(2)}) collective-permute-start(bf16[4,128,128]{2,1,0:T(8,128)(2,1)} %refs_10_.1), channel_id=1, source_target_pairs={{0,4},{4,0},{8,12},{12,8},{1,5},{5,1},{9,13},{13,9},{2,6},{6,2},{1... | collective-permute-start | bytes 393224 | tf_op jit(solution)/shard_map/ppermute | solution.py:375
  10.4 18.5 %copy-start.7 = (bf16[256,1024]{1,0:T(8,128)(2,1)S(1)}, bf16[256,1024]{1,0:T(8,128)(2,1)}, u32[]{:S(2)}) copy-start(bf16[256,1024]{1,0:T(8,128)(2,1)} %get-tuple-element.70) | copy-start | bytes 1572868
  10.4 23.9 %copy-start.5 = (f32[8,128,128]{2,1,0:T(8,128)S(1)}, f32[8,128,128]{2,1,0:T(8,128)}, u32[]{:S(2)}) copy-start(f32[8,128,128]{2,1,0:T(8,128)} %get-tuple-element.50) | copy-start | bytes 1572868
  11.8 2.1 %collective-permute-start.3 = (f32[8,128,128]{2,1,0:T(8,128)}, f32[8,128,128]{2,1,0:T(8,128)S(1)}, u32[]{:S(2)}, u32[]{:S(2)}) collective-permute-start(f32[8,128,128]{2,1,0:T(8,128)} %get-tuple-element.51), channel_id=1, source_target_pairs={{0,4},{4,0},{8,12},{12,8},{1,5},{5,1},{9,13},{13,9},{2,6},{6,2},{1... | collective-permute-start | bytes 1572872 | tf_op jit(solution)/shard_map/ppermute | solution.py:375
  11.8 6.4 %collective-permute-start.5 = (bf16[4,128,128]{2,1,0:T(8,128)(2,1)S(1)}, bf16[4,128,128]{2,1,0:T(8,128)(2,1)S(1)}, u32[]{:S(2)}, u32[]{:S(2)}) collective-permute-start(bf16[4,128,128]{2,1,0:T(8,128)(2,1)S(1)} %copy-done.1), channel_id=1, source_target_pairs={{0,8},{4,12},{8,0},{12,4},{1,9},{5,13},{9,1},{13,5},{2,10},{6,14},... | collective-permute-start | bytes 393224 | tf_op jit(solution)/shard_map/ppermute | solution.py:378
  13.6 12.9 %collective-permute-start.7 = (bf16[128,1024]{1,0:T(8,128)(2,1)}, bf16[128,1024]{1,0:T(8,128)(2,1)S(1)}, u32[]{:S(2)}, u32[]{:S(2)}) collective-permute-start(bf16[128,1024]{1,0:T(8,128)(2,1)} %get-tuple-element.58), channel_id=1, source_target_pairs={{0,8},{4,12},{8,0},{12,4},{1,9},{5,13},{9,1},{13,5},{2,10},{6,14},... | collective-permute-start | bytes 786440 | tf_op jit(solution)/shard_map/ppermute | solution.py:378
  14.9 14.0 %collective-permute-start.4 = (f32[4,128,128]{2,1,0:T(8,128)S(1)}, f32[4,128,128]{2,1,0:T(8,128)S(1)}, u32[]{:S(2)}, u32[]{:S(2)}) collective-permute-start(f32[4,128,128]{2,1,0:T(8,128)S(1)} %slice_add_fusion.1), channel_id=1, source_target_pairs={{0,8},{4,12},{8,0},{12,4},{1,9},{5,13},{9,1},{13,5},{2,10},{6,14},... | collective-permute-start | bytes 786440 | tf_op jit(solution)/shard_map/ppermute | solution.py:378
  18.1 3.4 %collective-permute-start.6 = (bf16[4,128,128]{2,1,0:T(8,128)(2,1)S(1)}, bf16[4,128,128]{2,1,0:T(8,128)(2,1)S(1)}, u32[]{:S(2)}, u32[]{:S(2)}) collective-permute-start(bf16[4,128,128]{2,1,0:T(8,128)(2,1)S(1)} %collective-permute-done.5.refs_8_.refs_11_.refs_12_), channel_id=1, source_target_pairs={{0,4},{4,0},{8,12},{12,8},{1,5},{5,1},{9,13},{13,9},{2,6},{6,2},{1... | collective-permute-start | bytes 393224 | tf_op jit(solution)/shard_map/ppermute | solution.py:375
  18.1 12.5 %collective-permute-start.9 = (bf16[128,1024]{1,0:T(8,128)(2,1)S(1)}, bf16[128,1024]{1,0:T(8,128)(2,1)S(1)}, u32[]{:S(2)}, u32[]{:S(2)}) collective-permute-start(bf16[128,1024]{1,0:T(8,128)(2,1)S(1)} %collective-permute-done.refs_5_), channel_id=1, source_target_pairs={{0,1},{1,0},{2,3},{3,2},{4,5},{5,4},{6,7},{7,6},{8,9},{9,8},{10,11... | collective-permute-start | bytes 786440 | tf_op jit(solution)/shard_map/ppermute | solution.py:384
  20.0 10.7 %collective-permute-start.8 = (bf16[128,1024]{1,0:T(8,128)(2,1)S(1)}, bf16[128,1024]{1,0:T(8,128)(2,1)S(1)}, u32[]{:S(2)}, u32[]{:S(2)}) collective-permute-start(bf16[128,1024]{1,0:T(8,128)(2,1)S(1)} %collective-permute-done.refs_5_), channel_id=1, source_target_pairs={{0,16},{16,0},{1,17},{17,1},{2,18},{18,2},{3,19},{19,3},{4,20},{20... | collective-permute-start | bytes 786440 | tf_op jit(solution)/shard_map/ppermute | solution.py:381
  28.9 14.9 %collective-permute-start.11 = (bf16[256,1024]{1,0:T(8,128)(2,1)S(1)}, bf16[256,1024]{1,0:T(8,128)(2,1)S(1)}, u32[]{:S(2)}, u32[]{:S(2)}) collective-permute-start(bf16[256,1024]{1,0:T(8,128)(2,1)S(1)} %copy-done.7), channel_id=1, source_target_pairs={{0,8},{4,12},{8,0},{12,4},{1,9},{5,13},{9,1},{13,5},{2,10},{6,14},... | collective-permute-start | bytes 1572872 | tf_op jit(solution)/shard_map/ppermute | solution.py:378
  30.7 13.0 %collective-permute-start.14 = (bf16[128,1024]{1,0:T(8,128)(2,1)S(1)}, bf16[128,1024]{1,0:T(8,128)(2,1)S(1)}, u32[]{:S(2)}, u32[]{:S(2)}) collective-permute-start(bf16[128,1024]{1,0:T(8,128)(2,1)S(1)} %collective-permute-done.9.refs_7_), channel_id=1, source_target_pairs={{0,16},{16,0},{1,17},{17,1},{2,18},{18,2},{3,19},{19,3},{4,20},{20... | collective-permute-start | bytes 786440 | tf_op jit(solution)/shard_map/ppermute | solution.py:381
  32.2 11.5 %collective-permute-start.13 = (bf16[128,1024]{1,0:T(8,128)(2,1)S(1)}, bf16[128,1024]{1,0:T(8,128)(2,1)S(1)}, u32[]{:S(2)}, u32[]{:S(2)}) collective-permute-start(bf16[128,1024]{1,0:T(8,128)(2,1)S(1)} %collective-permute-done.7.refs_8_), channel_id=1, source_target_pairs={{0,1},{1,0},{2,3},{3,2},{4,5},{5,4},{6,7},{7,6},{8,9},{9,8},{10,11... | collective-permute-start | bytes 786440 | tf_op jit(solution)/shard_map/ppermute | solution.py:384
  33.8 10.1 %collective-permute-start.12 = (bf16[128,1024]{1,0:T(8,128)(2,1)S(1)}, bf16[128,1024]{1,0:T(8,128)(2,1)S(1)}, u32[]{:S(2)}, u32[]{:S(2)}) collective-permute-start(bf16[128,1024]{1,0:T(8,128)(2,1)S(1)} %collective-permute-done.7.refs_8_), channel_id=1, source_target_pairs={{0,16},{16,0},{1,17},{17,1},{2,18},{18,2},{3,19},{19,3},{4,20},{20... | collective-permute-start | bytes 786440 | tf_op jit(solution)/shard_map/ppermute | solution.py:381
  34.3 9.3 %collective-permute-start.10 = (f32[2,128,128]{2,1,0:T(8,128)S(1)}, f32[2,128,128]{2,1,0:T(8,128)S(1)}, u32[]{:S(2)}, u32[]{:S(2)}) collective-permute-start(f32[2,128,128]{2,1,0:T(8,128)S(1)} %slice.26), channel_id=1, source_target_pairs={{0,1},{1,0},{2,3},{3,2},{4,5},{5,4},{6,7},{7,6},{8,9},{9,8},{10,11... | collective-permute-start | bytes 393224 | tf_op jit(solution)/shard_map/ppermute | solution.py:384
  43.9 6.4 %collective-permute-start.15 = (bf16[384,2560]{1,0:T(8,128)(2,1)S(1)}, bf16[384,2560]{1,0:T(8,128)(2,1)S(1)}, u32[]{:S(2)}, u32[]{:S(2)}) collective-permute-start(bf16[384,2560]{1,0:T(8,128)(2,1)S(1)} %get-tuple-element.76), channel_id=1, source_target_pairs={{0,4},{4,0},{8,12},{12,8},{1,5},{5,1},{9,13},{13,9},{2,6},{6,2},{1... | collective-permute-start | bytes 5898248 | tf_op jit(solution)/shard_map/ppermute | solution.py:375
  43.9 20.0 %collective-permute-start.16 = (bf16[384,1024]{1,0:T(8,128)(2,1)S(1)}, bf16[384,1024]{1,0:T(8,128)(2,1)S(1)}, u32[]{:S(2)}, u32[]{:S(2)}) collective-permute-start(bf16[384,1024]{1,0:T(8,128)(2,1)S(1)} %copy-done.6), channel_id=1, source_target_pairs={{0,8},{4,12},{8,0},{12,4},{1,9},{5,13},{9,1},{13,5},{2,10},{6,14},... | collective-permute-start | bytes 2359304 | tf_op jit(solution)/shard_map/ppermute | solution.py:378
  44.3 16.8 %collective-permute-start.18 = (bf16[256,1024]{1,0:T(8,128)(2,1)S(1)}, bf16[256,1024]{1,0:T(8,128)(2,1)S(1)}, u32[]{:S(2)}, u32[]{:S(2)}) collective-permute-start(bf16[256,1024]{1,0:T(8,128)(2,1)S(1)} %collective-permute-done.11.refs_8_), channel_id=1, source_target_pairs={{0,1},{1,0},{2,3},{3,2},{4,5},{5,4},{6,7},{7,6},{8,9},{9,8},{10,11... | collective-permute-start | bytes 1572872 | tf_op jit(solution)/shard_map/ppermute | solution.py:384
  46.0 15.1 %collective-permute-start.17 = (bf16[256,1024]{1,0:T(8,128)(2,1)S(1)}, bf16[256,1024]{1,0:T(8,128)(2,1)}, u32[]{:S(2)}, u32[]{:S(2)}) collective-permute-start(bf16[256,1024]{1,0:T(8,128)(2,1)S(1)} %collective-permute-done.11.refs_8_), channel_id=1, source_target_pairs={{0,16},{16,0},{1,17},{17,1},{2,18},{18,2},{3,19},{19,3},{4,20},{20... | collective-permute-start | bytes 1572872 | tf_op jit(solution)/shard_map/ppermute | solution.py:381
  47.6 12.8 %collective-permute-start.19 = (f32[2,128,128]{2,1,0:T(8,128)S(1)}, f32[2,128,128]{2,1,0:T(8,128)S(1)}, u32[]{:S(2)}, u32[]{:S(2)}) collective-permute-start(f32[2,128,128]{2,1,0:T(8,128)S(1)} %slice_add_fusion.2), channel_id=1, source_target_pairs={{0,2},{1,3},{2,0},{3,1},{4,6},{5,7},{6,4},{7,5},{8,10},{9,11},{10,... | collective-permute-start | bytes 393224 | tf_op jit(solution)/shard_map/ppermute | solution.py:384
  63.8 4.8 %collective-permute-start.20 = (bf16[384,1024]{1,0:T(8,128)(2,1)S(1)}, bf16[384,1024]{1,0:T(8,128)(2,1)S(1)}, u32[]{:S(2)}, u32[]{:S(2)}) collective-permute-start(bf16[384,1024]{1,0:T(8,128)(2,1)S(1)} %collective-permute-done.16.refs_4_), channel_id=1, source_target_pairs={{0,4},{4,0},{8,12},{12,8},{1,5},{5,1},{9,13},{13,9},{2,6},{6,2},{1... | collective-permute-start | bytes 2359304 | tf_op jit(solution)/shard_map/ppermute | solution.py:375
  63.8 4.8 %collective-permute-start.21 = (bf16[256,1024]{1,0:T(8,128)(2,1)}, bf16[256,1024]{1,0:T(8,128)(2,1)}, u32[]{:S(2)}, u32[]{:S(2)}) collective-permute-start(bf16[256,1024]{1,0:T(8,128)(2,1)} %collective-permute-done.17.refs_5_), channel_id=1, source_target_pairs={{0,4},{4,0},{8,12},{12,8},{1,5},{5,1},{9,13},{13,9},{2,6},{6,2},{1... | collective-permute-start | bytes 1572872 | tf_op jit(solution)/shard_map/ppermute | solution.py:375
  64.3 4.3 %collective-permute-start.22 = (bf16[256,1024]{1,0:T(8,128)(2,1)S(1)}, bf16[256,1024]{1,0:T(8,128)(2,1)}, u32[]{:S(2)}, u32[]{:S(2)}) collective-permute-start(bf16[256,1024]{1,0:T(8,128)(2,1)S(1)} %collective-permute-done.18.refs_6_), channel_id=1, source_target_pairs={{0,4},{4,0},{8,12},{12,8},{1,5},{5,1},{9,13},{13,9},{2,6},{6,2},{1... | collective-permute-start | bytes 1572872 | tf_op jit(solution)/shard_map/ppermute | solution.py:375
  64.3 4.3 %collective-permute-start.23 = (bf16[384,640]{1,0:T(8,128)(2,1)}, bf16[384,640]{1,0:T(8,128)(2,1)}, u32[]{:S(2)}, u32[]{:S(2)}) collective-permute-start(bf16[384,640]{1,0:T(8,128)(2,1)} %get-tuple-element.86), channel_id=1, source_target_pairs={{0,4},{4,0},{8,12},{12,8},{1,5},{5,1},{9,13},{13,9},{2,6},{6,2},{1... | collective-permute-start | bytes 1474568 | tf_op jit(solution)/shard_map/ppermute | solution.py:375
  64.9 9.0 %collective-permute-start.24 = (f32[2,128,128]{2,1,0:T(8,128)S(1)}, f32[2,128,128]{2,1,0:T(8,128)}, u32[]{:S(2)}, u32[]{:S(2)}) collective-permute-start(f32[2,128,128]{2,1,0:T(8,128)S(1)} %add.33), channel_id=1, source_target_pairs={{0,1},{1,0},{2,3},{3,2},{4,5},{5,4},{6,7},{7,6},{8,9},{9,8},{10,11... | collective-permute-start | bytes 393224 | tf_op jit(solution)/shard_map/ppermute | solution.py:384
  (1 other events, 4.0 us)
